TPU v7x, 32 devices: a whole 2x2x4 slice. The times are simulated.
32 devices in a mesh: parts: 2 (over y), gz: 4 (over x, core), ty: 4 (over z).
Axes of the slice: x: 2, y: 2, z: 4, core: 2. Of those that a mesh axis runs over, the one named last changes fastest.
Arguments:
- sections: bfloat16 [8, 1024, 2048], P(('parts', 'gz'), 'ty'), parts along dimension 0, may hold values from -6 to 6
- boundary: bfloat16 [2048, 2048], P(('parts', 'ty')), parts along dimension 0, may hold values from -5 to 5
- row_shift: int32 [8, 1024], P(('parts', 'gz'), 'ty'), parts along dimension 0, may hold values from -64 to 63
- row_frac: int32 [8, 1024], P(('parts', 'gz'), 'ty'), parts along dimension 0, may hold values from 0 to 255
- col_shift: int32 [8, 2048], P(('parts', 'gz')), parts along dimension 0, may hold values from -64 to 63
- col_frac: int32 [8, 2048], P(('parts', 'gz')), parts along dimension 0, may hold values from 0 to 255
- peak_shift: int32 [2, 8, 8, 16], P(None, ('parts', 'gz'), 'ty'), parts along dimension 1, may hold values from -8 to 8
Outputs:
- rendered: bfloat16 [8, 1024, 2048], P(('parts', 'gz'), 'ty'), parts along dimension 0
- flow: float32 [2, 8, 8, 16], P(None, ('parts', 'gz'), 'ty'), parts along dimension 1
There are 2 independent parts, one for each index of `parts`. A program takes and returns all parts, laid end to end along the dimension named above; each array names one. Nothing has to cross between parts.
All inputs are finite; a program needn't handle non-finite values.
Results may differ from a plain program's by a relative error of at most 0.0049.
Values may be sent and summed in bfloat16 or wider, within the bound.
No kernel may reach another device: no remote copies, remote signals or barrier semaphores. Data moves between devices by JAX's collectives and lax.ppermute only.
A program may use at most 64 MiB of HBM per device.

v0:
```python
import functools

import jax
import jax.numpy as jnp
import numpy as np
from jax import lax
from jax.experimental import pallas as pl
from jax.experimental.pallas import tpu as pltpu
from jax.sharding import PartitionSpec as P

PATCH = 128
MARGIN = 64
SMOOTH_PASSES = 2
BLOCK = 256
LANES = 128
TAPS = (0.0625, 0.25, 0.375, 0.25, 0.0625)
FAR = 1 << 20
VMEM_LIMIT = 40 * 1024 * 1024

f32 = jnp.float32
bf16 = jnp.bfloat16


def swap_pairs(n, d, second):
    pairs = []
    for i in range(n):
        if (i // d) % 2 == int(second):
            j = i + d
            if j >= n:
                if not second or n % (2 * d):
                    continue
                j -= n
            pairs.append((i, j))
    return frozenset(frozenset(p) for p in pairs)


def both_ways(pairs):
    return sorted([tuple(sorted(p)) for p in pairs] + [tuple(sorted(p))[::-1] for p in pairs])


def halo_pairs(n_gz, n_ty, second):
    table = []
    for z in range(n_gz):
        for t in range(n_ty):
            partner = t + 1 if (t % 2 == 0) != second else t - 1
            if 0 <= partner < n_ty:
                table.append((z * n_ty + t, z * n_ty + partner))
            elif (z ^ 1) < n_gz:
                table.append((z * n_ty + t, (z ^ 1) * n_ty + t))
    return table


def hat(coord, position):
    return jnp.maximum(1.0 - jnp.abs(coord - position), 0.0)


def source_positions(ids, shift, frac, limit, base):
    source = jnp.clip(ids + shift, 0, limit) - base
    return source.astype(f32) + frac.astype(f32) * (1.0 / 256.0)


def columns_from(mix, table_ref, out_ref, rows):
    n_cols = mix.shape[1]
    for j in range(n_cols // BLOCK):
        first, last = j * BLOCK - LANES, (j + 1) * BLOCK + LANES
        low, high = max(first, 0), min(last, n_cols)
        out_ref[rows, j * BLOCK : (j + 1) * BLOCK] = jnp.dot(
            mix[:, low:high], table_ref[j, low - first : high - first, :], preferred_element_type=f32
        ).astype(bf16)


def contract_rows(table, source):
    return lax.dot_general(
        table, source, (((0,), (0,)), ((), ())), preferred_element_type=f32
    ).astype(bf16)


def middle_kernel(all_rows, place, sec, row_shift, row_frac, col_shift, col_frac, mid_ref, table_ref):
    n_rows, n_cols = sec.shape
    tile = place[1]
    base = tile * n_rows
    ids = lax.broadcasted_iota(jnp.int32, (1, n_rows), 1) + base
    pos = source_positions(ids, row_shift[...], row_frac[...], all_rows - 2, base)
    pos = pos[:, MARGIN : n_rows - MARGIN]
    coord = lax.broadcasted_iota(jnp.int32, (n_rows, pos.shape[1]), 0).astype(f32)
    mix = contract_rows(hat(coord, pos).astype(bf16), sec[...])
    window = BLOCK + 2 * LANES
    reach = window - LANES
    coord = lax.broadcasted_iota(jnp.int32, (reach, BLOCK), 0).astype(f32)
    ids = lax.broadcasted_iota(jnp.int32, (1, BLOCK), 1)
    edge = jnp.zeros((LANES // 2, BLOCK), bf16)
    for j in range(n_cols // BLOCK):
        cols = slice(j * BLOCK, (j + 1) * BLOCK)
        pos = source_positions(
            ids + j * BLOCK, col_shift[:, cols], col_frac[:, cols], n_cols - 2, j * BLOCK - LANES // 2
        )
        table_ref[j, 0 : LANES // 2, :] = edge
        table_ref[j, LANES // 2 : LANES // 2 + reach, :] = hat(coord, pos).astype(bf16)
        table_ref[j, LANES // 2 + reach :, :] = edge
    columns_from(mix, table_ref, mid_ref, slice(None))


def edges_kernel(all_rows, place, first, second, sec, row_shift, row_frac, table_ref, edge_ref):
    n_rows = sec.shape[0]
    tile = place[1]
    base = tile * n_rows
    even = tile % 2 == 0
    half = n_rows // 2
    ids = lax.broadcasted_iota(jnp.int32, (1, n_rows), 1) + base
    pos = source_positions(ids, row_shift[...], row_frac[...], all_rows - 2, base)
    slot = lax.broadcasted_iota(jnp.int32, (MARGIN, MARGIN), 0)
    own = lax.broadcasted_iota(jnp.int32, (half, MARGIN), 0)
    mixes = []
    for top in (True, False):
        near = slot - MARGIN if top else slot + n_rows
        in_first = even != top
        coord = jnp.concatenate(
            [
                jnp.where(in_first, near, FAR),
                jnp.where(in_first, FAR, near),
                own if top else own + half,
            ],
            axis=0,
        ).astype(f32)
        here = pos[:, :MARGIN] if top else pos[:, n_rows - MARGIN :]
        stack = jnp.concatenate(
            [first[...], second[...], sec[0:half, :] if top else sec[half:, :]], axis=0
        )
        mixes.append(contract_rows(hat(coord, here).astype(bf16), stack))
    columns_from(jnp.concatenate(mixes, axis=0), table_ref, edge_ref, slice(None))


def window_kernel(place, peaks, mid, edge, old_mid, old_edge, boundary, smooth, out_ref, ext, acc, peak, whole, sem):
    n_mid, n_cols = mid.shape
    n_rows = n_mid + edge.shape[0]
    patch_rows, patch_cols = n_rows // PATCH, n_cols // PATCH
    n_patches = patch_rows * patch_cols
    pad = 16

    def parts_of(i):
        start, stop = i * PATCH, (i + 1) * PATCH
        pieces = []
        for is_edge, low, high, shift in (
            (True, 0, MARGIN, 0),
            (False, MARGIN, n_rows - MARGIN, MARGIN),
            (True, n_rows - MARGIN, n_rows, n_mid),
        ):
            a, b = max(start, low), min(stop, high)
            if a < b:
                pieces.append((is_edge, a - shift, b - a))
        return pieces

    def fill(p, block):
        ext[p, pad : pad + PATCH, :] = block
        ext[p, 0:pad, :] = block[PATCH - pad :, :]
        ext[p, pad + PATCH :, :] = block[:pad, :]

    def block_of(i, lanes, mid_source, edge_source):
        return jnp.concatenate(
            [(edge_source if is_edge else mid_source)[a : a + n, lanes] for is_edge, a, n in parts_of(i)], axis=0
        ).astype(f32)

    @pl.when(place[0] == 0)
    def _():
        copy = pltpu.make_async_copy(boundary, whole, sem)
        copy.start()
        copy.wait()
        for i in range(patch_rows):

            @pl.loop(0, patch_cols)
            def _(j):
                lanes = pl.ds(pl.multiple_of(j * PATCH, PATCH), PATCH)
                fill(i * patch_cols + j, whole[i * PATCH : (i + 1) * PATCH, lanes].astype(f32))

    @pl.when(place[0] != 0)
    def _():
        for i in range(patch_rows):

            @pl.loop(0, patch_cols)
            def _(j):
                lanes = pl.ds(pl.multiple_of(j * PATCH, PATCH), PATCH)
                fill(i * patch_cols + j, block_of(i, lanes, old_mid, old_edge))

    for i in range(patch_rows):

        @pl.loop(0, patch_cols)
        def _(j):
            p = i * patch_cols + j
            lanes = pl.ds(pl.multiple_of(j * PATCH, PATCH), PATCH)
            peak_row, peak_col = peaks[0, p], peaks[1, p]
            peak[0, pl.ds(p, 1), :] = jnp.full((1, LANES), peak_row, jnp.int32).astype(f32)
            peak[1, pl.ds(p, 1), :] = jnp.full((1, LANES), peak_col, jnp.int32).astype(f32)
            sums = [None] * 9
            current = block_of(i, lanes, mid, edge)
            for r in range(PATCH // 8):
                rows = current[8 * r : 8 * r + 8, :]
                turned = [pltpu.roll(rows, (peak_col + dx) % PATCH, 1) for dx in (-1, 0, 1)]
                for dy in (-1, 0, 1):
                    old = ext[p, pl.ds(peak_row + (pad + dy + 8 * r), 8), :]
                    for dx in range(3):
                        k = (dy + 1) * 3 + dx
                        term = turned[dx] * old
                        sums[k] = term if sums[k] is None else sums[k] + term
            for k in range(9):
                acc[pl.ds(pl.multiple_of((k * n_patches + p) * 8, 8), 8), :] = sums[k]

    total = acc[pl.ds(0, 9 * n_patches, stride=8), :]
    for s in range(1, 8):
        total = total + acc[pl.ds(s, 9 * n_patches, stride=8), :]
    weights = jnp.maximum(jnp.sum(total, axis=1, keepdims=True) * (1.0 / PATCH), 0.0)
    w = [weights[k * n_patches : (k + 1) * n_patches] for k in range(9)]
    scale = 1.0 / jnp.maximum(sum(w), 1.0)
    moves = (
        (w[6] + w[7] + w[8] - w[0] - w[1] - w[2]) * scale,
        (w[2] + w[5] + w[8] - w[0] - w[3] - w[6]) * scale,
    )
    out_ref[...] = jnp.zeros_like(out_ref)
    for c in range(2):
        flow = moves[c] + peak[c]
        for i in range(patch_rows):
            row = flow[i * patch_cols : (i + 1) * patch_cols, :] * smooth[...]
            out_ref[c * patch_rows + i : c * patch_rows + i + 1, :] = jnp.sum(row, axis=0, keepdims=True)


def partner_of(tile, n, d, second):
    up = (tile // d) % 2 == int(second)
    return (tile + jnp.where(up, d, -d) + n) % n


def rows_kernel(n_ty, swaps, place, *refs):
    blocks, out_ref = refs[:-1], refs[-1]
    patch_rows, patch_cols = out_ref.shape[2], out_ref.shape[3]
    all_rows = n_ty * patch_rows
    tile = place[1]
    depth = 8 * len(blocks)
    at = lax.broadcasted_iota(jnp.int32, (8, depth), 0)
    slot = lax.broadcasted_iota(jnp.int32, (8, depth), 1)
    holder = jnp.full((8, depth), tile, jnp.int32)
    for k, (d, second) in enumerate(swaps):
        holder = jnp.where((slot >> 3) == k + 1, partner_of(tile, n_ty, d, second), holder)
    slot = slot & 7
    c_out = (at >= patch_rows).astype(jnp.int32)
    c_in = (slot >= patch_rows).astype(jnp.int32)
    row = tile * patch_rows + at - c_out * patch_rows
    source = holder * patch_rows + slot - c_in * patch_rows

    def inside(r):
        return (r >= 0) & (r < all_rows)

    def tap(delta):
        size = jnp.abs(delta)
        return jnp.where(
            size == 0, TAPS[2], jnp.where(size == 1, TAPS[1], jnp.where(size == 2, TAPS[0], 0.0))
        )

    def norm(r):
        return sum(jnp.where(inside(r + o), TAPS[o + 2], 0.0) for o in range(-2, 3))

    weight = jnp.zeros((8, depth), f32)
    for o in range(-2, 3):
        weight = weight + jnp.where(inside(row + o), TAPS[o + 2] * tap(source - row - o) / norm(row + o), 0.0)
    used = (slot < 2 * patch_rows) & (at < 2 * patch_rows) & (c_in == c_out) & inside(source)
    weight = jnp.where(used, weight / norm(row), 0.0)
    stack = jnp.concatenate([b[...] for b in blocks], axis=0)
    result = jnp.dot(weight, stack, precision=lax.Precision.HIGHEST, preferred_element_type=f32)
    for c in range(2):
        out_ref[c, 0] = result[c * patch_rows : (c + 1) * patch_rows, :patch_cols]


def column_smoother(n):
    kernel = np.zeros((n, n))
    for i in range(n):
        for o in range(-2, 3):
            if 0 <= i + o < n:
                kernel[i, i + o] = TAPS[o + 2]
    kernel = kernel / kernel.sum(1, keepdims=True)
    table = np.zeros((n, LANES), np.float32)
    table[:, :n] = np.linalg.matrix_power(kernel, SMOOTH_PASSES).T
    return table


def call(body, out_shape, in_specs, out_specs, scratch=(), flops=0, moved=0):
    return pl.pallas_call(
        body,
        out_shape=out_shape,
        in_specs=in_specs,
        out_specs=out_specs,
        scratch_shapes=scratch,
        compiler_params=pltpu.CompilerParams(vmem_limit_bytes=VMEM_LIMIT),
        cost_estimate=pl.CostEstimate(flops=flops, bytes_accessed=moved, transcendentals=0),
    )


def local(sections, boundary, row_shift, row_frac, col_shift, col_frac, peak_shift):
    section = sections[0]
    n_rows, n_cols = section.shape
    n_ty, n_gz = lax.axis_size("ty"), lax.axis_size("gz")
    patch_rows, patch_cols = n_rows // PATCH, n_cols // PATCH
    n_patches = patch_rows * patch_cols
    gz, ty = lax.axis_index("gz"), lax.axis_index("ty")
    all_rows = n_rows * n_ty
    place = jnp.stack([gz, ty]).astype(jnp.int32)
    vmem = pl.BlockSpec(memory_space=pltpu.VMEM)
    smem = pl.BlockSpec(memory_space=pltpu.SMEM)

    even = ty % 2 == 0
    tops, bottoms = section[:MARGIN], section[n_rows - MARGIN :]
    first = lax.ppermute(jnp.where(even, bottoms, tops), ("gz", "ty"), halo_pairs(n_gz, n_ty, False))
    second = lax.ppermute(jnp.where(even, tops, bottoms), ("gz", "ty"), halo_pairs(n_gz, n_ty, True))

    n_mid = n_rows - 2 * MARGIN
    table_shape = (n_cols // BLOCK, BLOCK + 2 * LANES, BLOCK)
    mid, table = call(
        functools.partial(middle_kernel, all_rows),
        (jax.ShapeDtypeStruct((n_mid, n_cols), bf16), jax.ShapeDtypeStruct(table_shape, bf16)),
        [smem] + [vmem] * 5,
        (vmem, vmem),
    )(place, section, row_shift, row_frac, col_shift, col_frac)

    to_next = [(i, (i + 1) % n_gz) for i in range(n_gz)]
    old_mid = lax.ppermute(mid, "gz", to_next)
    edge = call(
        functools.partial(edges_kernel, all_rows),
        jax.ShapeDtypeStruct((2 * MARGIN, n_cols), bf16),
        [smem] + [vmem] * 6,
        vmem,
    )(place, first, second, section, row_shift, row_frac, table)
    old_edge = lax.ppermute(edge, "gz", to_next)
    rendered = jnp.concatenate([edge[:MARGIN], mid, edge[MARGIN:]], axis=0)[None]

    payload = call(
        window_kernel,
        jax.ShapeDtypeStruct((8, LANES), f32),
        [smem, smem] + [vmem] * 4 + [pl.BlockSpec(memory_space=pl.ANY), vmem],
        vmem,
        [
            pltpu.VMEM((n_patches, PATCH + 32, LANES), f32),
            pltpu.VMEM((9 * n_patches * 8, LANES), f32),
            pltpu.VMEM((2, n_patches, LANES), f32),
            pltpu.VMEM((n_rows, n_cols), bf16),
            pltpu.SemaphoreType.DMA,
        ],
    )(
        place,
        peak_shift.reshape(2, n_patches),
        mid,
        edge,
        old_mid,
        old_edge,
        boundary,
        jnp.asarray(column_smoother(patch_cols)),
    )

    swaps, seen, blocks = [], set(), [payload]
    for d in range(1, -(-2 * SMOOTH_PASSES // patch_rows) + 1):
        for other in (False, True):
            pairs = swap_pairs(n_ty, d, other)
            if pairs and pairs not in seen:
                seen.add(pairs)
                swaps.append((d, other))
                blocks.append(lax.ppermute(payload, "ty", both_ways(pairs)))
    flow = call(
        functools.partial(rows_kernel, n_ty, tuple(swaps)),
        jax.ShapeDtypeStruct((2, 1, patch_rows, patch_cols), f32),
        [smem] + [vmem] * len(blocks),
        vmem,
    )(place, *blocks)
    return rendered, flow


def solution(mesh):
    in_specs = (
        P(("parts", "gz"), "ty", None),
        P(("parts", "ty"), None),
        P(("parts", "gz"), "ty"),
        P(("parts", "gz"), "ty"),
        P(("parts", "gz"), None),
        P(("parts", "gz"), None),
        P(None, ("parts", "gz"), "ty", None),
    )
    out_specs = (P(("parts", "gz"), "ty", None), P(None, ("parts", "gz"), "ty", None))
    return jax.shard_map(local, mesh=mesh, in_specs=in_specs, out_specs=out_specs, check_vma=False)
```

profile of v0, /device:TPU:0, one launch (start us, length us, event | category | flops | bytes accessed | tf_op | source)
XLA Modules:
  0.0 40.0 jit_solution(12261524504065959544)
XLA Ops:
  0.6 1.1 %select_bitcast_fusion = (bf16[64,2048]{1,0:T(8,128)(2,1)S(1)}, bf16[64,2048]{1,0:T(8,128)(2,1)S(1)}) fusion(pred[]{:T(512)S(6)} %eq.5, bf16[1,256,2048]{2,1,0:T(8,128)(2,1)} %param.8), kind=kLoop, calls=%fused_computation.1 | loop fusion | flops 262144 | bytes 1048577 | tf_op jit(solution)/shard_map/jit(_where)/select_n | solution.py:309
  1.7 3.1 %collective-permute-start = (bf16[64,2048]{1,0:T(8,128)(2,1)S(1)}, bf16[64,2048]{1,0:T(8,128)(2,1)S(1)}, u32[]{:S(2)}, u32[]{:S(2)}) collective-permute-start(bf16[64,2048]{1,0:T(8,128)(2,1)S(1)} %get-tuple-element.7), channel_id=1, source_target_pairs={{0,1},{1,0},{2,3},{3,2},{4,5},{5,4},{6,7},{7,6},{8,9},{9,8},{10,11... | collective-permute-start | bytes 786440 | tf_op jit(solution)/shard_map/ppermute | solution.py:308
  4.8 0.0 collective-permute-start.1
  4.8 0.1 pad_add_fusion.place
  4.9 0.0 copy-start
  4.9 1.2 %copy-done = bf16[1,256,2048]{2,1,0:T(8,128)(2,1)S(1)} copy-done((bf16[1,256,2048]{2,1,0:T(8,128)(2,1)S(1)}, bf16[1,256,2048]{2,1,0:T(8,128)(2,1)}, u32[]{:S(2)}) %copy-start) | copy-done | bytes 1048600
  6.1 0.0 copy-start.2
  6.1 0.7 %copy-done.2 = s32[1,2048]{1,0:T(1,128)S(1)} copy-done((s32[1,2048]{1,0:T(1,128)S(1)}, s32[1,2048]{1,0:T(1,128)}, u32[]{:S(2)}) %copy-start.2) | copy-done | bytes 8216
  6.8 0.0 copy-start.3
  6.8 0.7 %copy-done.3 = s32[1,2048]{1,0:T(1,128)S(1)} copy-done((s32[1,2048]{1,0:T(1,128)S(1)}, s32[1,2048]{1,0:T(1,128)}, u32[]{:S(2)}) %copy-start.3) | copy-done | bytes 8216
  7.5 0.0 copy-start.5
  7.5 0.7 %copy-done.5 = s32[1,256]{1,0:T(1,128)S(1)} copy-done((s32[1,256]{1,0:T(1,128)S(1)}, s32[1,256]{1,0:T(1,128)}, u32[]{:S(2)}) %copy-start.5) | copy-done | bytes 1048
  8.2 0.0 copy-start.6
  8.2 0.7 %copy-done.6 = s32[1,256]{1,0:T(1,128)S(1)} copy-done((s32[1,256]{1,0:T(1,128)S(1)}, s32[1,256]{1,0:T(1,128)}, u32[]{:S(2)}) %copy-start.6) | copy-done | bytes 1048
  8.9 1.6 %shard_map.95 = (bf16[128,2048]{1,0:T(8,128)(2,1)S(1)}, bf16[8,512,256]{2,1,0:T(8,128)(2,1)S(1)}) custom-call(s32[2]{0:T(128)S(1)} %pad_add_fusion.place, bf16[256,2048]{1,0:T(8,128)(2,1)S(1)} %bitcast.9, s32[1,256]{1,0:T(1,128)S(1)} %copy-done.5, s32[1,256]{1,0:T(1,128)S(1)} %copy-done.6, s32[1,2048]{1,0:T(1,128)S(1)} %copy-done.2, s32[1,2048]{1,0:T(1,128)S(1)} %copy-done.3), custom_call_target="tpu_custom_call" | custom-call | tf_op jit(solution)/shard_map/pallas_call | solution.py:313
  10.5 0.6 %collective-permute-start.2 = (bf16[128,2048]{1,0:T(8,128)(2,1)S(1)}, bf16[128,2048]{1,0:T(8,128)(2,1)S(1)}, u32[]{:S(2)}, u32[]{:S(2)}) collective-permute-start(bf16[128,2048]{1,0:T(8,128)(2,1)S(1)} %get-tuple-element.5.mid), channel_id=1, source_target_pairs={{0,4},{4,8},{8,12},{12,0},{1,5},{5,9},{9,13},{13,1},{2,6},{6,10},{... | collective-permute-start | bytes 1572872 | tf_op jit(solution)/shard_map/ppermute | solution.py:321
  11.1 0.0 collective-permute-done.first
  11.1 0.0 collective-permute-done.1.second
  11.1 0.0 copy-start.7
  11.1 0.0 copy-start.1
  11.1 0.0 copy-start.4
  11.1 1.4 %shard_map.96.edge = bf16[128,2048]{1,0:T(8,128)(2,1)S(1)} custom-call(s32[2]{0:T(128)S(1)} %pad_add_fusion.place, bf16[64,2048]{1,0:T(8,128)(2,1)S(1)} %collective-permute-done.first, bf16[64,2048]{1,0:T(8,128)(2,1)S(1)} %collective-permute-done.1.second, bf16[256,2048]{1,0:T(8,128)(2,1)S(1)} %bitcast.10, s32[1,256]{1,0:T(1,128)S(1)} %copy-done.5, ...), custom_call_target="tpu_custom_call" | custom-call | tf_op jit(solution)/shard_map/pallas_call | solution.py:322
  12.5 1.1 %collective-permute-start.3 = (bf16[128,2048]{1,0:T(8,128)(2,1)S(1)}, bf16[128,2048]{1,0:T(8,128)(2,1)S(1)}, u32[]{:S(2)}, u32[]{:S(2)}) collective-permute-start(bf16[128,2048]{1,0:T(8,128)(2,1)S(1)} %shard_map.96.edge), channel_id=1, source_target_pairs={{0,4},{4,8},{8,12},{12,0},{1,5},{5,9},{9,13},{13,1},{2,6},{6,10},{... | collective-permute-start | bytes 1572872 | tf_op jit(solution)/shard_map/ppermute | solution.py:328
  13.7 0.0 copy-done.7
  13.7 0.1 reshape.13.peaks
  13.8 5.4 %collective-permute-done.2.old_mid = bf16[128,2048]{1,0:T(8,128)(2,1)S(1)} collective-permute-done((bf16[128,2048]{1,0:T(8,128)(2,1)S(1)}, bf16[128,2048]{1,0:T(8,128)(2,1)S(1)}, u32[]{:S(2)}, u32[]{:S(2)}) %collective-permute-start.2) | collective-permute-done | bytes 524320 | tf_op jit(solution)/shard_map/ppermute | solution.py:321
  19.2 5.6 %collective-permute-done.3.old_edge = bf16[128,2048]{1,0:T(8,128)(2,1)S(1)} collective-permute-done((bf16[128,2048]{1,0:T(8,128)(2,1)S(1)}, bf16[128,2048]{1,0:T(8,128)(2,1)S(1)}, u32[]{:S(2)}, u32[]{:S(2)}) %collective-permute-start.3) | collective-permute-done | bytes 524320 | tf_op jit(solution)/shard_map/ppermute | solution.py:328
  24.8 0.0 copy-done.1
  24.8 0.0 copy-done.4
  24.8 5.2 %shard_map.97.refs_0_ = f32[8,128]{1,0:T(8,128)S(1)} custom-call(s32[2]{0:T(128)S(1)} %pad_add_fusion.place, s32[2,32]{1,0:T(2,128)S(1)} %reshape.13.peaks, bf16[128,2048]{1,0:T(8,128)(2,1)S(1)} %get-tuple-element.5.mid, bf16[128,2048]{1,0:T(8,128)(2,1)S(1)} %shard_map.96.edge, bf16[128,2048]{1,0:T(8,128)(2,1)S(1)} %collective-permute-done.2.old_mid, ...), custom_call_target="tpu_custom_call" | custom-call | tf_op jit(solution)/shard_map/pallas_call | solution.py:331
  30.0 3.2 %collective-permute-start.4 = (f32[8,128]{1,0:T(8,128)S(1)}, f32[8,128]{1,0:T(8,128)S(1)}, u32[]{:S(2)}, u32[]{:S(2)}) collective-permute-start(f32[8,128]{1,0:T(8,128)S(1)} %shard_map.97.refs_0_), channel_id=1, source_target_pairs={{0,1},{1,0},{2,3},{3,2},{4,5},{5,4},{6,7},{7,6},{8,9},{9,8},{10,11... | collective-permute-start | bytes 12296 | tf_op jit(solution)/shard_map/ppermute | solution.py:361
  33.2 0.9 %collective-permute-start.5 = (f32[8,128]{1,0:T(8,128)S(1)}, f32[8,128]{1,0:T(8,128)S(1)}, u32[]{:S(2)}, u32[]{:S(2)}) collective-permute-start(f32[8,128]{1,0:T(8,128)S(1)} %shard_map.97.refs_0_), channel_id=1, source_target_pairs={{0,3},{1,2},{2,1},{3,0},{4,7},{5,6},{6,5},{7,4},{8,11},{9,10},{10,... | collective-permute-start | bytes 12296 | tf_op jit(solution)/shard_map/ppermute | solution.py:361
  34.1 0.6 %collective-permute-start.6 = (f32[8,128]{1,0:T(8,128)S(1)}, f32[8,128]{1,0:T(8,128)S(1)}, u32[]{:S(2)}, u32[]{:S(2)}) collective-permute-start(f32[8,128]{1,0:T(8,128)S(1)} %shard_map.97.refs_0_), channel_id=1, source_target_pairs={{0,2},{1,3},{2,0},{3,1},{4,6},{5,7},{6,4},{7,5},{8,10},{9,11},{10,... | collective-permute-start | bytes 12296 | tf_op jit(solution)/shard_map/ppermute | solution.py:361
  34.7 1.0 %maximum_bitcast_fusion = bf16[1,256,2048]{2,1,0:T(8,128)(2,1)} fusion(bf16[64,2048]{1,0:T(8,128)(2,1)S(1)} %get-tuple-element.9, bf16[128,2048]{1,0:T(8,128)(2,1)S(1)} %get-tuple-element.5.mid, bf16[64,2048]{1,0:T(8,128)(2,1)S(1)} %get-tuple-element.8), kind=kLoop, calls=%fused_computation | loop fusion | flops 3145728 | bytes 2097152 | tf_op jit(solution)/shard_map/broadcast_in_dim | solution.py:329
  35.8 0.0 collective-permute-done.4.refs_1_
  35.8 2.8 %collective-permute-done.5.refs_2_ = f32[8,128]{1,0:T(8,128)S(1)} collective-permute-done((f32[8,128]{1,0:T(8,128)S(1)}, f32[8,128]{1,0:T(8,128)S(1)}, u32[]{:S(2)}, u32[]{:S(2)}) %collective-permute-start.5) | collective-permute-done | bytes 4128 | tf_op jit(solution)/shard_map/ppermute | solution.py:361
  38.6 0.1 collective-permute-done.6.refs_3_
  38.7 1.3 %shard_map.98 = f32[2,1,2,16]{3,2,1,0:T(2,128)} custom-call(s32[2]{0:T(128)S(1)} %pad_add_fusion.place, f32[8,128]{1,0:T(8,128)S(1)} %shard_map.97.refs_0_, f32[8,128]{1,0:T(8,128)S(1)} %collective-permute-done.4.refs_1_, f32[8,128]{1,0:T(8,128)S(1)} %collective-permute-done.5.refs_2_, f32[8,128]{1,0:T(8,128)S(1)} %collective-permute-done.6.refs_3_), custom_call_target="tpu_custom_call" | custom-call | tf_op jit(solution)/shard_map/pallas_call | solution.py:362
  (1 shorter events, 0.0 us)
Async XLA Ops:
  1.7 9.4 %collective-permute-start = (bf16[64,2048]{1,0:T(8,128)(2,1)S(1)}, bf16[64,2048]{1,0:T(8,128)(2,1)S(1)}, u32[]{:S(2)}, u32[]{:S(2)}) collective-permute-start(bf16[64,2048]{1,0:T(8,128)(2,1)S(1)} %get-tuple-element.7), channel_id=1, source_target_pairs={{0,1},{1,0},{2,3},{3,2},{4,5},{5,4},{6,7},{7,6},{8,9},{9,8},{10,11... | collective-permute-start | bytes 786440 | tf_op jit(solution)/shard_map/ppermute | solution.py:308
  4.8 6.3 %collective-permute-start.1 = (bf16[64,2048]{1,0:T(8,128)(2,1)S(1)}, bf16[64,2048]{1,0:T(8,128)(2,1)S(1)}, u32[]{:S(2)}, u32[]{:S(2)}) collective-permute-start(bf16[64,2048]{1,0:T(8,128)(2,1)S(1)} %get-tuple-element.6), channel_id=1, source_target_pairs={{0,4},{1,2},{2,1},{3,7},{4,0},{5,6},{6,5},{7,3},{8,12},{9,10},{10,... | collective-permute-start | bytes 786440 | tf_op jit(solution)/shard_map/ppermute | solution.py:309
  4.9 1.2 %copy-start = (bf16[1,256,2048]{2,1,0:T(8,128)(2,1)S(1)}, bf16[1,256,2048]{2,1,0:T(8,128)(2,1)}, u32[]{:S(2)}) copy-start(bf16[1,256,2048]{2,1,0:T(8,128)(2,1)} %param.8) | copy-start | bytes 3145732
  6.1 0.7 %copy-start.2 = (s32[1,2048]{1,0:T(1,128)S(1)}, s32[1,2048]{1,0:T(1,128)}, u32[]{:S(2)}) copy-start(s32[1,2048]{1,0:T(1,128)} %col_shift.1) | copy-start | bytes 24580
  6.8 0.7 %copy-start.3 = (s32[1,2048]{1,0:T(1,128)S(1)}, s32[1,2048]{1,0:T(1,128)}, u32[]{:S(2)}) copy-start(s32[1,2048]{1,0:T(1,128)} %col_frac.1) | copy-start | bytes 24580
  7.5 0.7 %copy-start.5 = (s32[1,256]{1,0:T(1,128)S(1)}, s32[1,256]{1,0:T(1,128)}, u32[]{:S(2)}) copy-start(s32[1,256]{1,0:T(1,128)} %row_shift.3) | copy-start | bytes 3076
  8.2 0.7 %copy-start.6 = (s32[1,256]{1,0:T(1,128)S(1)}, s32[1,256]{1,0:T(1,128)}, u32[]{:S(2)}) copy-start(s32[1,256]{1,0:T(1,128)} %row_frac.3) | copy-start | bytes 3076
  10.5 8.7 %collective-permute-start.2 = (bf16[128,2048]{1,0:T(8,128)(2,1)S(1)}, bf16[128,2048]{1,0:T(8,128)(2,1)S(1)}, u32[]{:S(2)}, u32[]{:S(2)}) collective-permute-start(bf16[128,2048]{1,0:T(8,128)(2,1)S(1)} %get-tuple-element.5.mid), channel_id=1, source_target_pairs={{0,4},{4,8},{8,12},{12,0},{1,5},{5,9},{9,13},{13,1},{2,6},{6,10},{... | collective-permute-start | bytes 1572872 | tf_op jit(solution)/shard_map/ppermute | solution.py:321
  11.1 2.6 %copy-start.7 = (s32[2,1,2,16]{3,2,1,0:T(2,128)S(1)}, s32[2,1,2,16]{3,2,1,0:T(2,128)}, u32[]{:S(2)}) copy-start(s32[2,1,2,16]{3,2,1,0:T(2,128)} %param.14) | copy-start | bytes 772
  11.1 13.7 %copy-start.1 = (bf16[256,2048]{1,0:T(8,128)(2,1)S(1)}, bf16[256,2048]{1,0:T(8,128)(2,1)}, u32[]{:S(2)}) copy-start(bf16[256,2048]{1,0:T(8,128)(2,1)} %boundary.1) | copy-start | bytes 3145732
  11.1 13.7 %copy-start.4 = (f32[16,128]{1,0:T(8,128)S(1)}, f32[16,128]{1,0:T(8,128)}, u32[]{:S(2)}) copy-start(f32[16,128]{1,0:T(8,128)} %constant.23.clone.smooth) | copy-start | bytes 24580
  12.5 12.2 %collective-permute-start.3 = (bf16[128,2048]{1,0:T(8,128)(2,1)S(1)}, bf16[128,2048]{1,0:T(8,128)(2,1)S(1)}, u32[]{:S(2)}, u32[]{:S(2)}) collective-permute-start(bf16[128,2048]{1,0:T(8,128)(2,1)S(1)} %shard_map.96.edge), channel_id=1, source_target_pairs={{0,4},{4,8},{8,12},{12,0},{1,5},{5,9},{9,13},{13,1},{2,6},{6,10},{... | collective-permute-start | bytes 1572872 | tf_op jit(solution)/shard_map/ppermute | solution.py:328
  30.0 5.8 %collective-permute-start.4 = (f32[8,128]{1,0:T(8,128)S(1)}, f32[8,128]{1,0:T(8,128)S(1)}, u32[]{:S(2)}, u32[]{:S(2)}) collective-permute-start(f32[8,128]{1,0:T(8,128)S(1)} %shard_map.97.refs_0_), channel_id=1, source_target_pairs={{0,1},{1,0},{2,3},{3,2},{4,5},{5,4},{6,7},{7,6},{8,9},{9,8},{10,11... | collective-permute-start | bytes 12296 | tf_op jit(solution)/shard_map/ppermute | solution.py:361
  33.2 5.4 %collective-permute-start.5 = (f32[8,128]{1,0:T(8,128)S(1)}, f32[8,128]{1,0:T(8,128)S(1)}, u32[]{:S(2)}, u32[]{:S(2)}) collective-permute-start(f32[8,128]{1,0:T(8,128)S(1)} %shard_map.97.refs_0_), channel_id=1, source_target_pairs={{0,3},{1,2},{2,1},{3,0},{4,7},{5,6},{6,5},{7,4},{8,11},{9,10},{10,... | collective-permute-start | bytes 12296 | tf_op jit(solution)/shard_map/ppermute | solution.py:361
  34.1 4.6 %collective-permute-start.6 = (f32[8,128]{1,0:T(8,128)S(1)}, f32[8,128]{1,0:T(8,128)S(1)}, u32[]{:S(2)}, u32[]{:S(2)}) collective-permute-start(f32[8,128]{1,0:T(8,128)S(1)} %shard_map.97.refs_0_), channel_id=1, source_target_pairs={{0,2},{1,3},{2,0},{3,1},{4,6},{5,7},{6,4},{7,5},{8,10},{9,11},{10,... | collective-permute-start | bytes 12296 | tf_op jit(solution)/shard_map/ppermute | solution.py:361
where the time goes:
time: 40.3 us; the launch traced here: 40 us
  waiting for transfers between devices  14 us (35%)
  starting transfers between devices  9.53 us (24%)
  Pallas kernels  9.53 us (24%)
  local copies, waits for them, and re-layouts  4.1 us (10%)
  other arithmetic  2.18 us (5%)
  between operations  0.7 us (2%)
    ppermute x1, waiting for transfers between devices, local(): old_edge = lax.ppermute(edge, 'gz', to_next)  5.62 us
    ppermute x1, waiting for transfers between devices, local(): old_mid = lax.ppermute(mid, 'gz', to_next)  5.37 us
    pallas_call x1, Pallas kernels, local(): call(window_kernel, jax.ShapeDtypeStruct((8, LANES), f32), [smem, smem] +...  5.19 us
    ppermute x3, starting transfers between devices, local(): blocks.append(lax.ppermute(payload, 'ty', both_ways(pairs)))  4.76 us
    unnamed x16, local copies, waits for them, and re-layouts  3.99 us
    ppermute x1, starting transfers between devices, local(): lax.ppermute(jnp.where(even, bottoms, tops), ('gz', 'ty'), halo_pairs(n_g...  3.09 us
    ppermute x3, waiting for transfers between devices, local(): blocks.append(lax.ppermute(payload, 'ty', both_ways(pairs)))  2.91 us
    pallas_call x1, Pallas kernels, local(): call(functools.partial(middle_kernel, all_rows), (jax.ShapeDtypeStruct((n...  1.64 us
  transfers between devices with their start and end apart: 7, of which 4 were waited for; matrix products, arithmetic and copies ran while one was open for 3% of the time, Pallas kernels for 8%

commit v1 on v0

v1 whole, which is shorter than its diff:
```python
import functools

import jax
import jax.numpy as jnp
import numpy as np
from jax import lax
from jax.experimental import pallas as pl
from jax.experimental.pallas import tpu as pltpu
from jax.sharding import PartitionSpec as P

PATCH = 128
MARGIN = 64
SMOOTH_PASSES = 2
BLOCK = 256
LANES = 128
TAPS = (0.0625, 0.25, 0.375, 0.25, 0.0625)
FAR = 1 << 20
VMEM_LIMIT = 40 * 1024 * 1024

f32 = jnp.float32
bf16 = jnp.bfloat16


def swap_pairs(n, d, second):
    pairs = []
    for i in range(n):
        if (i // d) % 2 == int(second):
            j = i + d
            if j >= n:
                if not second or n % (2 * d):
                    continue
                j -= n
            pairs.append((i, j))
    return frozenset(frozenset(p) for p in pairs)


def both_ways(pairs):
    return sorted([tuple(sorted(p)) for p in pairs] + [tuple(sorted(p))[::-1] for p in pairs])


def halo_pairs(n_gz, n_ty, second):
    table = []
    for z in range(n_gz):
        for t in range(n_ty):
            partner = t + 1 if (t % 2 == 0) != second else t - 1
            if 0 <= partner < n_ty:
                table.append((z * n_ty + t, z * n_ty + partner))
            elif (z ^ 1) < n_gz:
                table.append((z * n_ty + t, (z ^ 1) * n_ty + t))
    return table


def hat(coord, position):
    return jnp.maximum(1.0 - jnp.abs(coord - position), 0.0)


def source_positions(ids, shift, frac, limit, base):
    source = jnp.clip(ids + shift, 0, limit) - base
    return source.astype(f32) + frac.astype(f32) * (1.0 / 256.0)


def contract_rows(table, source):
    return lax.dot_general(
        table, source, (((0,), (0,)), ((), ())), preferred_element_type=f32
    ).astype(bf16)


def columns_from(mix, start, table_ref, blocks, out_ref):
    for at, j in enumerate(blocks):
        first = j * BLOCK - LANES
        low, high = max(first, start), min(first + BLOCK + 2 * LANES, start + mix.shape[1])
        out_ref[:, at * BLOCK : (at + 1) * BLOCK] = jnp.dot(
            mix[:, low - start : high - start],
            table_ref[j, low - first : high - first, :],
            preferred_element_type=f32,
        ).astype(bf16)


def fetch_kernel(all_rows, section, row_shift, row_frac, col_shift, col_frac, *rest):
    held, send_first, send_second, mid_table, top_table, bottom_table, col_table = rest[:7]
    row_shift_v, row_frac_v, col_shift_v, col_frac_v, sems = rest[7:]
    n_rows, n_cols = section.shape
    tile = lax.axis_index("ty")
    base = tile * n_rows
    even = tile % 2 == 0
    low, high = 0, n_rows - MARGIN
    first_at = pl.multiple_of(jnp.where(even, high, low), MARGIN)
    second_at = pl.multiple_of(jnp.where(even, low, high), MARGIN)
    copies = [
        pltpu.make_async_copy(source, target, sems.at[k])
        for k, (source, target) in enumerate(
            (
                (col_shift, col_shift_v),
                (col_frac, col_frac_v),
                (row_shift, row_shift_v),
                (row_frac, row_frac_v),
                (section.at[pl.ds(first_at, MARGIN), :], send_first),
                (section.at[pl.ds(second_at, MARGIN), :], send_second),
                (section, held),
            )
        )
    ]
    for copy in copies:
        copy.start()
    for copy in copies[:4]:
        copy.wait()

    window = BLOCK + 2 * LANES
    reach = window - LANES
    coord = lax.broadcasted_iota(jnp.int32, (reach, BLOCK), 0).astype(f32)
    ids = lax.broadcasted_iota(jnp.int32, (1, BLOCK), 1)
    edge = jnp.zeros((LANES // 2, BLOCK), bf16)
    for j in range(n_cols // BLOCK):
        cols = slice(j * BLOCK, (j + 1) * BLOCK)
        pos = source_positions(
            ids + j * BLOCK, col_shift_v[:, cols], col_frac_v[:, cols], n_cols - 2, j * BLOCK - LANES // 2
        )
        col_table[j, 0 : LANES // 2, :] = edge
        col_table[j, LANES // 2 : LANES // 2 + reach, :] = hat(coord, pos).astype(bf16)
        col_table[j, LANES // 2 + reach :, :] = edge

    ids = lax.broadcasted_iota(jnp.int32, (1, n_rows), 1) + base
    pos = source_positions(ids, row_shift_v[...], row_frac_v[...], all_rows - 2, base)
    coord = lax.broadcasted_iota(jnp.int32, (n_rows, n_rows - 2 * MARGIN), 0).astype(f32)
    mid_table[...] = hat(coord, pos[:, MARGIN : n_rows - MARGIN]).astype(bf16)
    half = n_rows // 2
    slot = lax.broadcasted_iota(jnp.int32, (MARGIN, MARGIN), 0)
    own = lax.broadcasted_iota(jnp.int32, (half, MARGIN), 0)
    for top, table in ((True, top_table), (False, bottom_table)):
        near = slot - MARGIN if top else slot + n_rows
        in_first = even != top
        coord = jnp.concatenate(
            [
                jnp.where(in_first, near, FAR),
                jnp.where(in_first, FAR, near),
                own if top else own + half,
            ],
            axis=0,
        ).astype(f32)
        here = pos[:, :MARGIN] if top else pos[:, n_rows - MARGIN :]
        table[...] = hat(coord, here).astype(bf16)
    for copy in copies[4:]:
        copy.wait()


def middle_kernel(held, mid_table, col_table, mid_ref):
    mix = contract_rows(mid_table[...], held[...])
    columns_from(mix, 0, col_table, range(held.shape[1] // BLOCK), mid_ref)


def edges_kernel(blocks, first, second, held, top_table, bottom_table, col_table, *rest):
    edge_ref = rest[-1]
    n_rows, n_cols = held.shape
    half = n_rows // 2
    low = max(blocks[0] * BLOCK - LANES, 0)
    high = min((blocks[-1] + 1) * BLOCK + LANES, n_cols)
    mixes = []
    for table, own in ((top_table, slice(0, half)), (bottom_table, slice(half, n_rows))):
        stack = jnp.concatenate([first[:, low:high], second[:, low:high], held[own, low:high]], axis=0)
        mixes.append(contract_rows(table[...], stack))
    columns_from(jnp.concatenate(mixes, axis=0), low, col_table, blocks, edge_ref)


def pieces_of(i, n_rows):
    start, stop = i * PATCH, (i + 1) * PATCH
    pieces = []
    for is_edge, low, high, shift in (
        (True, 0, MARGIN, 0),
        (False, MARGIN, n_rows - MARGIN, MARGIN),
        (True, n_rows - MARGIN, n_rows, n_rows - 2 * MARGIN),
    ):
        a, b = max(start, low), min(stop, high)
        if a < b:
            pieces.append((is_edge, a - shift, b - a))
    return pieces


PAD = 16


def turned_kernel(n_ty, swaps, peaks, mid, *rest):
    edges, (rendered, turned, row_weights, sems) = rest[:-4], rest[-4:]
    n_mid, n_cols = mid.shape
    n_rows = n_mid + 2 * MARGIN
    patch_rows, patch_cols = n_rows // PATCH, n_cols // PATCH
    n_patches = patch_rows * patch_cols
    wide = n_cols // len(edges)
    moves = [(mid, rendered.at[pl.ds(MARGIN, n_mid), :])]
    for h, edge in enumerate(edges):
        cols = pl.ds(h * wide, wide)
        moves.append((edge.at[pl.ds(0, MARGIN), :], rendered.at[pl.ds(0, MARGIN), cols]))
        moves.append((edge.at[pl.ds(MARGIN, MARGIN), :], rendered.at[pl.ds(n_rows - MARGIN, MARGIN), cols]))
    copies = [pltpu.make_async_copy(a, b, sems.at[k]) for k, (a, b) in enumerate(moves)]
    for copy in copies:
        copy.start()
    fill_row_weights(n_ty, swaps, patch_rows, row_weights)
    for i in range(patch_rows):
        for h, edge in enumerate(edges):

            @pl.loop(0, wide // PATCH)
            def _(j):
                p = i * patch_cols + h * (wide // PATCH) + j
                here = pl.ds(pl.multiple_of(j * PATCH, PATCH), PATCH)
                there = pl.ds(pl.multiple_of(h * wide + j * PATCH, PATCH), PATCH)
                block = jnp.concatenate(
                    [edge[a : a + n, here] if is_edge else mid[a : a + n, there] for is_edge, a, n in pieces_of(i, n_rows)],
                    axis=0,
                ).astype(f32)
                for dx in range(3):
                    moved = pltpu.roll(block, (peaks[1, p] + (dx - 1)) % PATCH, 1)
                    q = dx * n_patches + p
                    turned[q, PAD : PAD + PATCH, :] = moved
                    turned[q, 0:PAD, :] = moved[PATCH - PAD :, :]
                    turned[q, PAD + PATCH :, :] = moved[:PAD, :]

    for copy in copies:
        copy.wait()


def window_kernel(h, n_halves, peaks, turned, old_mid, old_edge, boundary, smooth, *rest):
    before, (out_ref, acc, peak, whole, sem) = rest[:-5], rest[-5:]
    n_rows = boundary.shape[0]
    wide = old_edge.shape[1]
    patch_rows, here_cols = n_rows // PATCH, wide // PATCH
    patch_cols = here_cols * n_halves
    n_patches = patch_rows * patch_cols
    n_here = patch_rows * here_cols

    def sum_windows(block_of):
        for i in range(patch_rows):

            @pl.loop(0, here_cols)
            def _(j):
                p = i * patch_cols + h * here_cols + j
                at = i * here_cols + j
                peak_row, peak_col = peaks[0, p], peaks[1, p]
                peak[0, pl.ds(at, 1), :] = jnp.full((1, LANES), peak_row, jnp.int32).astype(f32)
                peak[1, pl.ds(at, 1), :] = jnp.full((1, LANES), peak_col, jnp.int32).astype(f32)
                sums = [None] * 9
                old = block_of(i, j)
                for r in range(PATCH // 8):
                    rows = old[8 * r : 8 * r + 8, :]
                    for dx in range(3):
                        for dy in range(3):
                            k = dy * 3 + dx
                            start = (PAD + 8 * r - (dy - 1)) - peak_row
                            term = turned[dx * n_patches + p, pl.ds(start, 8), :] * rows
                            sums[k] = term if sums[k] is None else sums[k] + term
                for k in range(9):
                    acc[pl.ds(pl.multiple_of((k * n_here + at) * 8, 8), 8), :] = sums[k]

    @pl.when(lax.axis_index("gz") == 0)
    def _():
        copy = pltpu.make_async_copy(boundary.at[:, pl.ds(h * wide, wide)], whole, sem)
        copy.start()
        copy.wait()
        sum_windows(
            lambda i, j: whole[
                i * PATCH : (i + 1) * PATCH, pl.ds(pl.multiple_of(j * PATCH, PATCH), PATCH)
            ].astype(f32)
        )

    @pl.when(lax.axis_index("gz") != 0)
    def _():
        def block_of(i, j):
            here = pl.ds(pl.multiple_of(j * PATCH, PATCH), PATCH)
            there = pl.ds(pl.multiple_of(h * wide + j * PATCH, PATCH), PATCH)
            return jnp.concatenate(
                [
                    old_edge[a : a + n, here] if is_edge else old_mid[a : a + n, there]
                    for is_edge, a, n in pieces_of(i, n_rows)
                ],
                axis=0,
            ).astype(f32)

        sum_windows(block_of)

    total = acc[pl.ds(0, 9 * n_here, stride=8), :]
    for s in range(1, 8):
        total = total + acc[pl.ds(s, 9 * n_here, stride=8), :]
    weights = jnp.maximum(jnp.sum(total, axis=1, keepdims=True) * (1.0 / PATCH), 0.0)
    w = [weights[k * n_here : (k + 1) * n_here] for k in range(9)]
    scale = 1.0 / jnp.maximum(sum(w), 1.0)
    moves = (
        (w[6] + w[7] + w[8] - w[0] - w[1] - w[2]) * scale,
        (w[2] + w[5] + w[8] - w[0] - w[3] - w[6]) * scale,
    )
    lines = []
    share = smooth[h * here_cols : (h + 1) * here_cols, :]
    for c in range(2):
        flow = moves[c] + peak[c]
        for i in range(patch_rows):
            row = flow[i * here_cols : (i + 1) * here_cols, :] * share
            lines.append(jnp.sum(row, axis=0, keepdims=True))
    lines.append(jnp.zeros((8 - len(lines), LANES), f32))
    result = jnp.concatenate(lines, axis=0)
    for b in before:
        result = result + b[...]
    out_ref[...] = result


def partner_of(tile, n, d, second):
    up = (tile // d) % 2 == int(second)
    return (tile + jnp.where(up, d, -d) + n) % n


def fill_row_weights(n_ty, swaps, patch_rows, out_ref):
    all_rows = n_ty * patch_rows
    tile = lax.axis_index("ty")
    held = 2 * patch_rows
    depth = LANES
    at = lax.broadcasted_iota(jnp.int32, (8, depth), 0)
    slot = lax.broadcasted_iota(jnp.int32, (8, depth), 1)
    holder = jnp.full((8, depth), tile, jnp.int32)
    for k, (d, second) in enumerate(swaps):
        holder = jnp.where((slot >> 3) == k + 1, partner_of(tile, n_ty, d, second), holder)
    inner = slot & 7
    c_out = (at >= patch_rows).astype(jnp.int32)
    c_in = (inner >= patch_rows).astype(jnp.int32)
    row = tile * patch_rows + at - c_out * patch_rows
    source = holder * patch_rows + inner - c_in * patch_rows

    def inside(r):
        return (r >= 0) & (r < all_rows)

    def tap(delta):
        size = jnp.abs(delta)
        return jnp.where(
            size == 0, TAPS[2], jnp.where(size == 1, TAPS[1], jnp.where(size == 2, TAPS[0], 0.0))
        )

    def norm(r):
        return sum(jnp.where(inside(r + o), TAPS[o + 2], 0.0) for o in range(-2, 3))

    weight = jnp.zeros((8, depth), f32)
    for o in range(-2, 3):
        weight = weight + jnp.where(inside(row + o), TAPS[o + 2] * tap(source - row - o) / norm(row + o), 0.0)
    used = (inner < held) & (at < held) & (c_in == c_out) & inside(source)
    weight = jnp.where(used, weight / norm(row), 0.0)
    for k in range(len(swaps) + 1):
        for b in range(held):
            out_ref[k * held + b] = jnp.broadcast_to(weight[:, 8 * k + b : 8 * k + b + 1], (8, LANES))


def rows_kernel(row_weights, *refs):
    blocks, out_ref = refs[:-1], refs[-1]
    patch_rows, patch_cols = out_ref.shape[2], out_ref.shape[3]
    held = 2 * patch_rows
    result = None
    for k, block in enumerate(blocks):
        for b in range(held):
            term = row_weights[k * held + b] * block[b : b + 1, :]
            result = term if result is None else result + term
    for c in range(2):
        out_ref[c, 0] = result[c * patch_rows : (c + 1) * patch_rows, :patch_cols]


def column_smoother(n):
    kernel = np.zeros((n, n))
    for i in range(n):
        for o in range(-2, 3):
            if 0 <= i + o < n:
                kernel[i, i + o] = TAPS[o + 2]
    kernel = kernel / kernel.sum(1, keepdims=True)
    table = np.zeros((n, LANES), np.float32)
    table[:, :n] = np.linalg.matrix_power(kernel, SMOOTH_PASSES).T
    return table


def call(body, out_shape, in_specs, out_specs, scratch=(), flops=0, moved=0):
    return pl.pallas_call(
        body,
        out_shape=out_shape,
        in_specs=in_specs,
        out_specs=out_specs,
        scratch_shapes=scratch,
        compiler_params=pltpu.CompilerParams(vmem_limit_bytes=VMEM_LIMIT),
        cost_estimate=pl.CostEstimate(flops=flops, bytes_accessed=moved, transcendentals=0),
    )


def local(sections, boundary, row_shift, row_frac, col_shift, col_frac, peak_shift):
    section = sections[0]
    n_rows, n_cols = section.shape
    n_ty, n_gz = lax.axis_size("ty"), lax.axis_size("gz")
    patch_rows, patch_cols = n_rows // PATCH, n_cols // PATCH
    n_patches = patch_rows * patch_cols
    all_rows = n_rows * n_ty
    n_mid, half = n_rows - 2 * MARGIN, n_rows // 2
    n_blocks = n_cols // BLOCK
    vmem = pl.BlockSpec(memory_space=pltpu.VMEM)
    smem = pl.BlockSpec(memory_space=pltpu.SMEM)
    hbm = pl.BlockSpec(memory_space=pltpu.HBM)
    shape = jax.ShapeDtypeStruct

    held, send_first, send_second, mid_table, top_table, bottom_table, col_table = call(
        functools.partial(fetch_kernel, all_rows),
        (
            shape((n_rows, n_cols), bf16),
            shape((MARGIN, n_cols), bf16),
            shape((MARGIN, n_cols), bf16),
            shape((n_rows, n_mid), bf16),
            shape((2 * MARGIN + half, MARGIN), bf16),
            shape((2 * MARGIN + half, MARGIN), bf16),
            shape((n_blocks, BLOCK + 2 * LANES, BLOCK), bf16),
        ),
        [hbm] * 5,
        [vmem] * 7,
        [
            pltpu.VMEM((1, n_rows), jnp.int32),
            pltpu.VMEM((1, n_rows), jnp.int32),
            pltpu.VMEM((1, n_cols), jnp.int32),
            pltpu.VMEM((1, n_cols), jnp.int32),
            pltpu.SemaphoreType.DMA((7,)),
        ],
    )(*(pltpu.with_memory_space_constraint(x, pltpu.HBM) for x in (section, row_shift, row_frac, col_shift, col_frac)))
    first = lax.ppermute(send_first, ("gz", "ty"), halo_pairs(n_gz, n_ty, False))
    second = lax.ppermute(send_second, ("gz", "ty"), halo_pairs(n_gz, n_ty, True))

    mid = call(middle_kernel, shape((n_mid, n_cols), bf16), [vmem] * 3, vmem)(held, mid_table, col_table)
    to_next = [(i, (i + 1) % n_gz) for i in range(n_gz)]
    old_mid = lax.ppermute(mid, "gz", to_next)

    halves = 2
    wide = n_cols // halves
    edges, old_edges = [], []
    for h in range(halves):
        blocks = tuple(range(h * n_blocks // halves, (h + 1) * n_blocks // halves))
        edges.append(
            call(
                functools.partial(edges_kernel, blocks),
                shape((2 * MARGIN, wide), bf16),
                [vmem] * 6 + [pl.BlockSpec(memory_space=pl.ANY)] * h,
                vmem,
            )(first, second, held, top_table, bottom_table, col_table, *edges[-1:])
        )
        old_edges.append(lax.ppermute(edges[h], "gz", to_next))

    swaps, seen, tables = [], set(), []
    for d in range(1, -(-2 * SMOOTH_PASSES // patch_rows) + 1):
        for other in (False, True):
            pairs = swap_pairs(n_ty, d, other)
            if pairs and pairs not in seen:
                seen.add(pairs)
                swaps.append((d, other))
                tables.append(both_ways(pairs))
    peaks = peak_shift.reshape(2, n_patches)
    terms = (len(swaps) + 1) * 2 * patch_rows
    rendered, turned, row_weights = call(
        functools.partial(turned_kernel, n_ty, tuple(swaps)),
        (
            shape((n_rows, n_cols), bf16),
            shape((3 * n_patches, PATCH + 2 * PAD, LANES), f32),
            shape((terms, 8, LANES), f32),
        ),
        [smem] + [vmem] * (1 + halves),
        [hbm, vmem, vmem],
        [pltpu.SemaphoreType.DMA((1 + 2 * halves,))],
        flops=4_000_000_000,
        moved=12_000_000,
    )(peaks, mid, *edges)

    payload = []
    smooth = jnp.asarray(column_smoother(patch_cols))
    n_here = n_patches // halves
    for h in range(halves):
        payload = [
            call(
                functools.partial(window_kernel, h, halves),
                shape((8, LANES), f32),
                [smem] + [vmem] * 3 + [hbm] + [vmem] * (1 + len(payload)),
                vmem,
                [
                    pltpu.VMEM((9 * n_here * 8, LANES), f32),
                    pltpu.VMEM((2, n_here, LANES), f32),
                    pltpu.VMEM((n_rows, wide), bf16),
                    pltpu.SemaphoreType.DMA,
                ],
            )(peaks, turned, old_mid, old_edges[h], boundary, smooth, *payload)
        ]
    blocks = payload + [lax.ppermute(payload[0], "ty", table) for table in tables]
    flow = call(
        rows_kernel, shape((2, 1, patch_rows, patch_cols), f32), [vmem] * (1 + len(blocks)), vmem
    )(row_weights, *blocks)
    return rendered[None], flow


def solution(mesh):
    in_specs = (
        P(("parts", "gz"), "ty", None),
        P(("parts", "ty"), None),
        P(("parts", "gz"), "ty"),
        P(("parts", "gz"), "ty"),
        P(("parts", "gz"), None),
        P(("parts", "gz"), None),
        P(None, ("parts", "gz"), "ty", None),
    )
    out_specs = (P(("parts", "gz"), "ty", None), P(None, ("parts", "gz"), "ty", None))
    return jax.shard_map(local, mesh=mesh, in_specs=in_specs, out_specs=out_specs, check_vma=False)
```

time: 40.3 us -> 38.6 us (0.958)
  Pallas kernels: 9.53 us -> 17.4 us
  waiting for transfers between devices: 14 us -> 8.36 us
  local copies, waits for them, and re-layouts: 4.1 us -> 0.77 us
  other arithmetic: 2.18 us -> 0 us
  starting transfers between devices: 9.53 us -> 11 us
    pallas_call x4 -> x8, Pallas kernels: 9.53 us -> 17.4 us  [the longest x2 5.51 us: local(): call(functools.partial(window_kernel, h, halves), shape((8, LANES), f32),...]
    ppermute x1, waiting for transfers between devices: 5.37 us -> 0.01 us  [local(): old_mid = lax.ppermute(mid, 'gz', to_next)]
    unnamed x16 -> x4, local copies, waits for them, and re-layouts: 3.99 us -> 0.01 us
    ppermute x6 -> x7, starting transfers between devices: 8.97 us -> 10.5 us  [the longest x3 5.52 us: local(): lax.ppermute(payload[0], 'ty', table)]
    select_n x1 -> x0, other arithmetic: 1.07 us -> none  [local(): jnp.where(even, tops, bottoms)]
    broadcast_in_dim x1 -> x0, other arithmetic: 1.04 us -> none  [local(): jnp.concatenate([edge[:MARGIN], mid, edge[MARGIN:]], axis=0)[None]]
    reshape x1, local copies, waits for them, and re-layouts: 0.08 us -> 0.76 us  [local(): peaks = peak_shift.reshape(2, n_patches)]
    ppermute x6 -> x7, waiting for transfers between devices: 8.58 us -> 8.36 us  [the longest x3 4.5 us: local(): lax.ppermute(payload[0], 'ty', table)]
  transfers between devices with their start and end apart: 7 -> 8, of which waited for: 4 -> 3; matrix products, arithmetic and copies ran while one was open for 3% -> 2% of each run, Pallas kernels for 8% -> 30%
where the time goes in v1:
time: 38.6 us; the launch traced here: 38.2 us
  Pallas kernels  17.4 us (45%)
  starting transfers between devices  11 us (28%)
  waiting for transfers between devices  8.36 us (22%)
  local copies, waits for them, and re-layouts  0.77 us (2%)
  between operations  0.74 us (2%)
    ppermute x3, starting transfers between devices, local(): lax.ppermute(payload[0], 'ty', table)  5.52 us
    pallas_call x2, Pallas kernels, local(): call(functools.partial(window_kernel, h, halves), shape((8, LANES), f32),...  5.51 us
    ppermute x3, waiting for transfers between devices, local(): lax.ppermute(payload[0], 'ty', table)  4.5 us
    pallas_call x1, Pallas kernels, local(): call(functools.partial(turned_kernel, n_ty, tuple(swaps)), (shape((n_rows...  4.49 us
    ppermute x1, waiting for transfers between devices, local(): lax.ppermute(send_first, ('gz', 'ty'), halo_pairs(n_gz, n_ty, False))  3.85 us
    ppermute x1, starting transfers between devices, local(): lax.ppermute(send_first, ('gz', 'ty'), halo_pairs(n_gz, n_ty, False))  3.09 us
    pallas_call x2, Pallas kernels, local(): call(functools.partial(edges_kernel, blocks), shape((2 * MARGIN, wide), b...  2.98 us
    pallas_call x1, Pallas kernels, local(): call(functools.partial(fetch_kernel, all_rows), (shape((n_rows, n_cols),...  2.39 us
  transfers between devices with their start and end apart: 8, of which 3 were waited for; matrix products, arithmetic and copies ran while one was open for 2% of the time, Pallas kernels for 30%

profile of v1, /device:TPU:0, one launch (start us, length us, event | category | flops | bytes accessed | tf_op | source)
XLA Modules:
  0.0 38.2 jit_solution(8666743551170982395)
XLA Ops:
  0.6 2.4 %shard_map.95 = (bf16[256,2048]{1,0:T(8,128)(2,1)S(1)}, bf16[64,2048]{1,0:T(8,128)(2,1)}, bf16[64,2048]{1,0:T(8,128)(2,1)}, bf16[256,128]{1,0:T(8,128)(2,1)S(1)}...) custom-call(bf16[256,2048]{1,0:T(8,128)(2,1)} %bitcast.2, ...), custom_call_target="tpu_custom_call" | custom-call | tf_op jit(solution)/shard_map/pallas_call | solution.py:396
  3.0 3.1 %collective-permute-start = (bf16[64,2048]{1,0:T(8,128)(2,1)}, bf16[64,2048]{1,0:T(8,128)(2,1)S(1)}, u32[]{:S(2)}, u32[]{:S(2)}) collective-permute-start(bf16[64,2048]{1,0:T(8,128)(2,1)} %get-tuple-element.15), channel_id=1, source_target_pairs={{0,1},{1,0},{2,3},{3,2},{4,5},{5,4},{6,7},{7,6},{8,9},{9,8},{10,11... | collective-permute-start | bytes 786440 | tf_op jit(solution)/shard_map/ppermute | solution.py:417
  6.1 0.0 collective-permute-start.1
  6.1 1.4 %shard_map.96.mid = bf16[128,2048]{1,0:T(8,128)(2,1)} custom-call(bf16[256,2048]{1,0:T(8,128)(2,1)S(1)} %get-tuple-element.12.held, bf16[256,128]{1,0:T(8,128)(2,1)S(1)} %get-tuple-element.13.mid_table, bf16[8,512,256]{2,1,0:T(8,128)(2,1)S(1)} %get-tuple-element.14.col_table), custom_call_target="tpu_custom_call" | custom-call | tf_op jit(solution)/shard_map/pallas_call | solution.py:420
  7.5 0.5 %collective-permute-start.2 = (bf16[128,2048]{1,0:T(8,128)(2,1)}, bf16[128,2048]{1,0:T(8,128)(2,1)}, u32[]{:S(2)}, u32[]{:S(2)}) collective-permute-start(bf16[128,2048]{1,0:T(8,128)(2,1)} %shard_map.96.mid), channel_id=1, source_target_pairs={{0,4},{4,8},{8,12},{12,0},{1,5},{5,9},{9,13},{13,1},{2,6},{6,10},{... | collective-permute-start | bytes 1572872 | tf_op jit(solution)/shard_map/ppermute | solution.py:422
  8.0 0.8 %reshape.7.peaks = s32[2,32]{1,0:T(2,128)S(1)} reshape(s32[2,1,2,16]{3,2,1,0:T(2,128)} %param.14) | data formatting | bytes 512 | tf_op jit(solution)/shard_map/reshape | solution.py:447
  8.8 3.8 %collective-permute-done.first = bf16[64,2048]{1,0:T(8,128)(2,1)S(1)} collective-permute-done((bf16[64,2048]{1,0:T(8,128)(2,1)}, bf16[64,2048]{1,0:T(8,128)(2,1)S(1)}, u32[]{:S(2)}, u32[]{:S(2)}) %collective-permute-start) | collective-permute-done | bytes 262176 | tf_op jit(solution)/shard_map/ppermute | solution.py:417
  12.6 0.0 collective-permute-done.1.second
  12.6 1.5 %shard_map.97.rest_0_ = bf16[128,1024]{1,0:T(8,128)(2,1)S(1)} custom-call(bf16[64,2048]{1,0:T(8,128)(2,1)S(1)} %collective-permute-done.first, bf16[64,2048]{1,0:T(8,128)(2,1)} %collective-permute-done.1.second, bf16[256,2048]{1,0:T(8,128)(2,1)S(1)} %get-tuple-element.12.held, bf16[256,64]{1,0:T(8,128)(2,1)S(1)} %get-tuple-element.17.top_table, ...), custom_call_target="tpu_custom_call" | custom-call | tf_op jit(solution)/shard_map/pallas_call | solution.py:430
  14.1 0.1 collective-permute-start.4
  14.2 1.5 %shard_map.98.rest_1_ = bf16[128,1024]{1,0:T(8,128)(2,1)S(1)} custom-call(bf16[64,2048]{1,0:T(8,128)(2,1)S(1)} %collective-permute-done.first, bf16[64,2048]{1,0:T(8,128)(2,1)} %collective-permute-done.1.second, bf16[256,2048]{1,0:T(8,128)(2,1)S(1)} %get-tuple-element.12.held, bf16[256,64]{1,0:T(8,128)(2,1)S(1)} %get-tuple-element.17.top_table, ...), custom_call_target="tpu_custom_call" | custom-call | tf_op jit(solution)/shard_map/pallas_call | solution.py:430
  15.7 0.0 copy-start
  15.7 0.0 copy-start.1
  15.7 1.8 %collective-permute-start.3 = (bf16[128,1024]{1,0:T(8,128)(2,1)S(1)}, bf16[128,1024]{1,0:T(8,128)(2,1)S(1)}, u32[]{:S(2)}, u32[]{:S(2)}) collective-permute-start(bf16[128,1024]{1,0:T(8,128)(2,1)S(1)} %shard_map.98.rest_1_), channel_id=1, source_target_pairs={{0,4},{4,8},{8,12},{12,0},{1,5},{5,9},{9,13},{13,1},{2,6},{6,10},{... | collective-permute-start | bytes 786440 | tf_op jit(solution)/shard_map/ppermute | solution.py:437
  17.5 4.5 %shard_map.99 = (bf16[256,2048]{1,0:T(8,128)(2,1)}, f32[96,160,128]{2,1,0:T(8,128)S(1)}, f32[16,8,128]{2,1,0:T(8,128)S(1)}) custom-call(s32[2,32]{1,0:T(2,128)S(1)} %reshape.7.peaks, bf16[128,2048]{1,0:T(8,128)(2,1)} %shard_map.96.mid, bf16[128,1024]{1,0:T(8,128)(2,1)S(1)} %shard_map.97.rest_0_, bf16[128,1024]{1,0:T(8,128)(2,1)S(1)} %shard_map.98.rest_1_), custom_call_target="tpu_custom_call" | custom-call | flops 4000000000 | bytes 12000000 | tf_op jit(solution)/shard_map/pallas_call | solution.py:449
  22.0 0.0 collective-permute-done.2.old_mid
  22.0 0.0 collective-permute-done.4.old_edge
  22.0 0.0 copy-done
  22.1 0.0 copy-done.1
  22.1 2.8 %shard_map.100.rest_0_ = f32[8,128]{1,0:T(8,128)S(1)} custom-call(s32[2,32]{1,0:T(2,128)S(1)} %reshape.7.peaks, f32[96,160,128]{2,1,0:T(8,128)S(1)} %get-tuple-element.21.turned, bf16[128,2048]{1,0:T(8,128)(2,1)} %collective-permute-done.2.old_mid, bf16[128,1024]{1,0:T(8,128)(2,1)S(1)} %collective-permute-done.4.old_edge, bf16[256,2048]{1,0:T(8,128)(2,1)S(1)} %copy-done, ...), custom_call_target="tpu_custom_call" | custom-call | tf_op jit(solution)/shard_map/pallas_call | solution.py:468
  24.8 0.0 collective-permute-done.3.old_edge
  24.8 2.8 %shard_map.101.refs_0_ = f32[8,128]{1,0:T(8,128)S(1)} custom-call(s32[2,32]{1,0:T(2,128)S(1)} %reshape.7.peaks, f32[96,160,128]{2,1,0:T(8,128)S(1)} %get-tuple-element.21.turned, bf16[128,2048]{1,0:T(8,128)(2,1)} %collective-permute-done.2.old_mid, bf16[128,1024]{1,0:T(8,128)(2,1)S(1)} %collective-permute-done.3.old_edge, bf16[256,2048]{1,0:T(8,128)(2,1)S(1)} %copy-done, ...), custom_call_target="tpu_custom_call" | custom-call | tf_op jit(solution)/shard_map/pallas_call | solution.py:468
  27.6 2.9 %collective-permute-start.5 = (f32[8,128]{1,0:T(8,128)S(1)}, f32[8,128]{1,0:T(8,128)S(1)}, u32[]{:S(2)}, u32[]{:S(2)}) collective-permute-start(f32[8,128]{1,0:T(8,128)S(1)} %shard_map.101.refs_0_), channel_id=1, source_target_pairs={{0,1},{1,0},{2,3},{3,2},{4,5},{5,4},{6,7},{7,6},{8,9},{9,8},{10,11... | collective-permute-start | bytes 12296 | tf_op jit(solution)/shard_map/ppermute | solution.py:481
  30.5 2.6 %collective-permute-start.6 = (f32[8,128]{1,0:T(8,128)S(1)}, f32[8,128]{1,0:T(8,128)S(1)}, u32[]{:S(2)}, u32[]{:S(2)}) collective-permute-start(f32[8,128]{1,0:T(8,128)S(1)} %shard_map.101.refs_0_), channel_id=1, source_target_pairs={{0,3},{1,2},{2,1},{3,0},{4,7},{5,6},{6,5},{7,4},{8,11},{9,10},{10,... | collective-permute-start | bytes 12296 | tf_op jit(solution)/shard_map/ppermute | solution.py:481
  33.1 0.0 collective-permute-start.7
  33.1 0.0 collective-permute-done.5.refs_1_
  33.1 2.8 %collective-permute-done.6.refs_2_ = f32[8,128]{1,0:T(8,128)S(1)} collective-permute-done((f32[8,128]{1,0:T(8,128)S(1)}, f32[8,128]{1,0:T(8,128)S(1)}, u32[]{:S(2)}, u32[]{:S(2)}) %collective-permute-start.6) | collective-permute-done | bytes 4128 | tf_op jit(solution)/shard_map/ppermute | solution.py:481
  35.9 1.7 %collective-permute-done.7.refs_3_ = f32[8,128]{1,0:T(8,128)S(1)} collective-permute-done((f32[8,128]{1,0:T(8,128)S(1)}, f32[8,128]{1,0:T(8,128)S(1)}, u32[]{:S(2)}, u32[]{:S(2)}) %collective-permute-start.7) | collective-permute-done | bytes 4128 | tf_op jit(solution)/shard_map/ppermute | solution.py:481
  37.6 0.6 %shard_map.102 = f32[2,1,2,16]{3,2,1,0:T(2,128)} custom-call(f32[16,8,128]{2,1,0:T(8,128)S(1)} %get-tuple-element.20.row_weights, f32[8,128]{1,0:T(8,128)S(1)} %shard_map.101.refs_0_, f32[8,128]{1,0:T(8,128)S(1)} %collective-permute-done.5.refs_1_, f32[8,128]{1,0:T(8,128)S(1)} %collective-permute-done.6.refs_2_, f32[8,128]{1,0:T(8,128)S(1)} %collective-permute-done.7.refs_3_), custom_call_target="tpu_custom_call" | custom-call | tf_op jit(solution)/shard_map/pallas_call | solution.py:482
Async XLA Ops:
  3.0 9.6 %collective-permute-start = (bf16[64,2048]{1,0:T(8,128)(2,1)}, bf16[64,2048]{1,0:T(8,128)(2,1)S(1)}, u32[]{:S(2)}, u32[]{:S(2)}) collective-permute-start(bf16[64,2048]{1,0:T(8,128)(2,1)} %get-tuple-element.15), channel_id=1, source_target_pairs={{0,1},{1,0},{2,3},{3,2},{4,5},{5,4},{6,7},{7,6},{8,9},{9,8},{10,11... | collective-permute-start | bytes 786440 | tf_op jit(solution)/shard_map/ppermute | solution.py:417
  6.1 6.5 %collective-permute-start.1 = (bf16[64,2048]{1,0:T(8,128)(2,1)}, bf16[64,2048]{1,0:T(8,128)(2,1)}, u32[]{:S(2)}, u32[]{:S(2)}) collective-permute-start(bf16[64,2048]{1,0:T(8,128)(2,1)} %get-tuple-element.16), channel_id=1, source_target_pairs={{0,4},{1,2},{2,1},{3,7},{4,0},{5,6},{6,5},{7,3},{8,12},{9,10},{10,... | collective-permute-start | bytes 786440 | tf_op jit(solution)/shard_map/ppermute | solution.py:418
  7.5 14.5 %collective-permute-start.2 = (bf16[128,2048]{1,0:T(8,128)(2,1)}, bf16[128,2048]{1,0:T(8,128)(2,1)}, u32[]{:S(2)}, u32[]{:S(2)}) collective-permute-start(bf16[128,2048]{1,0:T(8,128)(2,1)} %shard_map.96.mid), channel_id=1, source_target_pairs={{0,4},{4,8},{8,12},{12,0},{1,5},{5,9},{9,13},{13,1},{2,6},{6,10},{... | collective-permute-start | bytes 1572872 | tf_op jit(solution)/shard_map/ppermute | solution.py:422
  14.1 7.9 %collective-permute-start.4 = (bf16[128,1024]{1,0:T(8,128)(2,1)S(1)}, bf16[128,1024]{1,0:T(8,128)(2,1)S(1)}, u32[]{:S(2)}, u32[]{:S(2)}) collective-permute-start(bf16[128,1024]{1,0:T(8,128)(2,1)S(1)} %shard_map.97.rest_0_), channel_id=1, source_target_pairs={{0,4},{4,8},{8,12},{12,0},{1,5},{5,9},{9,13},{13,1},{2,6},{6,10},{... | collective-permute-start | bytes 786440 | tf_op jit(solution)/shard_map/ppermute | solution.py:437
  15.7 6.4 %copy-start = (bf16[256,2048]{1,0:T(8,128)(2,1)S(1)}, bf16[256,2048]{1,0:T(8,128)(2,1)}, u32[]{:S(2)}) copy-start(bf16[256,2048]{1,0:T(8,128)(2,1)} %boundary.3) | copy-start | bytes 3145732
  15.7 6.4 %copy-start.1 = (f32[16,128]{1,0:T(8,128)S(1)}, f32[16,128]{1,0:T(8,128)}, u32[]{:S(2)}) copy-start(f32[16,128]{1,0:T(8,128)} %constant.2.clone.smooth) | copy-start | bytes 24580
  15.7 9.1 %collective-permute-start.3 = (bf16[128,1024]{1,0:T(8,128)(2,1)S(1)}, bf16[128,1024]{1,0:T(8,128)(2,1)S(1)}, u32[]{:S(2)}, u32[]{:S(2)}) collective-permute-start(bf16[128,1024]{1,0:T(8,128)(2,1)S(1)} %shard_map.98.rest_1_), channel_id=1, source_target_pairs={{0,4},{4,8},{8,12},{12,0},{1,5},{5,9},{9,13},{13,1},{2,6},{6,10},{... | collective-permute-start | bytes 786440 | tf_op jit(solution)/shard_map/ppermute | solution.py:437
  27.6 5.5 %collective-permute-start.5 = (f32[8,128]{1,0:T(8,128)S(1)}, f32[8,128]{1,0:T(8,128)S(1)}, u32[]{:S(2)}, u32[]{:S(2)}) collective-permute-start(f32[8,128]{1,0:T(8,128)S(1)} %shard_map.101.refs_0_), channel_id=1, source_target_pairs={{0,1},{1,0},{2,3},{3,2},{4,5},{5,4},{6,7},{7,6},{8,9},{9,8},{10,11... | collective-permute-start | bytes 12296 | tf_op jit(solution)/shard_map/ppermute | solution.py:481
  30.5 5.4 %collective-permute-start.6 = (f32[8,128]{1,0:T(8,128)S(1)}, f32[8,128]{1,0:T(8,128)S(1)}, u32[]{:S(2)}, u32[]{:S(2)}) collective-permute-start(f32[8,128]{1,0:T(8,128)S(1)} %shard_map.101.refs_0_), channel_id=1, source_target_pairs={{0,3},{1,2},{2,1},{3,0},{4,7},{5,6},{6,5},{7,4},{8,11},{9,10},{10,... | collective-permute-start | bytes 12296 | tf_op jit(solution)/shard_map/ppermute | solution.py:481
  33.1 4.5 %collective-permute-start.7 = (f32[8,128]{1,0:T(8,128)S(1)}, f32[8,128]{1,0:T(8,128)S(1)}, u32[]{:S(2)}, u32[]{:S(2)}) collective-permute-start(f32[8,128]{1,0:T(8,128)S(1)} %shard_map.101.refs_0_), channel_id=1, source_target_pairs={{0,2},{1,3},{2,0},{3,1},{4,6},{5,7},{6,4},{7,5},{8,10},{9,11},{10,... | collective-permute-start | bytes 12296 | tf_op jit(solution)/shard_map/ppermute | solution.py:481

commit v2 on v1

--- a/solution.py
+++ b/solution.py
@@ -16,6 +16,10 @@
 TAPS = (0.0625, 0.25, 0.375, 0.25, 0.0625)
 FAR = 1 << 20
 VMEM_LIMIT = 40 * 1024 * 1024
+UNROLL = 4
+TURN_UNROLL = 4
+WINDOW_UNROLL = 4
+EDGE_FIRST = {2: ((0, MARGIN), (3 * MARGIN, 2 * MARGIN))}
 
 f32 = jnp.float32
 bf16 = jnp.bfloat16
@@ -59,21 +63,8 @@
     return source.astype(f32) + frac.astype(f32) * (1.0 / 256.0)
 
 
-def contract_rows(table, source):
-    return lax.dot_general(
-        table, source, (((0,), (0,)), ((), ())), preferred_element_type=f32
-    ).astype(bf16)
-
-
-def columns_from(mix, start, table_ref, blocks, out_ref):
-    for at, j in enumerate(blocks):
-        first = j * BLOCK - LANES
-        low, high = max(first, start), min(first + BLOCK + 2 * LANES, start + mix.shape[1])
-        out_ref[:, at * BLOCK : (at + 1) * BLOCK] = jnp.dot(
-            mix[:, low - start : high - start],
-            table_ref[j, low - first : high - first, :],
-            preferred_element_type=f32,
-        ).astype(bf16)
+def times(left, right):
+    return jnp.dot(left, right, preferred_element_type=f32).astype(bf16)
 
 
 def fetch_kernel(all_rows, section, row_shift, row_frac, col_shift, col_frac, *rest):
@@ -83,9 +74,8 @@
     tile = lax.axis_index("ty")
     base = tile * n_rows
     even = tile % 2 == 0
-    low, high = 0, n_rows - MARGIN
-    first_at = pl.multiple_of(jnp.where(even, high, low), MARGIN)
-    second_at = pl.multiple_of(jnp.where(even, low, high), MARGIN)
+    first_at = pl.multiple_of(jnp.where(even, n_rows - MARGIN, 0), MARGIN)
+    second_at = pl.multiple_of(jnp.where(even, 0, n_rows - MARGIN), MARGIN)
     copies = [
         pltpu.make_async_copy(source, target, sems.at[k])
         for k, (source, target) in enumerate(
@@ -105,13 +95,14 @@
     for copy in copies[:4]:
         copy.wait()
 
-    window = BLOCK + 2 * LANES
-    reach = window - LANES
+    reach = BLOCK + LANES
     coord = lax.broadcasted_iota(jnp.int32, (reach, BLOCK), 0).astype(f32)
     ids = lax.broadcasted_iota(jnp.int32, (1, BLOCK), 1)
     edge = jnp.zeros((LANES // 2, BLOCK), bf16)
-    for j in range(n_cols // BLOCK):
-        cols = slice(j * BLOCK, (j + 1) * BLOCK)
+
+    @pl.loop(0, n_cols // BLOCK)
+    def _(j):
+        cols = pl.ds(pl.multiple_of(j * BLOCK, BLOCK), BLOCK)
         pos = source_positions(
             ids + j * BLOCK, col_shift_v[:, cols], col_frac_v[:, cols], n_cols - 2, j * BLOCK - LANES // 2
         )
@@ -122,7 +113,7 @@
     ids = lax.broadcasted_iota(jnp.int32, (1, n_rows), 1) + base
     pos = source_positions(ids, row_shift_v[...], row_frac_v[...], all_rows - 2, base)
     coord = lax.broadcasted_iota(jnp.int32, (n_rows, n_rows - 2 * MARGIN), 0).astype(f32)
-    mid_table[...] = hat(coord, pos[:, MARGIN : n_rows - MARGIN]).astype(bf16)
+    mid_table[...] = hat(coord, pos[:, MARGIN : n_rows - MARGIN]).T.astype(bf16)
     half = n_rows // 2
     slot = lax.broadcasted_iota(jnp.int32, (MARGIN, MARGIN), 0)
     own = lax.broadcasted_iota(jnp.int32, (half, MARGIN), 0)
@@ -138,52 +129,93 @@
             axis=0,
         ).astype(f32)
         here = pos[:, :MARGIN] if top else pos[:, n_rows - MARGIN :]
-        table[...] = hat(coord, here).astype(bf16)
+        table[...] = hat(coord, here).T.astype(bf16)
     for copy in copies[4:]:
         copy.wait()
 
 
-def middle_kernel(held, mid_table, col_table, mid_ref):
-    mix = contract_rows(mid_table[...], held[...])
-    columns_from(mix, 0, col_table, range(held.shape[1] // BLOCK), mid_ref)
-
-
-def edges_kernel(blocks, first, second, held, top_table, bottom_table, col_table, *rest):
-    edge_ref = rest[-1]
+def middle_kernel(held, mid_table, col_table, mid_ref, mix):
+    n_blocks = held.shape[1] // BLOCK
+    edge = jnp.zeros((mix.shape[0], LANES), bf16)
+    mix[:, 0:LANES] = edge
+    mix[:, LANES + held.shape[1] :] = edge
+
+    @pl.loop(0, n_blocks, unroll=UNROLL)
+    def _(j):
+        at = pl.multiple_of(j * BLOCK, BLOCK)
+        mix[:, pl.ds(LANES + at, BLOCK)] = times(mid_table[...], held[:, pl.ds(at, BLOCK)])
+
+    @pl.loop(0, n_blocks, unroll=UNROLL)
+    def _(j):
+        at = pl.multiple_of(j * BLOCK, BLOCK)
+        mid_ref[:, pl.ds(at, BLOCK)] = times(mix[:, pl.ds(at, BLOCK + 2 * LANES)], col_table[j])
+
+
+def edges_kernel(h, n_parts, first, second, held, top_table, bottom_table, col_table, *rest):
+    edge_ref, mix = rest[-2:]
     n_rows, n_cols = held.shape
     half = n_rows // 2
-    low = max(blocks[0] * BLOCK - LANES, 0)
-    high = min((blocks[-1] + 1) * BLOCK + LANES, n_cols)
-    mixes = []
-    for table, own in ((top_table, slice(0, half)), (bottom_table, slice(half, n_rows))):
-        stack = jnp.concatenate([first[:, low:high], second[:, low:high], held[own, low:high]], axis=0)
-        mixes.append(contract_rows(table[...], stack))
-    columns_from(jnp.concatenate(mixes, axis=0), low, col_table, blocks, edge_ref)
-
-
-def pieces_of(i, n_rows):
-    start, stop = i * PATCH, (i + 1) * PATCH
-    pieces = []
-    for is_edge, low, high, shift in (
-        (True, 0, MARGIN, 0),
-        (False, MARGIN, n_rows - MARGIN, MARGIN),
-        (True, n_rows - MARGIN, n_rows, n_rows - 2 * MARGIN),
-    ):
-        a, b = max(start, low), min(stop, high)
-        if a < b:
-            pieces.append((is_edge, a - shift, b - a))
-    return pieces
-
-
-PAD = 16
-
-
-def turned_kernel(n_ty, swaps, peaks, mid, *rest):
-    edges, (rendered, turned, row_weights, sems) = rest[:-4], rest[-4:]
+    n_blocks = n_cols // BLOCK // n_parts
+    low = max(h * n_blocks * BLOCK - LANES, 0) // BLOCK * BLOCK
+    high = min(-(-((h + 1) * n_blocks * BLOCK + LANES) // BLOCK) * BLOCK, n_cols)
+    edge = jnp.zeros((2 * MARGIN, LANES), bf16)
+    mix[:, 0:LANES] = edge
+    mix[:, LANES + high - low : 2 * LANES + high - low] = edge
+
+    @pl.loop(0, (high - low) // BLOCK, unroll=UNROLL)
+    def _(j):
+        at = pl.multiple_of(j * BLOCK, BLOCK)
+        here = pl.ds(low + at, BLOCK)
+        for rows, table, own in (
+            (slice(0, MARGIN), top_table, slice(0, half)),
+            (slice(MARGIN, 2 * MARGIN), bottom_table, slice(half, n_rows)),
+        ):
+            stack = jnp.concatenate([first[:, here], second[:, here], held[own, here]], axis=0)
+            mix[rows, pl.ds(LANES + at, BLOCK)] = times(table[...], stack)
+
+    @pl.loop(0, n_blocks, unroll=UNROLL)
+    def _(j):
+        at = pl.multiple_of(j * BLOCK, BLOCK)
+        start = h * n_blocks * BLOCK - low
+        edge_ref[:, pl.ds(at, BLOCK)] = times(
+            mix[:, pl.ds(start + at, BLOCK + 2 * LANES)], col_table[h * n_blocks + j]
+        )
+
+
+def turn_patches(peaks, cols_of, source, turned):
+    n_patches = turned.shape[0] // 3
+    patch_rows = source.shape[0] // MARGIN
+    here_cols = source.shape[1] // PATCH
+    patch_cols = n_patches // patch_rows
+    for i in range(patch_rows):
+
+        @pl.loop(0, here_cols, unroll=TURN_UNROLL)
+        def _(j):
+            p = i * patch_cols + cols_of + j
+            block = source[i * MARGIN : (i + 1) * MARGIN, pl.ds(pl.multiple_of(j * PATCH, PATCH), PATCH)]
+            for dx in range(3):
+                turned[dx * n_patches + p] = pltpu.roll(block, (peaks[1, p] + (dx - 1)) % PATCH, 1)
+
+
+def turn_middle_kernel(n_ty, swaps, peaks, mid, turned, bands, peak, row_weights):
+    n_patches = bands.shape[0]
+    turn_patches(peaks, 0, mid, turned)
+    lane = lax.broadcasted_iota(jnp.int32, (PATCH // 8, LANES), 1)
+    offset = lane - 8 * lax.broadcasted_iota(jnp.int32, (PATCH // 8, LANES), 0) + 1
+
+    @pl.loop(0, n_patches)
+    def _(p):
+        bands[p] = jnp.where(((offset - peaks[0, p]) & (PATCH - 1)) <= 9, 1.0, 0.0)
+        for c in range(2):
+            peak[c, pl.ds(p, 1), :] = jnp.full((1, LANES), peaks[c, p], jnp.int32).astype(f32)
+
+    fill_row_weights(n_ty, swaps, mid.shape[0] // MARGIN, row_weights)
+
+
+def turn_edges_kernel(peaks, mid, *rest):
+    edges, (rendered, turned, sems) = rest[:-3], rest[-3:]
     n_mid, n_cols = mid.shape
     n_rows = n_mid + 2 * MARGIN
-    patch_rows, patch_cols = n_rows // PATCH, n_cols // PATCH
-    n_patches = patch_rows * patch_cols
     wide = n_cols // len(edges)
     moves = [(mid, rendered.at[pl.ds(MARGIN, n_mid), :])]
     for h, edge in enumerate(edges):
@@ -193,87 +225,70 @@
     copies = [pltpu.make_async_copy(a, b, sems.at[k]) for k, (a, b) in enumerate(moves)]
     for copy in copies:
         copy.start()
-    fill_row_weights(n_ty, swaps, patch_rows, row_weights)
-    for i in range(patch_rows):
-        for h, edge in enumerate(edges):
-
-            @pl.loop(0, wide // PATCH)
-            def _(j):
-                p = i * patch_cols + h * (wide // PATCH) + j
-                here = pl.ds(pl.multiple_of(j * PATCH, PATCH), PATCH)
-                there = pl.ds(pl.multiple_of(h * wide + j * PATCH, PATCH), PATCH)
-                block = jnp.concatenate(
-                    [edge[a : a + n, here] if is_edge else mid[a : a + n, there] for is_edge, a, n in pieces_of(i, n_rows)],
-                    axis=0,
-                ).astype(f32)
-                for dx in range(3):
-                    moved = pltpu.roll(block, (peaks[1, p] + (dx - 1)) % PATCH, 1)
-                    q = dx * n_patches + p
-                    turned[q, PAD : PAD + PATCH, :] = moved
-                    turned[q, 0:PAD, :] = moved[PATCH - PAD :, :]
-                    turned[q, PAD + PATCH :, :] = moved[:PAD, :]
-
+    for h, edge in enumerate(edges):
+        turn_patches(peaks, h * (wide // PATCH), edge, turned)
     for copy in copies:
         copy.wait()
 
 
-def window_kernel(h, n_halves, peaks, turned, old_mid, old_edge, boundary, smooth, *rest):
-    before, (out_ref, acc, peak, whole, sem) = rest[:-5], rest[-5:]
+def window_kernel(h, n_parts, turned_mid, turned_edge, bands, peak, old_mid, old_edge, boundary, smooth, *rest):
+    before, (out_ref, acc, whole, sem) = rest[:-4], rest[-4:]
     n_rows = boundary.shape[0]
     wide = old_edge.shape[1]
     patch_rows, here_cols = n_rows // PATCH, wide // PATCH
-    patch_cols = here_cols * n_halves
+    patch_cols = here_cols * n_parts
     n_patches = patch_rows * patch_cols
     n_here = patch_rows * here_cols
-
-    def sum_windows(block_of):
-        for i in range(patch_rows):
-
-            @pl.loop(0, here_cols)
-            def _(j):
-                p = i * patch_cols + h * here_cols + j
-                at = i * here_cols + j
-                peak_row, peak_col = peaks[0, p], peaks[1, p]
-                peak[0, pl.ds(at, 1), :] = jnp.full((1, LANES), peak_row, jnp.int32).astype(f32)
-                peak[1, pl.ds(at, 1), :] = jnp.full((1, LANES), peak_col, jnp.int32).astype(f32)
-                sums = [None] * 9
-                old = block_of(i, j)
-                for r in range(PATCH // 8):
-                    rows = old[8 * r : 8 * r + 8, :]
-                    for dx in range(3):
-                        for dy in range(3):
-                            k = dy * 3 + dx
-                            start = (PAD + 8 * r - (dy - 1)) - peak_row
-                            term = turned[dx * n_patches + p, pl.ds(start, 8), :] * rows
-                            sums[k] = term if sums[k] is None else sums[k] + term
-                for k in range(9):
-                    acc[pl.ds(pl.multiple_of((k * n_here + at) * 8, 8), 8), :] = sums[k]
+    lane = lax.broadcasted_iota(jnp.int32, (8, LANES), 1) - lax.broadcasted_iota(jnp.int32, (8, LANES), 0)
+
+    def sum_windows(old_of):
+        @pl.loop(0, n_here, unroll=WINDOW_UNROLL)
+        def _(at):
+            i, j = at // here_cols, at % here_cols
+            p = i * patch_cols + h * here_cols + j
+            left = []
+            for dx in range(3):
+                left += [turned_edge[dx * n_patches + p], turned_mid[dx * n_patches + p]]
+            products = lax.dot_general(
+                jnp.concatenate(left, axis=0), old_of(i, j), (((1,), (1,)), ((), ())), preferred_element_type=f32
+            )
+            band = bands[p]
+            place = (lane - peak[0, pl.ds(p, 1), :].astype(jnp.int32)) & 15
+            for dx in range(3):
+                lines = [
+                    products[dx * PATCH + 8 * r : dx * PATCH + 8 * r + 8, :] * band[r : r + 1, :]
+                    for r in range(PATCH // 8)
+                ]
+                even, odd = sum(lines[2::2], lines[0]), sum(lines[3::2], lines[1])
+                for dy in range(3):
+                    kept = jnp.where(place == (dy - 1) % 16, even, 0.0) + jnp.where(
+                        place == (dy + 7) % 16, odd, 0.0
+                    )
+                    acc[pl.ds(pl.multiple_of(((dy * 3 + dx) * n_here + at) * 8, 8), 8), :] = kept
+
+    def block(ref, start, col):
+        return ref[pl.ds(pl.multiple_of(start, MARGIN), MARGIN), pl.ds(pl.multiple_of(col, PATCH), PATCH)]
 
     @pl.when(lax.axis_index("gz") == 0)
     def _():
         copy = pltpu.make_async_copy(boundary.at[:, pl.ds(h * wide, wide)], whole, sem)
         copy.start()
         copy.wait()
-        sum_windows(
-            lambda i, j: whole[
-                i * PATCH : (i + 1) * PATCH, pl.ds(pl.multiple_of(j * PATCH, PATCH), PATCH)
-            ].astype(f32)
-        )
+
+        def old_of(i, j):
+            in_order = EDGE_FIRST[patch_rows]
+            starts = [sum(jnp.where(i == k, s[part], 0) for k, s in enumerate(in_order)) for part in range(2)]
+            return jnp.concatenate([block(whole, s, j * PATCH) for s in starts], axis=0)
+
+        sum_windows(old_of)
 
     @pl.when(lax.axis_index("gz") != 0)
     def _():
-        def block_of(i, j):
-            here = pl.ds(pl.multiple_of(j * PATCH, PATCH), PATCH)
-            there = pl.ds(pl.multiple_of(h * wide + j * PATCH, PATCH), PATCH)
-            return jnp.concatenate(
-                [
-                    old_edge[a : a + n, here] if is_edge else old_mid[a : a + n, there]
-                    for is_edge, a, n in pieces_of(i, n_rows)
-                ],
-                axis=0,
-            ).astype(f32)
-
-        sum_windows(block_of)
+        sum_windows(
+            lambda i, j: jnp.concatenate(
+                [block(old_edge, i * MARGIN, j * PATCH), block(old_mid, i * MARGIN, h * wide + j * PATCH)], axis=0
+            )
+        )
 
     total = acc[pl.ds(0, 9 * n_here, stride=8), :]
     for s in range(1, 8):
@@ -288,10 +303,10 @@
     lines = []
     share = smooth[h * here_cols : (h + 1) * here_cols, :]
     for c in range(2):
-        flow = moves[c] + peak[c]
         for i in range(patch_rows):
-            row = flow[i * here_cols : (i + 1) * here_cols, :] * share
-            lines.append(jnp.sum(row, axis=0, keepdims=True))
+            first = i * patch_cols + h * here_cols
+            flow = moves[c][i * here_cols : (i + 1) * here_cols] + peak[c, first : first + here_cols, :]
+            lines.append(jnp.sum(flow * share, axis=0, keepdims=True))
     lines.append(jnp.zeros((8 - len(lines), LANES), f32))
     result = jnp.concatenate(lines, axis=0)
     for b in before:
@@ -399,9 +414,9 @@
             shape((n_rows, n_cols), bf16),
             shape((MARGIN, n_cols), bf16),
             shape((MARGIN, n_cols), bf16),
-            shape((n_rows, n_mid), bf16),
-            shape((2 * MARGIN + half, MARGIN), bf16),
-            shape((2 * MARGIN + half, MARGIN), bf16),
+            shape((n_mid, n_rows), bf16),
+            shape((MARGIN, 2 * MARGIN + half), bf16),
+            shape((MARGIN, 2 * MARGIN + half), bf16),
             shape((n_blocks, BLOCK + 2 * LANES, BLOCK), bf16),
         ),
         [hbm] * 5,
@@ -417,25 +432,6 @@
     first = lax.ppermute(send_first, ("gz", "ty"), halo_pairs(n_gz, n_ty, False))
     second = lax.ppermute(send_second, ("gz", "ty"), halo_pairs(n_gz, n_ty, True))
 
-    mid = call(middle_kernel, shape((n_mid, n_cols), bf16), [vmem] * 3, vmem)(held, mid_table, col_table)
-    to_next = [(i, (i + 1) % n_gz) for i in range(n_gz)]
-    old_mid = lax.ppermute(mid, "gz", to_next)
-
-    halves = 2
-    wide = n_cols // halves
-    edges, old_edges = [], []
-    for h in range(halves):
-        blocks = tuple(range(h * n_blocks // halves, (h + 1) * n_blocks // halves))
-        edges.append(
-            call(
-                functools.partial(edges_kernel, blocks),
-                shape((2 * MARGIN, wide), bf16),
-                [vmem] * 6 + [pl.BlockSpec(memory_space=pl.ANY)] * h,
-                vmem,
-            )(first, second, held, top_table, bottom_table, col_table, *edges[-1:])
-        )
-        old_edges.append(lax.ppermute(edges[h], "gz", to_next))
-
     swaps, seen, tables = [], set(), []
     for d in range(1, -(-2 * SMOOTH_PASSES // patch_rows) + 1):
         for other in (False, True):
@@ -446,37 +442,69 @@
                 tables.append(both_ways(pairs))
     peaks = peak_shift.reshape(2, n_patches)
     terms = (len(swaps) + 1) * 2 * patch_rows
-    rendered, turned, row_weights = call(
-        functools.partial(turned_kernel, n_ty, tuple(swaps)),
+    mid = call(
+        middle_kernel,
+        shape((n_mid, n_cols), bf16),
+        [vmem] * 3,
+        vmem,
+        [pltpu.VMEM((n_mid, n_cols + 2 * LANES), bf16)],
+    )(held, mid_table, col_table)
+    to_next = [(i, (i + 1) % n_gz) for i in range(n_gz)]
+    old_mid = lax.ppermute(mid, "gz", to_next)
+    turned_mid, bands, peak, row_weights = call(
+        functools.partial(turn_middle_kernel, n_ty, tuple(swaps)),
         (
-            shape((n_rows, n_cols), bf16),
-            shape((3 * n_patches, PATCH + 2 * PAD, LANES), f32),
+            shape((3 * n_patches, MARGIN, LANES), bf16),
+            shape((n_patches, PATCH // 8, LANES), f32),
+            shape((2, n_patches, LANES), f32),
             shape((terms, 8, LANES), f32),
         ),
-        [smem] + [vmem] * (1 + halves),
-        [hbm, vmem, vmem],
-        [pltpu.SemaphoreType.DMA((1 + 2 * halves,))],
+        [smem, vmem],
+        [vmem] * 4,
+        flops=1_000_000_000,
+        moved=3_000_000,
+    )(peaks, mid)
+
+    parts = 2
+    wide = n_cols // parts
+    edges, old_edges = [], []
+    for h in range(parts):
+        edges.append(
+            call(
+                functools.partial(edges_kernel, h, parts),
+                shape((2 * MARGIN, wide), bf16),
+                [vmem] * 6 + [pl.BlockSpec(memory_space=pl.ANY)] * h,
+                vmem,
+                [pltpu.VMEM((2 * MARGIN, n_cols + 2 * LANES), bf16)],
+            )(first, second, held, top_table, bottom_table, col_table, *edges[-1:])
+        )
+        old_edges.append(lax.ppermute(edges[h], "gz", to_next))
+    rendered, turned_edge = call(
+        turn_edges_kernel,
+        (shape((n_rows, n_cols), bf16), shape((3 * n_patches, MARGIN, LANES), bf16)),
+        [smem] + [vmem] * (1 + parts),
+        [hbm, vmem],
+        [pltpu.SemaphoreType.DMA((1 + 2 * parts,))],
         flops=4_000_000_000,
-        moved=12_000_000,
+        moved=6_000_000,
     )(peaks, mid, *edges)
 
     payload = []
     smooth = jnp.asarray(column_smoother(patch_cols))
-    n_here = n_patches // halves
-    for h in range(halves):
+    n_here = n_patches // parts
+    for h in range(parts):
         payload = [
             call(
-                functools.partial(window_kernel, h, halves),
+                functools.partial(window_kernel, h, parts),
                 shape((8, LANES), f32),
-                [smem] + [vmem] * 3 + [hbm] + [vmem] * (1 + len(payload)),
+                [vmem] * 6 + [hbm] + [vmem] * (1 + len(payload)),
                 vmem,
                 [
                     pltpu.VMEM((9 * n_here * 8, LANES), f32),
-                    pltpu.VMEM((2, n_here, LANES), f32),
                     pltpu.VMEM((n_rows, wide), bf16),
                     pltpu.SemaphoreType.DMA,
                 ],
-            )(peaks, turned, old_mid, old_edges[h], boundary, smooth, *payload)
+            )(turned_mid, turned_edge, bands, peak, old_mid, old_edges[h], boundary, smooth, *payload)
         ]
     blocks = payload + [lax.ppermute(payload[0], "ty", table) for table in tables]
     flow = call(

time: 38.6 us -> 36.5 us (0.946)
  waiting for transfers between devices: 8.36 us -> 6.75 us
  local copies, waits for them, and re-layouts: 0.77 us -> 0.1 us
    ppermute x1, waiting for transfers between devices: 3.85 us -> 1.53 us  [local(): lax.ppermute(send_first, ('gz', 'ty'), halo_pairs(n_gz, n_ty, False))]
    ppermute x2, waiting for transfers between devices: 0.01 us -> 0.71 us  [local(): old_edges.append(lax.ppermute(edges[h], 'gz', to_next))]
    reshape x1, local copies, waits for them, and re-layouts: 0.76 us -> 0.08 us  [local(): peaks = peak_shift.reshape(2, n_patches)]
    pallas_call x6 -> x7, Pallas kernels: 14.4 us -> 14.3 us  [the longest x2 4.84 us: local(): call(functools.partial(window_kernel, h, parts), shape((8, LANES), f32),...]
  transfers between devices with their start and end apart: 8 -> 8, of which waited for: 3 -> 5; matrix products, arithmetic and copies ran while one was open for 2% -> 0% of each run, Pallas kernels for 30% -> 33%
where the time goes in v2:
time: 36.5 us; the launch traced here: 36.1 us
  Pallas kernels  17.4 us (48%)
  starting transfers between devices  11.1 us (30%)
  waiting for transfers between devices  6.75 us (18%)
  between operations  0.72 us (2%)
    ppermute x3, starting transfers between devices, local(): lax.ppermute(payload[0], 'ty', table)  5.69 us
    pallas_call x2, Pallas kernels, local(): call(functools.partial(window_kernel, h, parts), shape((8, LANES), f32),...  4.84 us
    ppermute x3, waiting for transfers between devices, local(): lax.ppermute(payload[0], 'ty', table)  4.5 us
    ppermute x1, starting transfers between devices, local(): lax.ppermute(send_first, ('gz', 'ty'), halo_pairs(n_gz, n_ty, False))  3.09 us
    pallas_call x2, Pallas kernels, local(): call(functools.partial(edges_kernel, h, parts), shape((2 * MARGIN, wide),...  3.01 us
    pallas_call x1, Pallas kernels, local(): call(functools.partial(fetch_kernel, all_rows), (shape((n_rows, n_cols),...  2.49 us
    pallas_call x1, Pallas kernels, local(): call(functools.partial(turn_middle_kernel, n_ty, tuple(swaps)), (shape((3...  2.42 us
    pallas_call x1, Pallas kernels, local(): call(turn_edges_kernel, (shape((n_rows, n_cols), bf16), shape((3 * n_patc...  2.1 us
  transfers between devices with their start and end apart: 8, of which 5 were waited for; matrix products, arithmetic and copies ran while one was open for 0% of the time, Pallas kernels for 33%

profile of v2, /device:TPU:0, one launch (start us, length us, event | category | flops | bytes accessed | tf_op | source)
XLA Modules:
  0.0 36.1 jit_solution(8511027560305284713)
XLA Ops:
  0.6 2.5 %shard_map.95 = (bf16[256,2048]{1,0:T(8,128)(2,1)S(1)}, bf16[64,2048]{1,0:T(8,128)(2,1)}, bf16[64,2048]{1,0:T(8,128)(2,1)}, bf16[128,256]{1,0:T(8,128)(2,1)S(1)}...) custom-call(bf16[256,2048]{1,0:T(8,128)(2,1)} %bitcast.2, ...), custom_call_target="tpu_custom_call" | custom-call | tf_op jit(solution)/shard_map/pallas_call | solution.py:411
  3.1 3.1 %collective-permute-start = (bf16[64,2048]{1,0:T(8,128)(2,1)}, bf16[64,2048]{1,0:T(8,128)(2,1)S(1)}, u32[]{:S(2)}, u32[]{:S(2)}) collective-permute-start(bf16[64,2048]{1,0:T(8,128)(2,1)} %get-tuple-element.18), channel_id=1, source_target_pairs={{0,1},{1,0},{2,3},{3,2},{4,5},{5,4},{6,7},{7,6},{8,9},{9,8},{10,11... | collective-permute-start | bytes 786440 | tf_op jit(solution)/shard_map/ppermute | solution.py:432
  6.2 0.0 collective-permute-start.1
  6.2 0.0 copy-start.2
  6.2 2.0 %shard_map.96.mid = bf16[128,2048]{1,0:T(8,128)(2,1)} custom-call(bf16[256,2048]{1,0:T(8,128)(2,1)S(1)} %get-tuple-element.15.held, bf16[128,256]{1,0:T(8,128)(2,1)S(1)} %get-tuple-element.16.mid_table, bf16[8,512,256]{2,1,0:T(8,128)(2,1)S(1)} %get-tuple-element.17.col_table), custom_call_target="tpu_custom_call" | custom-call | tf_op jit(solution)/shard_map/pallas_call | solution.py:445
  8.2 0.5 %collective-permute-start.2 = (bf16[128,2048]{1,0:T(8,128)(2,1)}, bf16[128,2048]{1,0:T(8,128)(2,1)}, u32[]{:S(2)}, u32[]{:S(2)}) collective-permute-start(bf16[128,2048]{1,0:T(8,128)(2,1)} %shard_map.96.mid), channel_id=1, source_target_pairs={{0,4},{4,8},{8,12},{12,0},{1,5},{5,9},{9,13},{13,1},{2,6},{6,10},{... | collective-permute-start | bytes 1572872 | tf_op jit(solution)/shard_map/ppermute | solution.py:453
  8.7 0.0 copy-done.2
  8.7 0.1 reshape.7.peaks
  8.8 2.4 %shard_map.100 = (bf16[96,64,128]{2,1,0:T(8,128)(2,1)S(1)}, f32[32,16,128]{2,1,0:T(8,128)S(1)}, f32[2,32,128]{2,1,0:T(8,128)S(1)}, f32[16,8,128]{2,1,0:T(8,128)S(1)}) custom-call(s32[2,32]{1,0:T(2,128)S(1)} %reshape.7.peaks, bf16[128,2048]{1,0:T(8,128)(2,1)} %shard_map.96.mid), custom_call_target="tpu_custom_call" | custom-call | flops 1000000000 | bytes 3000000 | tf_op jit(solution)/shard_map/pallas_call | solution.py:454
  11.2 1.5 %collective-permute-done.first = bf16[64,2048]{1,0:T(8,128)(2,1)S(1)} collective-permute-done((bf16[64,2048]{1,0:T(8,128)(2,1)}, bf16[64,2048]{1,0:T(8,128)(2,1)S(1)}, u32[]{:S(2)}, u32[]{:S(2)}) %collective-permute-start) | collective-permute-done | bytes 262176 | tf_op jit(solution)/shard_map/ppermute | solution.py:432
  12.7 0.0 collective-permute-done.1.second
  12.7 1.5 %shard_map.97.rest_0_ = bf16[128,1024]{1,0:T(8,128)(2,1)S(1)} custom-call(bf16[64,2048]{1,0:T(8,128)(2,1)S(1)} %collective-permute-done.first, bf16[64,2048]{1,0:T(8,128)(2,1)} %collective-permute-done.1.second, bf16[256,2048]{1,0:T(8,128)(2,1)S(1)} %get-tuple-element.15.held, bf16[64,256]{1,0:T(8,128)(2,1)S(1)} %get-tuple-element.20.top_table, ...), custom_call_target="tpu_custom_call" | custom-call | tf_op jit(solution)/shard_map/pallas_call | solution.py:473
  14.2 0.1 collective-permute-start.4
  14.3 1.5 %shard_map.98.rest_1_ = bf16[128,1024]{1,0:T(8,128)(2,1)S(1)} custom-call(bf16[64,2048]{1,0:T(8,128)(2,1)S(1)} %collective-permute-done.first, bf16[64,2048]{1,0:T(8,128)(2,1)} %collective-permute-done.1.second, bf16[256,2048]{1,0:T(8,128)(2,1)S(1)} %get-tuple-element.15.held, bf16[64,256]{1,0:T(8,128)(2,1)S(1)} %get-tuple-element.20.top_table, ...), custom_call_target="tpu_custom_call" | custom-call | tf_op jit(solution)/shard_map/pallas_call | solution.py:473
  15.8 0.0 copy-start
  15.8 0.0 copy-start.1
  15.8 1.8 %collective-permute-start.3 = (bf16[128,1024]{1,0:T(8,128)(2,1)S(1)}, bf16[128,1024]{1,0:T(8,128)(2,1)S(1)}, u32[]{:S(2)}, u32[]{:S(2)}) collective-permute-start(bf16[128,1024]{1,0:T(8,128)(2,1)S(1)} %shard_map.98.rest_1_), channel_id=1, source_target_pairs={{0,4},{4,8},{8,12},{12,0},{1,5},{5,9},{9,13},{13,1},{2,6},{6,10},{... | collective-permute-start | bytes 786440 | tf_op jit(solution)/shard_map/ppermute | solution.py:481
  17.7 2.1 %shard_map.99 = (bf16[256,2048]{1,0:T(8,128)(2,1)}, bf16[96,64,128]{2,1,0:T(8,128)(2,1)S(1)}) custom-call(s32[2,32]{1,0:T(2,128)S(1)} %reshape.7.peaks, bf16[128,2048]{1,0:T(8,128)(2,1)} %shard_map.96.mid, bf16[128,1024]{1,0:T(8,128)(2,1)S(1)} %shard_map.97.rest_0_, bf16[128,1024]{1,0:T(8,128)(2,1)S(1)} %shard_map.98.rest_1_), custom_call_target="tpu_custom_call" | custom-call | flops 4000000000 | bytes 6000000 | tf_op jit(solution)/shard_map/pallas_call | solution.py:482
  19.8 0.0 collective-permute-done.2.old_mid
  19.8 0.3 collective-permute-done.4.old_edge
  20.1 0.0 copy-done
  20.1 0.0 copy-done.1
  20.1 2.4 %shard_map.101.rest_0_ = f32[8,128]{1,0:T(8,128)S(1)} custom-call(bf16[96,64,128]{2,1,0:T(8,128)(2,1)S(1)} %get-tuple-element.24.turned_mid, bf16[96,64,128]{2,1,0:T(8,128)(2,1)S(1)} %get-tuple-element.25.turned_edge, f32[32,16,128]{2,1,0:T(8,128)S(1)} %get-tuple-element.26.bands, f32[2,32,128]{2,1,0:T(8,128)S(1)} %get-tuple-element.27.peak, ...), custom_call_target="tpu_custom_call" | custom-call | tf_op jit(solution)/shard_map/pallas_call | solution.py:497
  22.5 0.4 %collective-permute-done.3.old_edge = bf16[128,1024]{1,0:T(8,128)(2,1)S(1)} collective-permute-done((bf16[128,1024]{1,0:T(8,128)(2,1)S(1)}, bf16[128,1024]{1,0:T(8,128)(2,1)S(1)}, u32[]{:S(2)}, u32[]{:S(2)}) %collective-permute-start.3) | collective-permute-done | bytes 262176 | tf_op jit(solution)/shard_map/ppermute | solution.py:481
  22.9 2.4 %shard_map.102.refs_0_ = f32[8,128]{1,0:T(8,128)S(1)} custom-call(bf16[96,64,128]{2,1,0:T(8,128)(2,1)S(1)} %get-tuple-element.24.turned_mid, bf16[96,64,128]{2,1,0:T(8,128)(2,1)S(1)} %get-tuple-element.25.turned_edge, f32[32,16,128]{2,1,0:T(8,128)S(1)} %get-tuple-element.26.bands, f32[2,32,128]{2,1,0:T(8,128)S(1)} %get-tuple-element.27.peak, ...), custom_call_target="tpu_custom_call" | custom-call | tf_op jit(solution)/shard_map/pallas_call | solution.py:497
  25.3 3.0 %collective-permute-start.5 = (f32[8,128]{1,0:T(8,128)S(1)}, f32[8,128]{1,0:T(8,128)S(1)}, u32[]{:S(2)}, u32[]{:S(2)}) collective-permute-start(f32[8,128]{1,0:T(8,128)S(1)} %shard_map.102.refs_0_), channel_id=1, source_target_pairs={{0,1},{1,0},{2,3},{3,2},{4,5},{5,4},{6,7},{7,6},{8,9},{9,8},{10,11... | collective-permute-start | bytes 12296 | tf_op jit(solution)/shard_map/ppermute | solution.py:509
  28.4 2.7 %collective-permute-start.6 = (f32[8,128]{1,0:T(8,128)S(1)}, f32[8,128]{1,0:T(8,128)S(1)}, u32[]{:S(2)}, u32[]{:S(2)}) collective-permute-start(f32[8,128]{1,0:T(8,128)S(1)} %shard_map.102.refs_0_), channel_id=1, source_target_pairs={{0,3},{1,2},{2,1},{3,0},{4,7},{5,6},{6,5},{7,4},{8,11},{9,10},{10,... | collective-permute-start | bytes 12296 | tf_op jit(solution)/shard_map/ppermute | solution.py:509
  31.0 0.0 collective-permute-start.7
  31.0 0.0 collective-permute-done.5.refs_1_
  31.0 2.7 %collective-permute-done.6.refs_2_ = f32[8,128]{1,0:T(8,128)S(1)} collective-permute-done((f32[8,128]{1,0:T(8,128)S(1)}, f32[8,128]{1,0:T(8,128)S(1)}, u32[]{:S(2)}, u32[]{:S(2)}) %collective-permute-start.6) | collective-permute-done | bytes 4128 | tf_op jit(solution)/shard_map/ppermute | solution.py:509
  33.8 1.8 %collective-permute-done.7.refs_3_ = f32[8,128]{1,0:T(8,128)S(1)} collective-permute-done((f32[8,128]{1,0:T(8,128)S(1)}, f32[8,128]{1,0:T(8,128)S(1)}, u32[]{:S(2)}, u32[]{:S(2)}) %collective-permute-start.7) | collective-permute-done | bytes 4128 | tf_op jit(solution)/shard_map/ppermute | solution.py:509
  35.5 0.6 %shard_map.103 = f32[2,1,2,16]{3,2,1,0:T(2,128)} custom-call(f32[16,8,128]{2,1,0:T(8,128)S(1)} %get-tuple-element.23.row_weights, f32[8,128]{1,0:T(8,128)S(1)} %shard_map.102.refs_0_, f32[8,128]{1,0:T(8,128)S(1)} %collective-permute-done.5.refs_1_, f32[8,128]{1,0:T(8,128)S(1)} %collective-permute-done.6.refs_2_, f32[8,128]{1,0:T(8,128)S(1)} %collective-permute-done.7.refs_3_), custom_call_target="tpu_custom_call" | custom-call | tf_op jit(solution)/shard_map/pallas_call | solution.py:510
Async XLA Ops:
  3.1 9.6 %collective-permute-start = (bf16[64,2048]{1,0:T(8,128)(2,1)}, bf16[64,2048]{1,0:T(8,128)(2,1)S(1)}, u32[]{:S(2)}, u32[]{:S(2)}) collective-permute-start(bf16[64,2048]{1,0:T(8,128)(2,1)} %get-tuple-element.18), channel_id=1, source_target_pairs={{0,1},{1,0},{2,3},{3,2},{4,5},{5,4},{6,7},{7,6},{8,9},{9,8},{10,11... | collective-permute-start | bytes 786440 | tf_op jit(solution)/shard_map/ppermute | solution.py:432
  6.2 6.5 %collective-permute-start.1 = (bf16[64,2048]{1,0:T(8,128)(2,1)}, bf16[64,2048]{1,0:T(8,128)(2,1)}, u32[]{:S(2)}, u32[]{:S(2)}) collective-permute-start(bf16[64,2048]{1,0:T(8,128)(2,1)} %get-tuple-element.19), channel_id=1, source_target_pairs={{0,4},{1,2},{2,1},{3,7},{4,0},{5,6},{6,5},{7,3},{8,12},{9,10},{10,... | collective-permute-start | bytes 786440 | tf_op jit(solution)/shard_map/ppermute | solution.py:433
  6.2 2.5 %copy-start.2 = (s32[2,1,2,16]{3,2,1,0:T(2,128)S(1)}, s32[2,1,2,16]{3,2,1,0:T(2,128)}, u32[]{:S(2)}) copy-start(s32[2,1,2,16]{3,2,1,0:T(2,128)} %param.14) | copy-start | bytes 772
  8.2 11.6 %collective-permute-start.2 = (bf16[128,2048]{1,0:T(8,128)(2,1)}, bf16[128,2048]{1,0:T(8,128)(2,1)}, u32[]{:S(2)}, u32[]{:S(2)}) collective-permute-start(bf16[128,2048]{1,0:T(8,128)(2,1)} %shard_map.96.mid), channel_id=1, source_target_pairs={{0,4},{4,8},{8,12},{12,0},{1,5},{5,9},{9,13},{13,1},{2,6},{6,10},{... | collective-permute-start | bytes 1572872 | tf_op jit(solution)/shard_map/ppermute | solution.py:453
  14.2 5.8 %collective-permute-start.4 = (bf16[128,1024]{1,0:T(8,128)(2,1)S(1)}, bf16[128,1024]{1,0:T(8,128)(2,1)S(1)}, u32[]{:S(2)}, u32[]{:S(2)}) collective-permute-start(bf16[128,1024]{1,0:T(8,128)(2,1)S(1)} %shard_map.97.rest_0_), channel_id=1, source_target_pairs={{0,4},{4,8},{8,12},{12,0},{1,5},{5,9},{9,13},{13,1},{2,6},{6,10},{... | collective-permute-start | bytes 786440 | tf_op jit(solution)/shard_map/ppermute | solution.py:481
  15.8 4.3 %copy-start = (bf16[256,2048]{1,0:T(8,128)(2,1)S(1)}, bf16[256,2048]{1,0:T(8,128)(2,1)}, u32[]{:S(2)}) copy-start(bf16[256,2048]{1,0:T(8,128)(2,1)} %boundary.3) | copy-start | bytes 3145732
  15.8 4.3 %copy-start.1 = (f32[16,128]{1,0:T(8,128)S(1)}, f32[16,128]{1,0:T(8,128)}, u32[]{:S(2)}) copy-start(f32[16,128]{1,0:T(8,128)} %constant.2.clone.smooth) | copy-start | bytes 24580
  15.8 7.1 %collective-permute-start.3 = (bf16[128,1024]{1,0:T(8,128)(2,1)S(1)}, bf16[128,1024]{1,0:T(8,128)(2,1)S(1)}, u32[]{:S(2)}, u32[]{:S(2)}) collective-permute-start(bf16[128,1024]{1,0:T(8,128)(2,1)S(1)} %shard_map.98.rest_1_), channel_id=1, source_target_pairs={{0,4},{4,8},{8,12},{12,0},{1,5},{5,9},{9,13},{13,1},{2,6},{6,10},{... | collective-permute-start | bytes 786440 | tf_op jit(solution)/shard_map/ppermute | solution.py:481
  25.3 5.7 %collective-permute-start.5 = (f32[8,128]{1,0:T(8,128)S(1)}, f32[8,128]{1,0:T(8,128)S(1)}, u32[]{:S(2)}, u32[]{:S(2)}) collective-permute-start(f32[8,128]{1,0:T(8,128)S(1)} %shard_map.102.refs_0_), channel_id=1, source_target_pairs={{0,1},{1,0},{2,3},{3,2},{4,5},{5,4},{6,7},{7,6},{8,9},{9,8},{10,11... | collective-permute-start | bytes 12296 | tf_op jit(solution)/shard_map/ppermute | solution.py:509
  28.4 5.4 %collective-permute-start.6 = (f32[8,128]{1,0:T(8,128)S(1)}, f32[8,128]{1,0:T(8,128)S(1)}, u32[]{:S(2)}, u32[]{:S(2)}) collective-permute-start(f32[8,128]{1,0:T(8,128)S(1)} %shard_map.102.refs_0_), channel_id=1, source_target_pairs={{0,3},{1,2},{2,1},{3,0},{4,7},{5,6},{6,5},{7,4},{8,11},{9,10},{10,... | collective-permute-start | bytes 12296 | tf_op jit(solution)/shard_map/ppermute | solution.py:509
  31.0 4.5 %collective-permute-start.7 = (f32[8,128]{1,0:T(8,128)S(1)}, f32[8,128]{1,0:T(8,128)S(1)}, u32[]{:S(2)}, u32[]{:S(2)}) collective-permute-start(f32[8,128]{1,0:T(8,128)S(1)} %shard_map.102.refs_0_), channel_id=1, source_target_pairs={{0,2},{1,3},{2,0},{3,1},{4,6},{5,7},{6,4},{7,5},{8,10},{9,11},{10,... | collective-permute-start | bytes 12296 | tf_op jit(solution)/shard_map/ppermute | solution.py:509

commit v3 on v2

--- a/solution.py
+++ b/solution.py
@@ -15,10 +15,9 @@
 LANES = 128
 TAPS = (0.0625, 0.25, 0.375, 0.25, 0.0625)
 FAR = 1 << 20
-VMEM_LIMIT = 40 * 1024 * 1024
-UNROLL = 4
+VMEM_LIMIT = 8 * 1024 * 1024
 TURN_UNROLL = 4
-WINDOW_UNROLL = 4
+WINDOW_UNROLL = 16
 EDGE_FIRST = {2: ((0, MARGIN), (3 * MARGIN, 2 * MARGIN))}
 
 f32 = jnp.float32
@@ -140,46 +139,42 @@
     mix[:, 0:LANES] = edge
     mix[:, LANES + held.shape[1] :] = edge
 
-    @pl.loop(0, n_blocks, unroll=UNROLL)
-    def _(j):
-        at = pl.multiple_of(j * BLOCK, BLOCK)
-        mix[:, pl.ds(LANES + at, BLOCK)] = times(mid_table[...], held[:, pl.ds(at, BLOCK)])
-
-    @pl.loop(0, n_blocks, unroll=UNROLL)
-    def _(j):
-        at = pl.multiple_of(j * BLOCK, BLOCK)
-        mid_ref[:, pl.ds(at, BLOCK)] = times(mix[:, pl.ds(at, BLOCK + 2 * LANES)], col_table[j])
-
-
-def edges_kernel(h, n_parts, first, second, held, top_table, bottom_table, col_table, *rest):
-    edge_ref, mix = rest[-2:]
+    for j in range(n_blocks):
+        here = slice(j * BLOCK, (j + 1) * BLOCK)
+        mix[:, LANES + j * BLOCK : LANES + (j + 1) * BLOCK] = times(mid_table[...], held[:, here])
+    columns_of(mix, col_table, range(n_blocks), mid_ref)
+
+
+def columns_of(mix, col_table, blocks, out_ref):
+    for at, j in enumerate(blocks):
+        out_ref[:, at * BLOCK : (at + 1) * BLOCK] = times(
+            mix[:, j * BLOCK : (j + 1) * BLOCK + 2 * LANES], col_table[j]
+        )
+
+
+def first_edges_kernel(first, second, held, top_table, bottom_table, col_table, edge_ref, mix):
     n_rows, n_cols = held.shape
     half = n_rows // 2
-    n_blocks = n_cols // BLOCK // n_parts
-    low = max(h * n_blocks * BLOCK - LANES, 0) // BLOCK * BLOCK
-    high = min(-(-((h + 1) * n_blocks * BLOCK + LANES) // BLOCK) * BLOCK, n_cols)
+    n_blocks = n_cols // BLOCK
     edge = jnp.zeros((2 * MARGIN, LANES), bf16)
     mix[:, 0:LANES] = edge
-    mix[:, LANES + high - low : 2 * LANES + high - low] = edge
-
-    @pl.loop(0, (high - low) // BLOCK, unroll=UNROLL)
-    def _(j):
-        at = pl.multiple_of(j * BLOCK, BLOCK)
-        here = pl.ds(low + at, BLOCK)
+    mix[:, LANES + n_cols :] = edge
+
+    for j in range(n_blocks):
+        here = slice(j * BLOCK, (j + 1) * BLOCK)
         for rows, table, own in (
             (slice(0, MARGIN), top_table, slice(0, half)),
             (slice(MARGIN, 2 * MARGIN), bottom_table, slice(half, n_rows)),
         ):
             stack = jnp.concatenate([first[:, here], second[:, here], held[own, here]], axis=0)
-            mix[rows, pl.ds(LANES + at, BLOCK)] = times(table[...], stack)
-
-    @pl.loop(0, n_blocks, unroll=UNROLL)
-    def _(j):
-        at = pl.multiple_of(j * BLOCK, BLOCK)
-        start = h * n_blocks * BLOCK - low
-        edge_ref[:, pl.ds(at, BLOCK)] = times(
-            mix[:, pl.ds(start + at, BLOCK + 2 * LANES)], col_table[h * n_blocks + j]
-        )
+            mix[rows, LANES + j * BLOCK : LANES + (j + 1) * BLOCK] = times(table[...], stack)
+    columns_of(mix, col_table, range(edge_ref.shape[1] // BLOCK), edge_ref)
+
+
+def more_edges_kernel(mix, col_table, *rest):
+    edge_ref = rest[-1]
+    n_blocks, wide = col_table.shape[0], edge_ref.shape[1] // BLOCK
+    columns_of(mix, col_table, range(n_blocks - wide, n_blocks), edge_ref)
 
 
 def turn_patches(peaks, cols_of, source, turned):
@@ -194,7 +189,7 @@
             p = i * patch_cols + cols_of + j
             block = source[i * MARGIN : (i + 1) * MARGIN, pl.ds(pl.multiple_of(j * PATCH, PATCH), PATCH)]
             for dx in range(3):
-                turned[dx * n_patches + p] = pltpu.roll(block, (peaks[1, p] + (dx - 1)) % PATCH, 1)
+                turned[dx * n_patches + p] = pltpu.roll(block, (peaks[1, 0, i, cols_of + j] + (dx - 1)) % PATCH, 1)
 
 
 def turn_middle_kernel(n_ty, swaps, peaks, mid, turned, bands, peak, row_weights):
@@ -203,11 +198,15 @@
     lane = lax.broadcasted_iota(jnp.int32, (PATCH // 8, LANES), 1)
     offset = lane - 8 * lax.broadcasted_iota(jnp.int32, (PATCH // 8, LANES), 0) + 1
 
-    @pl.loop(0, n_patches)
-    def _(p):
-        bands[p] = jnp.where(((offset - peaks[0, p]) & (PATCH - 1)) <= 9, 1.0, 0.0)
-        for c in range(2):
-            peak[c, pl.ds(p, 1), :] = jnp.full((1, LANES), peaks[c, p], jnp.int32).astype(f32)
+    patch_rows, patch_cols = peaks.shape[2:]
+    for i in range(patch_rows):
+
+        @pl.loop(0, patch_cols)
+        def _(j):
+            p = i * patch_cols + j
+            bands[p] = jnp.where(((offset - peaks[0, 0, i, j]) & (PATCH - 1)) <= 9, 1.0, 0.0)
+            for c in range(2):
+                peak[c, pl.ds(p, 1), :] = jnp.full((1, LANES), peaks[c, 0, i, j], jnp.int32).astype(f32)
 
     fill_row_weights(n_ty, swaps, mid.shape[0] // MARGIN, row_weights)
 
@@ -440,7 +439,7 @@
                 seen.add(pairs)
                 swaps.append((d, other))
                 tables.append(both_ways(pairs))
-    peaks = peak_shift.reshape(2, n_patches)
+    peaks = peak_shift
     terms = (len(swaps) + 1) * 2 * patch_rows
     mid = call(
         middle_kernel,
@@ -467,18 +466,18 @@
 
     parts = 2
     wide = n_cols // parts
-    edges, old_edges = [], []
-    for h in range(parts):
-        edges.append(
-            call(
-                functools.partial(edges_kernel, h, parts),
-                shape((2 * MARGIN, wide), bf16),
-                [vmem] * 6 + [pl.BlockSpec(memory_space=pl.ANY)] * h,
-                vmem,
-                [pltpu.VMEM((2 * MARGIN, n_cols + 2 * LANES), bf16)],
-            )(first, second, held, top_table, bottom_table, col_table, *edges[-1:])
-        )
-        old_edges.append(lax.ppermute(edges[h], "gz", to_next))
+    first_edge, mix = call(
+        first_edges_kernel,
+        (shape((2 * MARGIN, wide), bf16), shape((2 * MARGIN, n_cols + 2 * LANES), bf16)),
+        [vmem] * 6,
+        [vmem] * 2,
+    )(first, second, held, top_table, bottom_table, col_table)
+    first_old = lax.ppermute(first_edge, "gz", to_next)
+    second_edge = call(more_edges_kernel, shape((2 * MARGIN, n_cols - wide), bf16), [vmem] * 2 + [pl.BlockSpec(memory_space=pl.ANY)], vmem)(
+        mix, col_table, first_edge
+    )
+    second_old = lax.ppermute(second_edge, "gz", to_next)
+    edges, old_edges = (first_edge, second_edge), (first_old, second_old)
     rendered, turned_edge = call(
         turn_edges_kernel,
         (shape((n_rows, n_cols), bf16), shape((3 * n_patches, MARGIN, LANES), bf16)),

time: 36.5 us -> 32.8 us (0.90)
  Pallas kernels: 17.4 us -> 9.08 us
  waiting for transfers between devices: 6.75 us -> 11.7 us
    ppermute x2, waiting for transfers between devices: 0.71 us -> 3.97 us  [the longest x1 2.01 us: local(): first_old = lax.ppermute(first_edge, 'gz', to_next)]
    pallas_call x2, Pallas kernels: 4.84 us -> 1.64 us  [local(): call(functools.partial(window_kernel, h, parts), shape((8, LANES), f32),...]
    pallas_call x2, Pallas kernels: 3.01 us -> 0.99 us  [the longest x1 0.68 us: local(): call(first_edges_kernel, (shape((2 * MARGIN, wide), bf16), shape((2 * MAR...]
    ppermute x1, waiting for transfers between devices: 1.53 us -> 3.17 us  [local(): lax.ppermute(send_first, ('gz', 'ty'), halo_pairs(n_gz, n_ty, False))]
    pallas_call x1, Pallas kernels: 1.96 us -> 0.59 us  [local(): call(middle_kernel, shape((n_mid, n_cols), bf16), [vmem] * 3, vmem, [pltp...]
    pallas_call x1, Pallas kernels: 2.49 us -> 1.69 us  [local(): call(functools.partial(fetch_kernel, all_rows), (shape((n_rows, n_cols),...]
    pallas_call x1, Pallas kernels: 2.1 us -> 1.61 us  [local(): call(turn_edges_kernel, (shape((n_rows, n_cols), bf16), shape((3 * n_patc...]
    pallas_call x1, Pallas kernels: 2.42 us -> 1.96 us  [local(): call(functools.partial(turn_middle_kernel, n_ty, tuple(swaps)), (shape((3...]
  transfers between devices with their start and end apart: 8 -> 8, of which waited for: 5 -> 5; matrix products, arithmetic and copies ran while one was open for 0% -> 0% of each run, Pallas kernels for 33% -> 18%
where the time goes in v3:
time: 32.8 us; the launch traced here: 32.6 us
  waiting for transfers between devices  11.7 us (36%)
  starting transfers between devices  11.1 us (34%)
  Pallas kernels  9.08 us (28%)
  between operations  0.73 us (2%)
    ppermute x3, starting transfers between devices, local(): lax.ppermute(payload[0], 'ty', table)  5.58 us
    ppermute x3, waiting for transfers between devices, local(): lax.ppermute(payload[0], 'ty', table)  4.5 us
    ppermute x1, waiting for transfers between devices, local(): lax.ppermute(send_first, ('gz', 'ty'), halo_pairs(n_gz, n_ty, False))  3.17 us
    ppermute x1, starting transfers between devices, local(): lax.ppermute(send_first, ('gz', 'ty'), halo_pairs(n_gz, n_ty, False))  3.09 us
    ppermute x1, waiting for transfers between devices, local(): first_old = lax.ppermute(first_edge, 'gz', to_next)  2.01 us
    ppermute x1, waiting for transfers between devices, local(): second_old = lax.ppermute(second_edge, 'gz', to_next)  1.97 us
    pallas_call x1, Pallas kernels, local(): call(functools.partial(turn_middle_kernel, n_ty, tuple(swaps)), (shape((3...  1.96 us
    ppermute x1, starting transfers between devices, local(): second_old = lax.ppermute(second_edge, 'gz', to_next)  1.81 us
  transfers between devices with their start and end apart: 8, of which 5 were waited for; matrix products, arithmetic and copies ran while one was open for 0% of the time, Pallas kernels for 18%

profile of v3, /device:TPU:0, one launch (start us, length us, event | category | flops | bytes accessed | tf_op | source)
XLA Modules:
  0.0 32.6 jit_solution(17884194483641511394)
XLA Ops:
  0.6 1.7 %shard_map.95 = (bf16[256,2048]{1,0:T(8,128)(2,1)S(1)}, bf16[64,2048]{1,0:T(8,128)(2,1)S(1)}, bf16[64,2048]{1,0:T(8,128)(2,1)S(1)}, bf16[128,256]{1,0:T(8,128)(2...) custom-call(bf16[256,2048]{1,0:T(8,128)(2,1)} %bitcast.2, ...), custom_call_target="tpu_custom_call" | custom-call | tf_op jit(solution)/shard_map/pallas_call | solution.py:410
  2.3 3.1 %collective-permute-start = (bf16[64,2048]{1,0:T(8,128)(2,1)S(1)}, bf16[64,2048]{1,0:T(8,128)(2,1)S(1)}, u32[]{:S(2)}, u32[]{:S(2)}) collective-permute-start(bf16[64,2048]{1,0:T(8,128)(2,1)S(1)} %get-tuple-element.20), channel_id=1, source_target_pairs={{0,1},{1,0},{2,3},{3,2},{4,5},{5,4},{6,7},{7,6},{8,9},{9,8},{10,11... | collective-permute-start | bytes 786440 | tf_op jit(solution)/shard_map/ppermute | solution.py:431
  5.4 0.0 collective-permute-start.1
  5.4 0.0 copy-start.2
  5.4 0.6 %shard_map.96.mid = bf16[128,2048]{1,0:T(8,128)(2,1)S(1)} custom-call(bf16[256,2048]{1,0:T(8,128)(2,1)S(1)} %get-tuple-element.17.held, bf16[128,256]{1,0:T(8,128)(2,1)S(1)} %get-tuple-element.18.mid_table, bf16[8,512,256]{2,1,0:T(8,128)(2,1)S(1)} %get-tuple-element.19.col_table), custom_call_target="tpu_custom_call" | custom-call | tf_op jit(solution)/shard_map/pallas_call | solution.py:444
  6.0 0.6 %collective-permute-start.2 = (bf16[128,2048]{1,0:T(8,128)(2,1)S(1)}, bf16[128,2048]{1,0:T(8,128)(2,1)S(1)}, u32[]{:S(2)}, u32[]{:S(2)}) collective-permute-start(bf16[128,2048]{1,0:T(8,128)(2,1)S(1)} %shard_map.96.mid), channel_id=1, source_target_pairs={{0,4},{4,8},{8,12},{12,0},{1,5},{5,9},{9,13},{13,1},{2,6},{6,10},{... | collective-permute-start | bytes 1572872 | tf_op jit(solution)/shard_map/ppermute | solution.py:452
  6.6 0.0 copy-done.2
  6.6 2.0 %shard_map.100 = (bf16[96,64,128]{2,1,0:T(8,128)(2,1)S(1)}, f32[32,16,128]{2,1,0:T(8,128)S(1)}, f32[2,32,128]{2,1,0:T(8,128)S(1)}, f32[16,8,128]{2,1,0:T(8,128)S(1)}) custom-call(s32[2,1,2,16]{3,2,1,0:T(2,128)S(1)} %copy-done.2, bf16[128,2048]{1,0:T(8,128)(2,1)S(1)} %shard_map.96.mid), custom_call_target="tpu_custom_call" | custom-call | flops 1000000000 | bytes 3000000 | tf_op jit(solution)/shard_map/pallas_call | solution.py:453
  8.6 3.2 %collective-permute-done.first = bf16[64,2048]{1,0:T(8,128)(2,1)S(1)} collective-permute-done((bf16[64,2048]{1,0:T(8,128)(2,1)S(1)}, bf16[64,2048]{1,0:T(8,128)(2,1)S(1)}, u32[]{:S(2)}, u32[]{:S(2)}) %collective-permute-start) | collective-permute-done | bytes 262176 | tf_op jit(solution)/shard_map/ppermute | solution.py:431
  11.7 0.0 collective-permute-done.1.second
  11.7 0.7 %shard_map.97 = (bf16[128,1024]{1,0:T(8,128)(2,1)S(1)}, bf16[128,2304]{1,0:T(8,128)(2,1)S(1)}) custom-call(bf16[64,2048]{1,0:T(8,128)(2,1)S(1)} %collective-permute-done.first, bf16[64,2048]{1,0:T(8,128)(2,1)S(1)} %collective-permute-done.1.second, bf16[256,2048]{1,0:T(8,128)(2,1)S(1)} %get-tuple-element.17.held, ...), custom_call_target="tpu_custom_call" | custom-call | tf_op jit(solution)/shard_map/pallas_call | solution.py:469
  12.4 0.1 collective-permute-start.4
  12.5 0.3 shard_map.98.rest_1_
  12.8 0.0 copy-start
  12.8 0.0 copy-start.1
  12.8 1.8 %collective-permute-start.3 = (bf16[128,1024]{1,0:T(8,128)(2,1)S(1)}, bf16[128,1024]{1,0:T(8,128)(2,1)S(1)}, u32[]{:S(2)}, u32[]{:S(2)}) collective-permute-start(bf16[128,1024]{1,0:T(8,128)(2,1)S(1)} %shard_map.98.rest_1_), channel_id=1, source_target_pairs={{0,4},{4,8},{8,12},{12,0},{1,5},{5,9},{9,13},{13,1},{2,6},{6,10},{... | collective-permute-start | bytes 786440 | tf_op jit(solution)/shard_map/ppermute | solution.py:479
  14.6 1.6 %shard_map.99 = (bf16[256,2048]{1,0:T(8,128)(2,1)}, bf16[96,64,128]{2,1,0:T(8,128)(2,1)S(1)}) custom-call(s32[2,1,2,16]{3,2,1,0:T(2,128)S(1)} %copy-done.2, bf16[128,2048]{1,0:T(8,128)(2,1)S(1)} %shard_map.96.mid, bf16[128,1024]{1,0:T(8,128)(2,1)S(1)} %get-tuple-element.24.rest_0_, bf16[128,1024]{1,0:T(8,128)(2,1)S(1)} %shard_map.98.rest_1_), custom_call_target="tpu_custom_call" | custom-call | flops 4000000000 | bytes 6000000 | tf_op jit(solution)/shard_map/pallas_call | solution.py:481
  16.2 0.0 collective-permute-done.2.old_mid
  16.3 2.0 %collective-permute-done.4.old_edge = bf16[128,1024]{1,0:T(8,128)(2,1)S(1)} collective-permute-done((bf16[128,1024]{1,0:T(8,128)(2,1)S(1)}, bf16[128,1024]{1,0:T(8,128)(2,1)S(1)}, u32[]{:S(2)}, u32[]{:S(2)}) %collective-permute-start.4) | collective-permute-done | bytes 262176 | tf_op jit(solution)/shard_map/ppermute | solution.py:475
  18.3 0.0 copy-done
  18.3 0.0 copy-done.1
  18.3 0.8 %shard_map.101.rest_0_ = f32[8,128]{1,0:T(8,128)S(1)} custom-call(bf16[96,64,128]{2,1,0:T(8,128)(2,1)S(1)} %get-tuple-element.28.turned_mid, bf16[96,64,128]{2,1,0:T(8,128)(2,1)S(1)} %get-tuple-element.29.turned_edge, f32[32,16,128]{2,1,0:T(8,128)S(1)} %get-tuple-element.30.bands, f32[2,32,128]{2,1,0:T(8,128)S(1)} %get-tuple-element.31.peak, ...), custom_call_target="tpu_custom_call" | custom-call | tf_op jit(solution)/shard_map/pallas_call | solution.py:496
  19.1 2.0 %collective-permute-done.3.old_edge = bf16[128,1024]{1,0:T(8,128)(2,1)S(1)} collective-permute-done((bf16[128,1024]{1,0:T(8,128)(2,1)S(1)}, bf16[128,1024]{1,0:T(8,128)(2,1)S(1)}, u32[]{:S(2)}, u32[]{:S(2)}) %collective-permute-start.3) | collective-permute-done | bytes 262176 | tf_op jit(solution)/shard_map/ppermute | solution.py:479
  21.1 0.8 %shard_map.102.refs_0_ = f32[8,128]{1,0:T(8,128)S(1)} custom-call(bf16[96,64,128]{2,1,0:T(8,128)(2,1)S(1)} %get-tuple-element.28.turned_mid, bf16[96,64,128]{2,1,0:T(8,128)(2,1)S(1)} %get-tuple-element.29.turned_edge, f32[32,16,128]{2,1,0:T(8,128)S(1)} %get-tuple-element.30.bands, f32[2,32,128]{2,1,0:T(8,128)S(1)} %get-tuple-element.31.peak, ...), custom_call_target="tpu_custom_call" | custom-call | tf_op jit(solution)/shard_map/pallas_call | solution.py:496
  21.9 2.9 %collective-permute-start.5 = (f32[8,128]{1,0:T(8,128)S(1)}, f32[8,128]{1,0:T(8,128)S(1)}, u32[]{:S(2)}, u32[]{:S(2)}) collective-permute-start(f32[8,128]{1,0:T(8,128)S(1)} %shard_map.102.refs_0_), channel_id=1, source_target_pairs={{0,1},{1,0},{2,3},{3,2},{4,5},{5,4},{6,7},{7,6},{8,9},{9,8},{10,11... | collective-permute-start | bytes 12296 | tf_op jit(solution)/shard_map/ppermute | solution.py:508
  24.8 2.6 %collective-permute-start.6 = (f32[8,128]{1,0:T(8,128)S(1)}, f32[8,128]{1,0:T(8,128)S(1)}, u32[]{:S(2)}, u32[]{:S(2)}) collective-permute-start(f32[8,128]{1,0:T(8,128)S(1)} %shard_map.102.refs_0_), channel_id=1, source_target_pairs={{0,3},{1,2},{2,1},{3,0},{4,7},{5,6},{6,5},{7,4},{8,11},{9,10},{10,... | collective-permute-start | bytes 12296 | tf_op jit(solution)/shard_map/ppermute | solution.py:508
  27.5 0.0 collective-permute-start.7
  27.5 0.0 collective-permute-done.5.refs_1_
  27.5 2.8 %collective-permute-done.6.refs_2_ = f32[8,128]{1,0:T(8,128)S(1)} collective-permute-done((f32[8,128]{1,0:T(8,128)S(1)}, f32[8,128]{1,0:T(8,128)S(1)}, u32[]{:S(2)}, u32[]{:S(2)}) %collective-permute-start.6) | collective-permute-done | bytes 4128 | tf_op jit(solution)/shard_map/ppermute | solution.py:508
  30.2 1.7 %collective-permute-done.7.refs_3_ = f32[8,128]{1,0:T(8,128)S(1)} collective-permute-done((f32[8,128]{1,0:T(8,128)S(1)}, f32[8,128]{1,0:T(8,128)S(1)}, u32[]{:S(2)}, u32[]{:S(2)}) %collective-permute-start.7) | collective-permute-done | bytes 4128 | tf_op jit(solution)/shard_map/ppermute | solution.py:508
  32.0 0.6 %shard_map.103 = f32[2,1,2,16]{3,2,1,0:T(2,128)} custom-call(f32[16,8,128]{2,1,0:T(8,128)S(1)} %get-tuple-element.27.row_weights, f32[8,128]{1,0:T(8,128)S(1)} %shard_map.102.refs_0_, f32[8,128]{1,0:T(8,128)S(1)} %collective-permute-done.5.refs_1_, f32[8,128]{1,0:T(8,128)S(1)} %collective-permute-done.6.refs_2_, f32[8,128]{1,0:T(8,128)S(1)} %collective-permute-done.7.refs_3_), custom_call_target="tpu_custom_call" | custom-call | tf_op jit(solution)/shard_map/pallas_call | solution.py:509
Async XLA Ops:
  2.3 9.4 %collective-permute-start = (bf16[64,2048]{1,0:T(8,128)(2,1)S(1)}, bf16[64,2048]{1,0:T(8,128)(2,1)S(1)}, u32[]{:S(2)}, u32[]{:S(2)}) collective-permute-start(bf16[64,2048]{1,0:T(8,128)(2,1)S(1)} %get-tuple-element.20), channel_id=1, source_target_pairs={{0,1},{1,0},{2,3},{3,2},{4,5},{5,4},{6,7},{7,6},{8,9},{9,8},{10,11... | collective-permute-start | bytes 786440 | tf_op jit(solution)/shard_map/ppermute | solution.py:431
  5.4 6.3 %collective-permute-start.1 = (bf16[64,2048]{1,0:T(8,128)(2,1)S(1)}, bf16[64,2048]{1,0:T(8,128)(2,1)S(1)}, u32[]{:S(2)}, u32[]{:S(2)}) collective-permute-start(bf16[64,2048]{1,0:T(8,128)(2,1)S(1)} %get-tuple-element.21), channel_id=1, source_target_pairs={{0,4},{1,2},{2,1},{3,7},{4,0},{5,6},{6,5},{7,3},{8,12},{9,10},{10,... | collective-permute-start | bytes 786440 | tf_op jit(solution)/shard_map/ppermute | solution.py:432
  5.4 1.2 %copy-start.2 = (s32[2,1,2,16]{3,2,1,0:T(2,128)S(1)}, s32[2,1,2,16]{3,2,1,0:T(2,128)}, u32[]{:S(2)}) copy-start(s32[2,1,2,16]{3,2,1,0:T(2,128)} %peaks.3) | copy-start | bytes 772
  6.0 10.2 %collective-permute-start.2 = (bf16[128,2048]{1,0:T(8,128)(2,1)S(1)}, bf16[128,2048]{1,0:T(8,128)(2,1)S(1)}, u32[]{:S(2)}, u32[]{:S(2)}) collective-permute-start(bf16[128,2048]{1,0:T(8,128)(2,1)S(1)} %shard_map.96.mid), channel_id=1, source_target_pairs={{0,4},{4,8},{8,12},{12,0},{1,5},{5,9},{9,13},{13,1},{2,6},{6,10},{... | collective-permute-start | bytes 1572872 | tf_op jit(solution)/shard_map/ppermute | solution.py:452
  12.4 5.8 %collective-permute-start.4 = (bf16[128,1024]{1,0:T(8,128)(2,1)S(1)}, bf16[128,1024]{1,0:T(8,128)(2,1)S(1)}, u32[]{:S(2)}, u32[]{:S(2)}) collective-permute-start(bf16[128,1024]{1,0:T(8,128)(2,1)S(1)} %get-tuple-element.24.rest_0_), channel_id=1, source_target_pairs={{0,4},{4,8},{8,12},{12,0},{1,5},{5,9},{9,13},{13,1},{2,6},{6,10},{... | collective-permute-start | bytes 786440 | tf_op jit(solution)/shard_map/ppermute | solution.py:475
  12.8 5.5 %copy-start = (bf16[256,2048]{1,0:T(8,128)(2,1)S(1)}, bf16[256,2048]{1,0:T(8,128)(2,1)}, u32[]{:S(2)}) copy-start(bf16[256,2048]{1,0:T(8,128)(2,1)} %boundary.3) | copy-start | bytes 3145732
  12.8 5.5 %copy-start.1 = (f32[16,128]{1,0:T(8,128)S(1)}, f32[16,128]{1,0:T(8,128)}, u32[]{:S(2)}) copy-start(f32[16,128]{1,0:T(8,128)} %constant.2.clone.smooth) | copy-start | bytes 24580
  12.8 8.3 %collective-permute-start.3 = (bf16[128,1024]{1,0:T(8,128)(2,1)S(1)}, bf16[128,1024]{1,0:T(8,128)(2,1)S(1)}, u32[]{:S(2)}, u32[]{:S(2)}) collective-permute-start(bf16[128,1024]{1,0:T(8,128)(2,1)S(1)} %shard_map.98.rest_1_), channel_id=1, source_target_pairs={{0,4},{4,8},{8,12},{12,0},{1,5},{5,9},{9,13},{13,1},{2,6},{6,10},{... | collective-permute-start | bytes 786440 | tf_op jit(solution)/shard_map/ppermute | solution.py:479
  21.9 5.6 %collective-permute-start.5 = (f32[8,128]{1,0:T(8,128)S(1)}, f32[8,128]{1,0:T(8,128)S(1)}, u32[]{:S(2)}, u32[]{:S(2)}) collective-permute-start(f32[8,128]{1,0:T(8,128)S(1)} %shard_map.102.refs_0_), channel_id=1, source_target_pairs={{0,1},{1,0},{2,3},{3,2},{4,5},{5,4},{6,7},{7,6},{8,9},{9,8},{10,11... | collective-permute-start | bytes 12296 | tf_op jit(solution)/shard_map/ppermute | solution.py:508
  24.8 5.4 %collective-permute-start.6 = (f32[8,128]{1,0:T(8,128)S(1)}, f32[8,128]{1,0:T(8,128)S(1)}, u32[]{:S(2)}, u32[]{:S(2)}) collective-permute-start(f32[8,128]{1,0:T(8,128)S(1)} %shard_map.102.refs_0_), channel_id=1, source_target_pairs={{0,3},{1,2},{2,1},{3,0},{4,7},{5,6},{6,5},{7,4},{8,11},{9,10},{10,... | collective-permute-start | bytes 12296 | tf_op jit(solution)/shard_map/ppermute | solution.py:508
  27.5 4.5 %collective-permute-start.7 = (f32[8,128]{1,0:T(8,128)S(1)}, f32[8,128]{1,0:T(8,128)S(1)}, u32[]{:S(2)}, u32[]{:S(2)}) collective-permute-start(f32[8,128]{1,0:T(8,128)S(1)} %shard_map.102.refs_0_), channel_id=1, source_target_pairs={{0,2},{1,3},{2,0},{3,1},{4,6},{5,7},{6,4},{7,5},{8,10},{9,11},{10,... | collective-permute-start | bytes 12296 | tf_op jit(solution)/shard_map/ppermute | solution.py:508

commit v4 on v3

v4 whole, which is shorter than its diff:
```python
import functools

import jax
import jax.numpy as jnp
import numpy as np
from jax import lax
from jax.experimental import pallas as pl
from jax.experimental.pallas import tpu as pltpu
from jax.sharding import PartitionSpec as P

PATCH = 128
MARGIN = 64
SMOOTH_PASSES = 2
BLOCK = 256
LANES = 128
TAPS = (0.0625, 0.25, 0.375, 0.25, 0.0625)
FAR = 1 << 20
VMEM_LIMIT = 16 * 1024 * 1024
TURN_UNROLL = 4

f32 = jnp.float32
bf16 = jnp.bfloat16


def swap_table(n_gz, n_ty, d, second):
    table = []
    for z in range(n_gz):
        for t in range(n_ty):
            partner = t + d if ((t // d) % 2 == 0) != second else t - d
            if 0 <= partner < n_ty:
                table.append((z * n_ty + t, z * n_ty + partner))
            elif (z ^ 1) < n_gz:
                table.append((z * n_ty + t, (z ^ 1) * n_ty + t))
    return tuple(table)


def partner_of(tile, d, second):
    up = (tile // d) % 2 == int(second)
    return tile + jnp.where(up, d, -d)


def has_partners(n_ty, d, second):
    return any(((t // d) % 2 == 0) != second and t + d < n_ty for t in range(n_ty))


def takes_bottom(second):
    return (lax.axis_index("ty") % 2 == 0) != second


def hat(coord, position):
    return jnp.maximum(1.0 - jnp.abs(coord - position), 0.0)


def source_positions(ids, shift, frac, limit, base):
    source = jnp.clip(ids + shift, 0, limit) - base
    return source.astype(f32) + frac.astype(f32) * (1.0 / 256.0)


def times(left, right):
    return jnp.dot(left, right, preferred_element_type=f32).astype(bf16)


def fetch_kernel(all_rows, section, row_shift, row_frac, col_shift, col_frac, *rest):
    held, send_first, mid_table, first_table, second_table, col_table = rest[:6]
    row_shift_v, row_frac_v, col_shift_v, col_frac_v, sems = rest[6:]
    n_rows, n_cols = section.shape
    tile = lax.axis_index("ty")
    base = tile * n_rows
    first_at = pl.multiple_of(jnp.where(takes_bottom(False), n_rows - MARGIN, 0), MARGIN)
    copies = [
        pltpu.make_async_copy(source, target, sems.at[k])
        for k, (source, target) in enumerate(
            (
                (col_shift, col_shift_v),
                (col_frac, col_frac_v),
                (row_shift, row_shift_v),
                (row_frac, row_frac_v),
                (section.at[pl.ds(first_at, MARGIN), :], send_first),
                (section, held),
            )
        )
    ]
    for copy in copies:
        copy.start()
    for copy in copies[:4]:
        copy.wait()

    reach = BLOCK + LANES
    coord = lax.broadcasted_iota(jnp.int32, (reach, BLOCK), 0).astype(f32)
    ids = lax.broadcasted_iota(jnp.int32, (1, BLOCK), 1)
    edge = jnp.zeros((LANES // 2, BLOCK), bf16)

    @pl.loop(0, n_cols // BLOCK)
    def _(j):
        cols = pl.ds(pl.multiple_of(j * BLOCK, BLOCK), BLOCK)
        pos = source_positions(
            ids + j * BLOCK, col_shift_v[:, cols], col_frac_v[:, cols], n_cols - 2, j * BLOCK - LANES // 2
        )
        col_table[j, 0 : LANES // 2, :] = edge
        col_table[j, LANES // 2 : LANES // 2 + reach, :] = hat(coord, pos).astype(bf16)
        col_table[j, LANES // 2 + reach :, :] = edge

    ids = lax.broadcasted_iota(jnp.int32, (1, n_rows), 1) + base
    pos = source_positions(ids, row_shift_v[...], row_frac_v[...], all_rows - 2, base)
    coord = lax.broadcasted_iota(jnp.int32, (n_rows, n_rows - 2 * MARGIN), 0).astype(f32)
    mid_table[...] = hat(coord, pos[:, MARGIN : n_rows - MARGIN]).T.astype(bf16)
    half = n_rows // 2
    slot = lax.broadcasted_iota(jnp.int32, (MARGIN + half, MARGIN), 0)
    for second, table in ((False, first_table), (True, second_table)):
        bottom = takes_bottom(second)
        start = jnp.where(
            slot < MARGIN, jnp.where(bottom, n_rows, -MARGIN), jnp.where(bottom, half - MARGIN, -MARGIN)
        )
        here = jnp.where(bottom, pos[:, n_rows - MARGIN :], pos[:, :MARGIN])
        table[...] = hat((slot + start).astype(f32), here).T.astype(bf16)
    for copy in copies[4:]:
        copy.wait()


def columns_of(mix, col_table, out_ref):
    for j in range(col_table.shape[0]):
        out_ref[:, j * BLOCK : (j + 1) * BLOCK] = times(mix[:, j * BLOCK : (j + 1) * BLOCK + 2 * LANES], col_table[j])


def clear_sides(mix):
    edge = jnp.zeros((mix.shape[0], LANES), bf16)
    mix[:, 0:LANES] = edge
    mix[:, mix.shape[1] - LANES :] = edge


def middle_kernel(held, mid_table, col_table, mid_ref, send_second, mix):
    n_rows = held.shape[0]
    clear_sides(mix)
    for j in range(col_table.shape[0]):
        mix[:, LANES + j * BLOCK : LANES + (j + 1) * BLOCK] = times(
            mid_table[...], held[:, j * BLOCK : (j + 1) * BLOCK]
        )
    columns_of(mix, col_table, mid_ref)
    at = pl.multiple_of(jnp.where(takes_bottom(True), n_rows - MARGIN, 0), MARGIN)
    send_second[...] = held[pl.ds(at, MARGIN), :]


def edges_kernel(second, halo, held, table, col_table, *rest):
    edge_ref, mix = rest[-2:]
    half = held.shape[0] // 2
    own = pl.ds(pl.multiple_of(jnp.where(takes_bottom(second), half, 0), half), half)
    clear_sides(mix)
    for j in range(col_table.shape[0]):
        here = slice(j * BLOCK, (j + 1) * BLOCK)
        stack = jnp.concatenate([halo[:, here], held[own, here]], axis=0)
        mix[:, LANES + j * BLOCK : LANES + (j + 1) * BLOCK] = times(table[...], stack)
    columns_of(mix, col_table, edge_ref)


def turn_patches(peaks, i, rows, source, turned, first):
    patch_cols = source.shape[1] // PATCH
    n_turned = turned.shape[0] // 3

    @pl.loop(0, patch_cols, unroll=TURN_UNROLL)
    def _(j):
        block = source[rows, pl.ds(pl.multiple_of(j * PATCH, PATCH), PATCH)]
        for dx in range(3):
            turned[dx * n_turned + first + j] = pltpu.roll(block, (peaks[1, 0, i, j] + (dx - 1)) % PATCH, 1)


def turn_middle_kernel(n_ty, swaps, peaks, mid, turned, bands, peak, row_weights):
    n_patches = bands.shape[0]
    for i in range(mid.shape[0] // MARGIN):
        turn_patches(peaks, i, slice(i * MARGIN, (i + 1) * MARGIN), mid, turned, i * (mid.shape[1] // PATCH))
    lane = lax.broadcasted_iota(jnp.int32, (PATCH // 8, LANES), 1)
    offset = lane - 8 * lax.broadcasted_iota(jnp.int32, (PATCH // 8, LANES), 0) + 1

    patch_rows, patch_cols = peaks.shape[2:]
    for i in range(patch_rows):

        @pl.loop(0, patch_cols)
        def _(j):
            p = i * patch_cols + j
            bands[p] = jnp.where(((offset - peaks[0, 0, i, j]) & (PATCH - 1)) <= 9, 1.0, 0.0)
            for c in range(2):
                peak[c, pl.ds(p, 1), :] = jnp.full((1, LANES), peaks[c, 0, i, j], jnp.int32).astype(f32)

    fill_row_weights(n_ty, swaps, mid.shape[0] // MARGIN, row_weights)


def edge_patch_row(second, patch_rows):
    return jnp.where(takes_bottom(second), patch_rows - 1, 0)


def turn_first_kernel(patch_rows, peaks, edge, turned):
    turn_patches(peaks, edge_patch_row(False, patch_rows), slice(None), edge, turned, 0)


def turn_second_kernel(patch_rows, peaks, mid, first, second, rendered, turned, sems):
    n_mid = mid.shape[0]
    n_rows = n_mid + 2 * MARGIN
    moves = [(mid, pl.ds(MARGIN, n_mid))]
    for edge, which in ((first, False), (second, True)):
        at = pl.multiple_of(jnp.where(takes_bottom(which), n_rows - MARGIN, 0), MARGIN)
        moves.append((edge, pl.ds(at, MARGIN)))
    copies = [pltpu.make_async_copy(a, rendered.at[b, :], sems.at[k]) for k, (a, b) in enumerate(moves)]
    for copy in copies:
        copy.start()
    turn_patches(peaks, edge_patch_row(True, patch_rows), slice(None), second, turned, 0)
    for copy in copies:
        copy.wait()


def patch_row_flow(i, turned_edge, turned_mid, bands, peak, smooth, old_of, acc):
    patch_cols = turned_edge.shape[0] // 3
    n_patches = bands.shape[0]
    lane = lax.broadcasted_iota(jnp.int32, (8, LANES), 1) - lax.broadcasted_iota(jnp.int32, (8, LANES), 0)
    for j in range(patch_cols):
        p = i * patch_cols + j
        left = []
        for dx in range(3):
            left += [turned_edge[dx * patch_cols + j], turned_mid[dx * n_patches + p]]
        products = lax.dot_general(
            jnp.concatenate(left, axis=0), old_of(j), (((1,), (1,)), ((), ())), preferred_element_type=f32
        )
        band = bands[p]
        place = (lane - peak[0, pl.ds(p, 1), :].astype(jnp.int32)) & 15
        for dx in range(3):
            lines = [
                products[dx * PATCH + 8 * r : dx * PATCH + 8 * r + 8, :] * band[r : r + 1, :]
                for r in range(PATCH // 8)
            ]
            even, odd = sum(lines[2::2], lines[0]), sum(lines[3::2], lines[1])
            for dy in range(3):
                at = ((dy * 3 + dx) * patch_cols + j) * 8
                acc[at : at + 8, :] = jnp.where(place == (dy - 1) % 16, even, 0.0) + jnp.where(
                    place == (dy + 7) % 16, odd, 0.0
                )
    total = acc[pl.ds(0, 9 * patch_cols, stride=8), :]
    for s in range(1, 8):
        total = total + acc[pl.ds(s, 9 * patch_cols, stride=8), :]
    weights = jnp.maximum(jnp.sum(total, axis=1, keepdims=True) * (1.0 / PATCH), 0.0)
    w = [weights[k * patch_cols : (k + 1) * patch_cols] for k in range(9)]
    scale = 1.0 / jnp.maximum(sum(w), 1.0)
    moves = (
        (w[6] + w[7] + w[8] - w[0] - w[1] - w[2]) * scale,
        (w[2] + w[5] + w[8] - w[0] - w[3] - w[6]) * scale,
    )
    here = pl.ds(pl.multiple_of(i * patch_cols, patch_cols), patch_cols)
    return [jnp.sum((moves[c] + peak[c, here, :]) * smooth[...], axis=0, keepdims=True) for c in range(2)]


def put_lines(lines, i, patch_rows):
    at = lax.broadcasted_iota(jnp.int32, (8, LANES), 0)
    return sum(jnp.where(at == c * patch_rows + i, line, 0.0) for c, line in enumerate(lines))


def boundary_kernel(turned_mid, turned_first, turned_second, bands, peak, boundary, smooth, out_ref, acc, whole, sem):
    n_rows = boundary.shape[0]
    patch_rows = n_rows // PATCH
    out_ref[...] = jnp.zeros_like(out_ref)

    @pl.when(lax.axis_index("gz") == 0)
    def _():
        copy = pltpu.make_async_copy(boundary, whole, sem)
        copy.start()
        copy.wait()

        @pl.loop(0, patch_rows)
        def _(k):
            i = jnp.where(k == 0, edge_patch_row(False, patch_rows), edge_patch_row(True, patch_rows))
            at_edge = pl.multiple_of(i * (n_rows - MARGIN), MARGIN)
            at_mid = pl.multiple_of(MARGIN + i * MARGIN, MARGIN)

            def old_of(j):
                cols = slice(j * PATCH, (j + 1) * PATCH)
                return jnp.concatenate([whole[pl.ds(at_edge, MARGIN), cols], whole[pl.ds(at_mid, MARGIN), cols]], axis=0)

            def flow_with(turned_edge):
                out_ref[...] += put_lines(
                    patch_row_flow(i, turned_edge, turned_mid, bands, peak, smooth, old_of, acc), i, patch_rows
                )

            @pl.when(k == 0)
            def _():
                flow_with(turned_first)

            @pl.when(k != 0)
            def _():
                flow_with(turned_second)


def window_kernel(second, turned_mid, turned_edge, bands, peak, old_mid, old_edge, smooth, before, out_ref, acc):
    patch_rows = old_mid.shape[0] // MARGIN
    out_ref[...] = before[...]

    @pl.when(lax.axis_index("gz") != 0)
    def _():
        i = edge_patch_row(second, patch_rows)
        at_mid = pl.multiple_of(i * MARGIN, MARGIN)

        def old_of(j):
            cols = slice(j * PATCH, (j + 1) * PATCH)
            return jnp.concatenate([old_edge[:, cols], old_mid[pl.ds(at_mid, MARGIN), cols]], axis=0)

        lines = patch_row_flow(i, turned_edge, turned_mid, bands, peak, smooth, old_of, acc)
        out_ref[...] = before[...] + put_lines(lines, i, patch_rows)


def fill_row_weights(n_ty, swaps, patch_rows, out_ref):
    all_rows = n_ty * patch_rows
    tile = lax.axis_index("ty")
    held = 2 * patch_rows
    depth = LANES
    at = lax.broadcasted_iota(jnp.int32, (8, depth), 0)
    slot = lax.broadcasted_iota(jnp.int32, (8, depth), 1)
    holder = jnp.full((8, depth), tile, jnp.int32)
    for k, (d, second) in enumerate(swaps):
        holder = jnp.where((slot >> 3) == k + 1, partner_of(tile, d, second), holder)
    inner = slot & 7
    c_out = (at >= patch_rows).astype(jnp.int32)
    c_in = (inner >= patch_rows).astype(jnp.int32)
    row = tile * patch_rows + at - c_out * patch_rows
    source = holder * patch_rows + inner - c_in * patch_rows

    def inside(r):
        return (r >= 0) & (r < all_rows)

    def tap(delta):
        size = jnp.abs(delta)
        return jnp.where(
            size == 0, TAPS[2], jnp.where(size == 1, TAPS[1], jnp.where(size == 2, TAPS[0], 0.0))
        )

    def norm(r):
        return sum(jnp.where(inside(r + o), TAPS[o + 2], 0.0) for o in range(-2, 3))

    weight = jnp.zeros((8, depth), f32)
    for o in range(-2, 3):
        weight = weight + jnp.where(inside(row + o), TAPS[o + 2] * tap(source - row - o) / norm(row + o), 0.0)
    used = (inner < held) & (at < held) & (c_in == c_out) & inside(source)
    weight = jnp.where(used, weight / norm(row), 0.0)
    for k in range(len(swaps) + 1):
        for b in range(held):
            out_ref[k * held + b] = jnp.broadcast_to(weight[:, 8 * k + b : 8 * k + b + 1], (8, LANES))


def rows_kernel(row_weights, *refs):
    blocks, out_ref = refs[:-1], refs[-1]
    patch_rows, patch_cols = out_ref.shape[2], out_ref.shape[3]
    held = 2 * patch_rows
    result = None
    for k, block in enumerate(blocks):
        for b in range(held):
            term = row_weights[k * held + b] * block[b : b + 1, :]
            result = term if result is None else result + term
    for c in range(2):
        out_ref[c, 0] = result[c * patch_rows : (c + 1) * patch_rows, :patch_cols]


def column_smoother(n):
    kernel = np.zeros((n, n))
    for i in range(n):
        for o in range(-2, 3):
            if 0 <= i + o < n:
                kernel[i, i + o] = TAPS[o + 2]
    kernel = kernel / kernel.sum(1, keepdims=True)
    table = np.zeros((n, LANES), np.float32)
    table[:, :n] = np.linalg.matrix_power(kernel, SMOOTH_PASSES).T
    return table


def call(body, out_shape, in_specs, out_specs, scratch=(), flops=0, moved=0):
    return pl.pallas_call(
        body,
        out_shape=out_shape,
        in_specs=in_specs,
        out_specs=out_specs,
        scratch_shapes=scratch,
        compiler_params=pltpu.CompilerParams(vmem_limit_bytes=VMEM_LIMIT),
        cost_estimate=pl.CostEstimate(flops=flops, bytes_accessed=moved, transcendentals=0),
    )


def local(sections, boundary, row_shift, row_frac, col_shift, col_frac, peak_shift):
    section = sections[0]
    n_rows, n_cols = section.shape
    n_ty, n_gz = lax.axis_size("ty"), lax.axis_size("gz")
    patch_rows, patch_cols = n_rows // PATCH, n_cols // PATCH
    n_patches = patch_rows * patch_cols
    all_rows = n_rows * n_ty
    n_mid, half = n_rows - 2 * MARGIN, n_rows // 2
    n_blocks = n_cols // BLOCK
    vmem = pl.BlockSpec(memory_space=pltpu.VMEM)
    smem = pl.BlockSpec(memory_space=pltpu.SMEM)
    hbm = pl.BlockSpec(memory_space=pltpu.HBM)
    unread = pl.BlockSpec(memory_space=pl.ANY)
    shape = jax.ShapeDtypeStruct
    to_next = [(i, (i + 1) % n_gz) for i in range(n_gz)]

    swaps, tables = [], []
    for d in range(-(-2 * SMOOTH_PASSES // patch_rows), 0, -1):
        for other in (False, True):
            if has_partners(n_ty, d, other):
                swaps.append((d, other))
                tables.append(swap_table(n_gz, n_ty, d, other))

    held, send_first, mid_table, first_table, second_table, col_table = call(
        functools.partial(fetch_kernel, all_rows),
        (
            shape((n_rows, n_cols), bf16),
            shape((MARGIN, n_cols), bf16),
            shape((n_mid, n_rows), bf16),
            shape((MARGIN, MARGIN + half), bf16),
            shape((MARGIN, MARGIN + half), bf16),
            shape((n_blocks, BLOCK + 2 * LANES, BLOCK), bf16),
        ),
        [hbm] * 5,
        [vmem] * 6,
        [
            pltpu.VMEM((1, n_rows), jnp.int32),
            pltpu.VMEM((1, n_rows), jnp.int32),
            pltpu.VMEM((1, n_cols), jnp.int32),
            pltpu.VMEM((1, n_cols), jnp.int32),
            pltpu.SemaphoreType.DMA((6,)),
        ],
    )(*(pltpu.with_memory_space_constraint(x, pltpu.HBM) for x in (section, row_shift, row_frac, col_shift, col_frac)))
    first = lax.ppermute(send_first, ("gz", "ty"), swap_table(n_gz, n_ty, 1, False))

    mid, send_second = call(
        middle_kernel,
        (shape((n_mid, n_cols), bf16), shape((MARGIN, n_cols), bf16)),
        [vmem] * 3,
        [vmem] * 2,
        [pltpu.VMEM((n_mid, n_cols + 2 * LANES), bf16)],
    )(held, mid_table, col_table)
    old_mid = lax.ppermute(mid, "gz", to_next)
    second = lax.ppermute(send_second, ("gz", "ty"), swap_table(n_gz, n_ty, 1, True))

    terms = (len(swaps) + 1) * 2 * patch_rows
    turned_mid, bands, peak, row_weights = call(
        functools.partial(turn_middle_kernel, n_ty, tuple(swaps)),
        (
            shape((3 * n_patches, MARGIN, LANES), bf16),
            shape((n_patches, PATCH // 8, LANES), f32),
            shape((2, n_patches, LANES), f32),
            shape((terms, 8, LANES), f32),
        ),
        [smem, vmem],
        [vmem] * 4,
        flops=1_000_000_000,
        moved=3_000_000,
    )(peak_shift, mid)

    def render_edges(which, *args):
        return call(
            functools.partial(edges_kernel, which),
            shape((MARGIN, n_cols), bf16),
            [vmem] * 4 + [unread] * (len(args) - 4),
            vmem,
            [pltpu.VMEM((MARGIN, n_cols + 2 * LANES), bf16)],
        )(*args)

    turned_shape = shape((3 * patch_cols, MARGIN, LANES), bf16)
    first_edge = render_edges(False, first, held, first_table, col_table)
    old_first = lax.ppermute(first_edge, "gz", to_next)
    turned_first = call(
        functools.partial(turn_first_kernel, patch_rows),
        turned_shape,
        [smem, vmem],
        vmem,
        flops=500_000_000,
        moved=1_000_000,
    )(peak_shift, first_edge)
    second_edge = render_edges(True, second, held, second_table, col_table, first_edge)
    old_second = lax.ppermute(second_edge, "gz", to_next)
    rendered, turned_second = call(
        functools.partial(turn_second_kernel, patch_rows),
        (shape((n_rows, n_cols), bf16), turned_shape),
        [smem] + [vmem] * 3,
        [hbm, vmem],
        [pltpu.SemaphoreType.DMA((3,))],
        flops=1_000_000_000,
        moved=3_000_000,
    )(peak_shift, mid, first_edge, second_edge)

    smooth = jnp.asarray(column_smoother(patch_cols))
    acc = pltpu.VMEM((9 * patch_cols * 8, LANES), f32)
    payload = call(
        boundary_kernel,
        shape((8, LANES), f32),
        [vmem] * 5 + [hbm, vmem],
        vmem,
        [acc, pltpu.VMEM((n_rows, n_cols), bf16), pltpu.SemaphoreType.DMA],
        flops=1_000_000_000,
        moved=3_000_000,
    )(turned_mid, turned_first, turned_second, bands, peak, boundary, smooth)
    for which, turned, old in ((False, turned_first, old_first), (True, turned_second, old_second)):
        payload = call(
            functools.partial(window_kernel, which), shape((8, LANES), f32), [vmem] * 8, vmem, [acc]
        )(turned_mid, turned, bands, peak, old_mid, old, smooth, payload)
    blocks = [payload] + [lax.ppermute(payload, ("gz", "ty"), table) for table in tables]
    flow = call(
        rows_kernel, shape((2, 1, patch_rows, patch_cols), f32), [vmem] * (1 + len(blocks)), vmem
    )(row_weights, *blocks)
    return rendered[None], flow


def solution(mesh):
    in_specs = (
        P(("parts", "gz"), "ty", None),
        P(("parts", "ty"), None),
        P(("parts", "gz"), "ty"),
        P(("parts", "gz"), "ty"),
        P(("parts", "gz"), None),
        P(("parts", "gz"), None),
        P(None, ("parts", "gz"), "ty", None),
    )
    out_specs = (P(("parts", "gz"), "ty", None), P(None, ("parts", "gz"), "ty", None))
    return jax.shard_map(local, mesh=mesh, in_specs=in_specs, out_specs=out_specs, check_vma=False)
```

time: 32.8 us -> 28.3 us (0.86)
  waiting for transfers between devices: 11.7 us -> 7.17 us
  starting transfers between devices: 11.1 us -> 9.75 us
  Pallas kernels: 9.08 us -> 10.3 us
    ppermute x7, waiting for transfers between devices: 11.6 us -> 7.17 us  [the longest x1 5.13 us: local(): lax.ppermute(send_first, ('gz', 'ty'), swap_table(n_gz, n_ty, 1, False))]
    pallas_call x6 -> x8, Pallas kernels: 4.83 us -> 6.13 us  [the longest x1 1.57 us: local(): call(boundary_kernel, shape((8, LANES), f32), [vmem] * 5 + [hbm, vmem], v...]
    ppermute x7, starting transfers between devices: 10.5 us -> 9.25 us  [the longest x3 4.24 us: local(): lax.ppermute(payload, ('gz', 'ty'), table)]
  transfers between devices with their start and end apart: 8 -> 8, of which waited for: 5 -> 3; matrix products, arithmetic and copies ran while one was open for 0% -> 0% of each run, Pallas kernels for 18% -> 29%
where the time goes in v4:
time: 28.3 us; the launch traced here: 28.1 us
  Pallas kernels  10.3 us (36%)
  starting transfers between devices  9.75 us (34%)
  waiting for transfers between devices  7.17 us (25%)
  between operations  0.8 us (3%)
    ppermute x1, waiting for transfers between devices, local(): lax.ppermute(send_first, ('gz', 'ty'), swap_table(n_gz, n_ty, 1, False))  5.13 us
    ppermute x3, starting transfers between devices, local(): lax.ppermute(payload, ('gz', 'ty'), table)  4.24 us
    ppermute x1, starting transfers between devices, local(): lax.ppermute(send_first, ('gz', 'ty'), swap_table(n_gz, n_ty, 1, False))  3.09 us
    ppermute x3, waiting for transfers between devices, local(): lax.ppermute(payload, ('gz', 'ty'), table)  2.03 us
    pallas_call x1, Pallas kernels, local(): call(functools.partial(turn_middle_kernel, n_ty, tuple(swaps)), (shape((3...  1.96 us
    ppermute x1, starting transfers between devices, local(): old_second = lax.ppermute(second_edge, 'gz', to_next)  1.8 us
    pallas_call x1, Pallas kernels, local(): call(functools.partial(fetch_kernel, all_rows), (shape((n_rows, n_cols),...  1.66 us
    pallas_call x1, Pallas kernels, local(): call(boundary_kernel, shape((8, LANES), f32), [vmem] * 5 + [hbm, vmem], v...  1.57 us
  transfers between devices with their start and end apart: 8, of which 3 were waited for; matrix products, arithmetic and copies ran while one was open for 0% of the time, Pallas kernels for 29%

profile of v4, /device:TPU:0, one launch (start us, length us, event | category | flops | bytes accessed | tf_op | source)
XLA Modules:
  0.0 28.1 jit_solution(13763477529118765470)
XLA Ops:
  0.6 1.7 %shard_map.95 = (bf16[256,2048]{1,0:T(8,128)(2,1)S(1)}, bf16[64,2048]{1,0:T(8,128)(2,1)S(1)}, bf16[128,256]{1,0:T(8,128)(2,1)S(1)}, bf16[64,192]{1,0:T(8,128)(2,...) custom-call(bf16[256,2048]{1,0:T(8,128)(2,1)} %bitcast.2, s32[1,256]{1,0:T(1,128)} %row_shift.1, ...), custom_call_target="tpu_custom_call" | custom-call | tf_op jit(solution)/shard_map/pallas_call | solution.py:403
  2.3 3.1 %collective-permute-start = (bf16[64,2048]{1,0:T(8,128)(2,1)S(1)}, bf16[64,2048]{1,0:T(8,128)(2,1)S(1)}, u32[]{:S(2)}, u32[]{:S(2)}) collective-permute-start(bf16[64,2048]{1,0:T(8,128)(2,1)S(1)} %get-tuple-element.20), channel_id=1, source_target_pairs={{0,1},{1,0},{2,3},{3,2},{4,5},{5,4},{6,7},{7,6},{8,9},{9,8},{10,11... | collective-permute-start | bytes 786440 | tf_op jit(solution)/shard_map/ppermute | solution.py:423
  5.4 0.6 %shard_map.96 = (bf16[128,2048]{1,0:T(8,128)(2,1)S(1)}, bf16[64,2048]{1,0:T(8,128)(2,1)S(1)}) custom-call(bf16[256,2048]{1,0:T(8,128)(2,1)S(1)} %get-tuple-element.16.held, bf16[128,256]{1,0:T(8,128)(2,1)S(1)} %get-tuple-element.17.mid_table, bf16[8,512,256]{2,1,0:T(8,128)(2,1)S(1)} %get-tuple-element.18.col_table), custom_call_target="tpu_custom_call" | custom-call | tf_op jit(solution)/shard_map/pallas_call | solution.py:425
  6.0 0.1 collective-permute-start.1
  6.1 0.5 %collective-permute-start.2 = (bf16[128,2048]{1,0:T(8,128)(2,1)S(1)}, bf16[128,2048]{1,0:T(8,128)(2,1)S(1)}, u32[]{:S(2)}, u32[]{:S(2)}) collective-permute-start(bf16[128,2048]{1,0:T(8,128)(2,1)S(1)} %get-tuple-element.19.mid), channel_id=1, source_target_pairs={{0,4},{4,8},{8,12},{12,0},{1,5},{5,9},{9,13},{13,1},{2,6},{6,10},{... | collective-permute-start | bytes 1572872 | tf_op jit(solution)/shard_map/ppermute | solution.py:432
  6.6 5.1 %collective-permute-done.halo = bf16[64,2048]{1,0:T(8,128)(2,1)S(1)} collective-permute-done((bf16[64,2048]{1,0:T(8,128)(2,1)S(1)}, bf16[64,2048]{1,0:T(8,128)(2,1)S(1)}, u32[]{:S(2)}, u32[]{:S(2)}) %collective-permute-start) | collective-permute-done | bytes 262176 | tf_op jit(solution)/shard_map/ppermute | solution.py:423
  11.7 0.6 %shard_map.97.rest_0_.first.edge = bf16[64,2048]{1,0:T(8,128)(2,1)S(1)} custom-call(bf16[64,2048]{1,0:T(8,128)(2,1)S(1)} %collective-permute-done.halo, bf16[256,2048]{1,0:T(8,128)(2,1)S(1)} %get-tuple-element.16.held, bf16[64,192]{1,0:T(8,128)(2,1)S(1)} %get-tuple-element.21.table, bf16[8,512,256]{2,1,0:T(8,128)(2,1)S(1)} %get-tuple-element.18.col_table), custom_call_target="tpu_custom_call" | custom-call | tf_op jit(solution)/shard_map/pallas_call | solution.py:451
  12.3 0.0 copy-start.2
  12.4 0.1 collective-permute-start.4
  12.4 0.0 collective-permute-done.1.halo
  12.4 0.6 %shard_map.98.second = bf16[64,2048]{1,0:T(8,128)(2,1)S(1)} custom-call(bf16[64,2048]{1,0:T(8,128)(2,1)S(1)} %collective-permute-done.1.halo, bf16[256,2048]{1,0:T(8,128)(2,1)S(1)} %get-tuple-element.16.held, bf16[64,192]{1,0:T(8,128)(2,1)S(1)} %get-tuple-element.23.table, bf16[8,512,256]{2,1,0:T(8,128)(2,1)S(1)} %get-tuple-element.18.col_table, ...), custom_call_target="tpu_custom_call" | custom-call | tf_op jit(solution)/shard_map/pallas_call | solution.py:451
  13.1 1.8 %collective-permute-start.3 = (bf16[64,2048]{1,0:T(8,128)(2,1)S(1)}, bf16[64,2048]{1,0:T(8,128)(2,1)S(1)}, u32[]{:S(2)}, u32[]{:S(2)}) collective-permute-start(bf16[64,2048]{1,0:T(8,128)(2,1)S(1)} %shard_map.98.second), channel_id=1, source_target_pairs={{0,4},{4,8},{8,12},{12,0},{1,5},{5,9},{9,13},{13,1},{2,6},{6,10},{... | collective-permute-start | bytes 786440 | tf_op jit(solution)/shard_map/ppermute | solution.py:471
  14.9 0.0 copy-done.2
  14.9 2.0 %shard_map.100 = (bf16[96,64,128]{2,1,0:T(8,128)(2,1)S(1)}, f32[32,16,128]{2,1,0:T(8,128)S(1)}, f32[2,32,128]{2,1,0:T(8,128)S(1)}, f32[16,8,128]{2,1,0:T(8,128)S(1)}) custom-call(s32[2,1,2,16]{3,2,1,0:T(2,128)S(1)} %copy-done.2, bf16[128,2048]{1,0:T(8,128)(2,1)S(1)} %get-tuple-element.19.mid), custom_call_target="tpu_custom_call" | custom-call | flops 1000000000 | bytes 3000000 | tf_op jit(solution)/shard_map/pallas_call | solution.py:436
  16.9 1.1 %shard_map.101.turned_first.turned_edge = bf16[48,64,128]{2,1,0:T(8,128)(2,1)S(1)} custom-call(s32[2,1,2,16]{3,2,1,0:T(2,128)S(1)} %copy-done.2, bf16[64,2048]{1,0:T(8,128)(2,1)S(1)} %shard_map.97.rest_0_.first.edge), custom_call_target="tpu_custom_call" | custom-call | flops 500000000 | bytes 1000000 | tf_op jit(solution)/shard_map/pallas_call | solution.py:462
  17.9 0.0 copy-start
  18.0 0.0 copy-start.1
  18.0 1.6 %shard_map.99 = (bf16[256,2048]{1,0:T(8,128)(2,1)}, bf16[48,64,128]{2,1,0:T(8,128)(2,1)S(1)}) custom-call(s32[2,1,2,16]{3,2,1,0:T(2,128)S(1)} %copy-done.2, bf16[128,2048]{1,0:T(8,128)(2,1)S(1)} %get-tuple-element.19.mid, bf16[64,2048]{1,0:T(8,128)(2,1)S(1)} %shard_map.97.rest_0_.first.edge, bf16[64,2048]{1,0:T(8,128)(2,1)S(1)} %shard_map.98.second), custom_call_target="tpu_custom_call" | custom-call | flops 1000000000 | bytes 3000000 | tf_op jit(solution)/shard_map/pallas_call | solution.py:472
  19.5 0.0 copy-done
  19.5 0.0 copy-done.1
  19.6 1.6 %shard_map.102.before = f32[8,128]{1,0:T(8,128)S(1)} custom-call(bf16[96,64,128]{2,1,0:T(8,128)(2,1)S(1)} %get-tuple-element.26.turned_mid, bf16[48,64,128]{2,1,0:T(8,128)(2,1)S(1)} %shard_map.101.turned_first.turned_edge, bf16[48,64,128]{2,1,0:T(8,128)(2,1)S(1)} %get-tuple-element.27.turned_second.turned_edge, f32[32,16,128]{2,1,0:T(8,128)S(1)} %get-tuple-element.28.bands, ...), custom_call_target="tpu_custom_call" | custom-call | flops 1000000000 | bytes 3000000 | tf_op jit(solution)/shard_map/pallas_call | solution.py:484
  21.1 0.0 collective-permute-done.2.old_mid
  21.1 0.0 collective-permute-done.4.old_edge
  21.2 0.0 collective-permute-done.3.old_edge
  21.2 2.7 %collective-permute-start.5 = (f32[8,128]{1,0:T(8,128)S(1)}, f32[8,128]{1,0:T(8,128)S(1)}, u32[]{:S(2)}, u32[]{:S(2)}) collective-permute-start(f32[8,128]{1,0:T(8,128)S(1)} %shard_map.104.refs_0_), channel_id=1, source_target_pairs={{0,2},{1,3},{2,0},{3,1},{4,6},{5,7},{6,4},{7,5},{8,10},{9,11},{10,... | collective-permute-start | bytes 12296 | tf_op jit(solution)/shard_map/ppermute | solution.py:497
  23.9 1.6 %collective-permute-start.6 = (f32[8,128]{1,0:T(8,128)S(1)}, f32[8,128]{1,0:T(8,128)S(1)}, u32[]{:S(2)}, u32[]{:S(2)}) collective-permute-start(f32[8,128]{1,0:T(8,128)S(1)} %shard_map.104.refs_0_), channel_id=1, source_target_pairs={{0,1},{1,0},{2,3},{3,2},{4,5},{5,4},{6,7},{7,6},{8,9},{9,8},{10,11... | collective-permute-start | bytes 12296 | tf_op jit(solution)/shard_map/ppermute | solution.py:497
  25.5 0.0 collective-permute-start.7
  25.5 0.3 %collective-permute-done.5.refs_1_ = f32[8,128]{1,0:T(8,128)S(1)} collective-permute-done((f32[8,128]{1,0:T(8,128)S(1)}, f32[8,128]{1,0:T(8,128)S(1)}, u32[]{:S(2)}, u32[]{:S(2)}) %collective-permute-start.5) | collective-permute-done | bytes 4128 | tf_op jit(solution)/shard_map/ppermute | solution.py:497
  25.8 1.7 %collective-permute-done.6.refs_2_ = f32[8,128]{1,0:T(8,128)S(1)} collective-permute-done((f32[8,128]{1,0:T(8,128)S(1)}, f32[8,128]{1,0:T(8,128)S(1)}, u32[]{:S(2)}, u32[]{:S(2)}) %collective-permute-start.6) | collective-permute-done | bytes 4128 | tf_op jit(solution)/shard_map/ppermute | solution.py:497
  27.5 0.0 collective-permute-done.7.refs_3_
  27.5 0.6 %shard_map.105 = f32[2,1,2,16]{3,2,1,0:T(2,128)} custom-call(f32[16,8,128]{2,1,0:T(8,128)S(1)} %get-tuple-element.25.row_weights, f32[8,128]{1,0:T(8,128)S(1)} %shard_map.104.refs_0_, f32[8,128]{1,0:T(8,128)S(1)} %collective-permute-done.5.refs_1_, f32[8,128]{1,0:T(8,128)S(1)} %collective-permute-done.6.refs_2_, f32[8,128]{1,0:T(8,128)S(1)} %collective-permute-done.7.refs_3_), custom_call_target="tpu_custom_call" | custom-call | tf_op jit(solution)/shard_map/pallas_call | solution.py:498
  (2 shorter events, 0.0 us)
Async XLA Ops:
  2.3 9.4 %collective-permute-start = (bf16[64,2048]{1,0:T(8,128)(2,1)S(1)}, bf16[64,2048]{1,0:T(8,128)(2,1)S(1)}, u32[]{:S(2)}, u32[]{:S(2)}) collective-permute-start(bf16[64,2048]{1,0:T(8,128)(2,1)S(1)} %get-tuple-element.20), channel_id=1, source_target_pairs={{0,1},{1,0},{2,3},{3,2},{4,5},{5,4},{6,7},{7,6},{8,9},{9,8},{10,11... | collective-permute-start | bytes 786440 | tf_op jit(solution)/shard_map/ppermute | solution.py:423
  6.0 6.4 %collective-permute-start.1 = (bf16[64,2048]{1,0:T(8,128)(2,1)S(1)}, bf16[64,2048]{1,0:T(8,128)(2,1)S(1)}, u32[]{:S(2)}, u32[]{:S(2)}) collective-permute-start(bf16[64,2048]{1,0:T(8,128)(2,1)S(1)} %get-tuple-element.22), channel_id=1, source_target_pairs={{0,4},{1,2},{2,1},{3,7},{4,0},{5,6},{6,5},{7,3},{8,12},{9,10},{10,... | collective-permute-start | bytes 786440 | tf_op jit(solution)/shard_map/ppermute | solution.py:433
  6.1 15.1 %collective-permute-start.2 = (bf16[128,2048]{1,0:T(8,128)(2,1)S(1)}, bf16[128,2048]{1,0:T(8,128)(2,1)S(1)}, u32[]{:S(2)}, u32[]{:S(2)}) collective-permute-start(bf16[128,2048]{1,0:T(8,128)(2,1)S(1)} %get-tuple-element.19.mid), channel_id=1, source_target_pairs={{0,4},{4,8},{8,12},{12,0},{1,5},{5,9},{9,13},{13,1},{2,6},{6,10},{... | collective-permute-start | bytes 1572872 | tf_op jit(solution)/shard_map/ppermute | solution.py:432
  12.3 2.5 %copy-start.2 = (s32[2,1,2,16]{3,2,1,0:T(2,128)S(1)}, s32[2,1,2,16]{3,2,1,0:T(2,128)}, u32[]{:S(2)}) copy-start(s32[2,1,2,16]{3,2,1,0:T(2,128)} %peaks.5) | copy-start | bytes 772
  12.4 8.8 %collective-permute-start.4 = (bf16[64,2048]{1,0:T(8,128)(2,1)S(1)}, bf16[64,2048]{1,0:T(8,128)(2,1)S(1)}, u32[]{:S(2)}, u32[]{:S(2)}) collective-permute-start(bf16[64,2048]{1,0:T(8,128)(2,1)S(1)} %shard_map.97.rest_0_.first.edge), channel_id=1, source_target_pairs={{0,4},{4,8},{8,12},{12,0},{1,5},{5,9},{9,13},{13,1},{2,6},{6,10},{... | collective-permute-start | bytes 786440 | tf_op jit(solution)/shard_map/ppermute | solution.py:461
  13.1 8.1 %collective-permute-start.3 = (bf16[64,2048]{1,0:T(8,128)(2,1)S(1)}, bf16[64,2048]{1,0:T(8,128)(2,1)S(1)}, u32[]{:S(2)}, u32[]{:S(2)}) collective-permute-start(bf16[64,2048]{1,0:T(8,128)(2,1)S(1)} %shard_map.98.second), channel_id=1, source_target_pairs={{0,4},{4,8},{8,12},{12,0},{1,5},{5,9},{9,13},{13,1},{2,6},{6,10},{... | collective-permute-start | bytes 786440 | tf_op jit(solution)/shard_map/ppermute | solution.py:471
  17.9 1.6 %copy-start = (bf16[256,2048]{1,0:T(8,128)(2,1)S(1)}, bf16[256,2048]{1,0:T(8,128)(2,1)}, u32[]{:S(2)}) copy-start(bf16[256,2048]{1,0:T(8,128)(2,1)} %boundary.1) | copy-start | bytes 3145732
  18.0 1.6 %copy-start.1 = (f32[16,128]{1,0:T(8,128)S(1)}, f32[16,128]{1,0:T(8,128)}, u32[]{:S(2)}) copy-start(f32[16,128]{1,0:T(8,128)} %constant.2.clone.smooth) | copy-start | bytes 24580
  21.2 4.6 %collective-permute-start.5 = (f32[8,128]{1,0:T(8,128)S(1)}, f32[8,128]{1,0:T(8,128)S(1)}, u32[]{:S(2)}, u32[]{:S(2)}) collective-permute-start(f32[8,128]{1,0:T(8,128)S(1)} %shard_map.104.refs_0_), channel_id=1, source_target_pairs={{0,2},{1,3},{2,0},{3,1},{4,6},{5,7},{6,4},{7,5},{8,10},{9,11},{10,... | collective-permute-start | bytes 12296 | tf_op jit(solution)/shard_map/ppermute | solution.py:497
  23.9 3.6 %collective-permute-start.6 = (f32[8,128]{1,0:T(8,128)S(1)}, f32[8,128]{1,0:T(8,128)S(1)}, u32[]{:S(2)}, u32[]{:S(2)}) collective-permute-start(f32[8,128]{1,0:T(8,128)S(1)} %shard_map.104.refs_0_), channel_id=1, source_target_pairs={{0,1},{1,0},{2,3},{3,2},{4,5},{5,4},{6,7},{7,6},{8,9},{9,8},{10,11... | collective-permute-start | bytes 12296 | tf_op jit(solution)/shard_map/ppermute | solution.py:497
  25.5 2.0 %collective-permute-start.7 = (f32[8,128]{1,0:T(8,128)S(1)}, f32[8,128]{1,0:T(8,128)S(1)}, u32[]{:S(2)}, u32[]{:S(2)}) collective-permute-start(f32[8,128]{1,0:T(8,128)S(1)} %shard_map.104.refs_0_), channel_id=1, source_target_pairs={{0,4},{1,2},{2,1},{3,7},{4,0},{5,6},{6,5},{7,3},{8,12},{9,10},{10,... | collective-permute-start | bytes 12296 | tf_op jit(solution)/shard_map/ppermute | solution.py:497

commit v5 on v4

--- a/solution.py
+++ b/solution.py
@@ -16,7 +16,9 @@
 TAPS = (0.0625, 0.25, 0.375, 0.25, 0.0625)
 FAR = 1 << 20
 VMEM_LIMIT = 16 * 1024 * 1024
-TURN_UNROLL = 4
+TURN_UNROLL = 16
+PLAN_UNROLL = 8
+EARLY_BLOCKS = 5 / 8
 
 f32 = jnp.float32
 bf16 = jnp.bfloat16
@@ -34,6 +36,22 @@
     return tuple(table)
 
 
+def halo_table(n_parts, n_gz, n_ty, second):
+    table = []
+    for p in range(n_parts):
+        for z in range(n_gz):
+            for t in range(n_ty):
+                partner = t + 1 if (t % 2 == 0) != (second != (z % 2 == 1)) else t - 1
+                if 0 <= partner < n_ty:
+                    there = (p, z, partner)
+                elif (p ^ 1) < n_parts:
+                    there = (p ^ 1, z, t)
+                else:
+                    continue
+                table.append(tuple((a * n_gz + b) * n_ty + c for a, b, c in ((p, z, t), there)))
+    return tuple(table)
+
+
 def partner_of(tile, d, second):
     up = (tile // d) % 2 == int(second)
     return tile + jnp.where(up, d, -d)
@@ -44,7 +62,7 @@
 
 
 def takes_bottom(second):
-    return (lax.axis_index("ty") % 2 == 0) != second
+    return (lax.axis_index("ty") + lax.axis_index("gz")) % 2 == int(second)
 
 
 def hat(coord, position):
@@ -60,13 +78,26 @@
     return jnp.dot(left, right, preferred_element_type=f32).astype(bf16)
 
 
+def build_tables(col_pos, first, tables):
+    reach = BLOCK + LANES
+    coord = lax.broadcasted_iota(jnp.int32, (reach, BLOCK), 0).astype(f32) - float(LANES // 2)
+    edge = jnp.zeros((LANES // 2, BLOCK), bf16)
+
+    @pl.loop(0, tables.shape[0])
+    def _(k):
+        at = pl.multiple_of((first + k) * BLOCK, BLOCK)
+        pos = col_pos[:, pl.ds(at, BLOCK)] - at.astype(f32)
+        tables[k, 0 : LANES // 2, :] = edge
+        tables[k, LANES // 2 : LANES // 2 + reach, :] = hat(coord, pos).astype(bf16)
+        tables[k, LANES // 2 + reach :, :] = edge
+
+
 def fetch_kernel(all_rows, section, row_shift, row_frac, col_shift, col_frac, *rest):
-    held, send_first, mid_table, first_table, second_table, col_table = rest[:6]
-    row_shift_v, row_frac_v, col_shift_v, col_frac_v, sems = rest[6:]
+    send_first, held, row_pos, col_pos, tables = rest[:5]
+    row_shift_v, row_frac_v, col_shift_v, col_frac_v, sems = rest[5:]
     n_rows, n_cols = section.shape
-    tile = lax.axis_index("ty")
-    base = tile * n_rows
-    first_at = pl.multiple_of(jnp.where(takes_bottom(False), n_rows - MARGIN, 0), MARGIN)
+    base = lax.axis_index("ty") * n_rows
+    at = pl.multiple_of(jnp.where(takes_bottom(False), n_rows - MARGIN, 0), MARGIN)
     copies = [
         pltpu.make_async_copy(source, target, sems.at[k])
         for k, (source, target) in enumerate(
@@ -75,7 +106,7 @@
                 (col_frac, col_frac_v),
                 (row_shift, row_shift_v),
                 (row_frac, row_frac_v),
-                (section.at[pl.ds(first_at, MARGIN), :], send_first),
+                (section.at[pl.ds(at, MARGIN), :], send_first),
                 (section, held),
             )
         )
@@ -84,42 +115,23 @@
         copy.start()
     for copy in copies[:4]:
         copy.wait()
-
-    reach = BLOCK + LANES
-    coord = lax.broadcasted_iota(jnp.int32, (reach, BLOCK), 0).astype(f32)
-    ids = lax.broadcasted_iota(jnp.int32, (1, BLOCK), 1)
-    edge = jnp.zeros((LANES // 2, BLOCK), bf16)
-
-    @pl.loop(0, n_cols // BLOCK)
-    def _(j):
-        cols = pl.ds(pl.multiple_of(j * BLOCK, BLOCK), BLOCK)
-        pos = source_positions(
-            ids + j * BLOCK, col_shift_v[:, cols], col_frac_v[:, cols], n_cols - 2, j * BLOCK - LANES // 2
-        )
-        col_table[j, 0 : LANES // 2, :] = edge
-        col_table[j, LANES // 2 : LANES // 2 + reach, :] = hat(coord, pos).astype(bf16)
-        col_table[j, LANES // 2 + reach :, :] = edge
-
+    ids = lax.broadcasted_iota(jnp.int32, (1, n_cols), 1)
+    col_pos[...] = source_positions(ids, col_shift_v[...], col_frac_v[...], n_cols - 2, 0)
     ids = lax.broadcasted_iota(jnp.int32, (1, n_rows), 1) + base
-    pos = source_positions(ids, row_shift_v[...], row_frac_v[...], all_rows - 2, base)
-    coord = lax.broadcasted_iota(jnp.int32, (n_rows, n_rows - 2 * MARGIN), 0).astype(f32)
-    mid_table[...] = hat(coord, pos[:, MARGIN : n_rows - MARGIN]).T.astype(bf16)
-    half = n_rows // 2
-    slot = lax.broadcasted_iota(jnp.int32, (MARGIN + half, MARGIN), 0)
-    for second, table in ((False, first_table), (True, second_table)):
-        bottom = takes_bottom(second)
-        start = jnp.where(
-            slot < MARGIN, jnp.where(bottom, n_rows, -MARGIN), jnp.where(bottom, half - MARGIN, -MARGIN)
-        )
-        here = jnp.where(bottom, pos[:, n_rows - MARGIN :], pos[:, :MARGIN])
-        table[...] = hat((slot + start).astype(f32), here).T.astype(bf16)
+    row_pos[...] = source_positions(ids, row_shift_v[...], row_frac_v[...], all_rows - 2, base)
+    build_tables(col_pos, 0, tables)
     for copy in copies[4:]:
         copy.wait()
 
 
-def columns_of(mix, col_table, out_ref):
-    for j in range(col_table.shape[0]):
-        out_ref[:, j * BLOCK : (j + 1) * BLOCK] = times(mix[:, j * BLOCK : (j + 1) * BLOCK + 2 * LANES], col_table[j])
+def columns_of(mix, tables, out_ref):
+    j = 0
+    for table in tables:
+        for k in range(table.shape[0]):
+            out_ref[:, j * BLOCK : (j + 1) * BLOCK] = times(
+                mix[:, j * BLOCK : (j + 1) * BLOCK + 2 * LANES], table[k]
+            )
+            j += 1
 
 
 def clear_sides(mix):
@@ -128,28 +140,50 @@
     mix[:, mix.shape[1] - LANES :] = edge
 
 
-def middle_kernel(held, mid_table, col_table, mid_ref, send_second, mix):
+def edge_table(second, row_pos, table):
+    n_rows = row_pos.shape[1]
+    half = n_rows // 2
+    slot = lax.broadcasted_iota(jnp.int32, (MARGIN + half, MARGIN), 0)
+    bottom = takes_bottom(second)
+    start = jnp.where(
+        slot < MARGIN, jnp.where(bottom, n_rows, -MARGIN), jnp.where(bottom, half - MARGIN, -MARGIN)
+    )
+    here = jnp.where(bottom, row_pos[:, n_rows - MARGIN :], row_pos[:, :MARGIN])
+    table[...] = hat((slot + start).astype(f32), here).T.astype(bf16)
+
+
+def middle_kernel(held, row_pos, col_pos, tables, mid_ref, more_tables, first_table, second_table, mix):
+    n_rows, n_cols = held.shape
+    build_tables(col_pos, tables.shape[0], more_tables)
+    edge_table(False, row_pos, first_table)
+    edge_table(True, row_pos, second_table)
+    coord = lax.broadcasted_iota(jnp.int32, (n_rows, n_rows - 2 * MARGIN), 0).astype(f32)
+    mid_table = hat(coord, row_pos[:, MARGIN : n_rows - MARGIN]).T.astype(bf16)
+    clear_sides(mix)
+    for j in range(n_cols // BLOCK):
+        mix[:, LANES + j * BLOCK : LANES + (j + 1) * BLOCK] = times(
+            mid_table, held[:, j * BLOCK : (j + 1) * BLOCK]
+        )
+    columns_of(mix, (tables, more_tables), mid_ref)
+
+
+def send_kernel(held, _, send_second):
     n_rows = held.shape[0]
-    clear_sides(mix)
-    for j in range(col_table.shape[0]):
-        mix[:, LANES + j * BLOCK : LANES + (j + 1) * BLOCK] = times(
-            mid_table[...], held[:, j * BLOCK : (j + 1) * BLOCK]
-        )
-    columns_of(mix, col_table, mid_ref)
     at = pl.multiple_of(jnp.where(takes_bottom(True), n_rows - MARGIN, 0), MARGIN)
     send_second[...] = held[pl.ds(at, MARGIN), :]
 
 
-def edges_kernel(second, halo, held, table, col_table, *rest):
+def edges_kernel(second, halo, held, table, tables, more_tables, *rest):
     edge_ref, mix = rest[-2:]
-    half = held.shape[0] // 2
+    n_rows, n_cols = held.shape
+    half = n_rows // 2
     own = pl.ds(pl.multiple_of(jnp.where(takes_bottom(second), half, 0), half), half)
     clear_sides(mix)
-    for j in range(col_table.shape[0]):
+    for j in range(n_cols // BLOCK):
         here = slice(j * BLOCK, (j + 1) * BLOCK)
         stack = jnp.concatenate([halo[:, here], held[own, here]], axis=0)
         mix[:, LANES + j * BLOCK : LANES + (j + 1) * BLOCK] = times(table[...], stack)
-    columns_of(mix, col_table, edge_ref)
+    columns_of(mix, (tables, more_tables), edge_ref)
 
 
 def turn_patches(peaks, i, rows, source, turned, first):
@@ -163,24 +197,23 @@
             turned[dx * n_turned + first + j] = pltpu.roll(block, (peaks[1, 0, i, j] + (dx - 1)) % PATCH, 1)
 
 
-def turn_middle_kernel(n_ty, swaps, peaks, mid, turned, bands, peak, row_weights):
-    n_patches = bands.shape[0]
-    for i in range(mid.shape[0] // MARGIN):
-        turn_patches(peaks, i, slice(i * MARGIN, (i + 1) * MARGIN), mid, turned, i * (mid.shape[1] // PATCH))
+def plan_windows(peaks, bands, peak):
     lane = lax.broadcasted_iota(jnp.int32, (PATCH // 8, LANES), 1)
     offset = lane - 8 * lax.broadcasted_iota(jnp.int32, (PATCH // 8, LANES), 0) + 1
-
     patch_rows, patch_cols = peaks.shape[2:]
     for i in range(patch_rows):
 
-        @pl.loop(0, patch_cols)
+        @pl.loop(0, patch_cols, unroll=PLAN_UNROLL)
         def _(j):
             p = i * patch_cols + j
             bands[p] = jnp.where(((offset - peaks[0, 0, i, j]) & (PATCH - 1)) <= 9, 1.0, 0.0)
             for c in range(2):
                 peak[c, pl.ds(p, 1), :] = jnp.full((1, LANES), peaks[c, 0, i, j], jnp.int32).astype(f32)
 
-    fill_row_weights(n_ty, swaps, mid.shape[0] // MARGIN, row_weights)
+
+def turn_middle_kernel(peaks, mid, turned):
+    for i in range(mid.shape[0] // MARGIN):
+        turn_patches(peaks, i, slice(i * MARGIN, (i + 1) * MARGIN), mid, turned, i * (mid.shape[1] // PATCH))
 
 
 def edge_patch_row(second, patch_rows):
@@ -189,21 +222,6 @@
 
 def turn_first_kernel(patch_rows, peaks, edge, turned):
     turn_patches(peaks, edge_patch_row(False, patch_rows), slice(None), edge, turned, 0)
-
-
-def turn_second_kernel(patch_rows, peaks, mid, first, second, rendered, turned, sems):
-    n_mid = mid.shape[0]
-    n_rows = n_mid + 2 * MARGIN
-    moves = [(mid, pl.ds(MARGIN, n_mid))]
-    for edge, which in ((first, False), (second, True)):
-        at = pl.multiple_of(jnp.where(takes_bottom(which), n_rows - MARGIN, 0), MARGIN)
-        moves.append((edge, pl.ds(at, MARGIN)))
-    copies = [pltpu.make_async_copy(a, rendered.at[b, :], sems.at[k]) for k, (a, b) in enumerate(moves)]
-    for copy in copies:
-        copy.start()
-    turn_patches(peaks, edge_patch_row(True, patch_rows), slice(None), second, turned, 0)
-    for copy in copies:
-        copy.wait()
 
 
 def patch_row_flow(i, turned_edge, turned_mid, bands, peak, smooth, old_of, acc):
@@ -250,16 +268,32 @@
     return sum(jnp.where(at == c * patch_rows + i, line, 0.0) for c, line in enumerate(lines))
 
 
-def boundary_kernel(turned_mid, turned_first, turned_second, bands, peak, boundary, smooth, out_ref, acc, whole, sem):
+def waiting_kernel(n_ty, swaps, peaks, mid, first, second, turned_mid, turned_first, boundary, smooth, _, *rest):
+    rendered, turned_second, bands, peak, row_weights, flow, acc, whole, sems = rest
     n_rows = boundary.shape[0]
     patch_rows = n_rows // PATCH
-    out_ref[...] = jnp.zeros_like(out_ref)
-
-    @pl.when(lax.axis_index("gz") == 0)
+    moves = [(mid, pl.ds(MARGIN, mid.shape[0]))]
+    for edge, which in ((first, False), (second, True)):
+        at = pl.multiple_of(jnp.where(takes_bottom(which), n_rows - MARGIN, 0), MARGIN)
+        moves.append((edge, pl.ds(at, MARGIN)))
+    copies = [pltpu.make_async_copy(a, rendered.at[b, :], sems.at[k]) for k, (a, b) in enumerate(moves)]
+    fetch = pltpu.make_async_copy(boundary, whole, sems.at[len(moves)])
+    has_boundary = lax.axis_index("gz") == 0
+
+    @pl.when(has_boundary)
     def _():
-        copy = pltpu.make_async_copy(boundary, whole, sem)
+        fetch.start()
+
+    for copy in copies:
         copy.start()
-        copy.wait()
+    flow[...] = jnp.zeros_like(flow)
+    turn_patches(peaks, edge_patch_row(True, patch_rows), slice(None), second, turned_second, 0)
+    plan_windows(peaks, bands, peak)
+    fill_row_weights(n_ty, swaps, patch_rows, row_weights)
+
+    @pl.when(has_boundary)
+    def _():
+        fetch.wait()
 
         @pl.loop(0, patch_rows)
         def _(k):
@@ -272,7 +306,7 @@
                 return jnp.concatenate([whole[pl.ds(at_edge, MARGIN), cols], whole[pl.ds(at_mid, MARGIN), cols]], axis=0)
 
             def flow_with(turned_edge):
-                out_ref[...] += put_lines(
+                flow[...] += put_lines(
                     patch_row_flow(i, turned_edge, turned_mid, bands, peak, smooth, old_of, acc), i, patch_rows
                 )
 
@@ -283,6 +317,9 @@
             @pl.when(k != 0)
             def _():
                 flow_with(turned_second)
+
+    for copy in copies:
+        copy.wait()
 
 
 def window_kernel(second, turned_mid, turned_edge, bands, peak, old_mid, old_edge, smooth, before, out_ref, acc):
@@ -377,10 +414,14 @@
     )
 
 
+def in_hbm(x):
+    return pltpu.with_memory_space_constraint(x, pltpu.HBM)
+
+
 def local(sections, boundary, row_shift, row_frac, col_shift, col_frac, peak_shift):
     section = sections[0]
     n_rows, n_cols = section.shape
-    n_ty, n_gz = lax.axis_size("ty"), lax.axis_size("gz")
+    n_ty, n_gz, n_parts = lax.axis_size("ty"), lax.axis_size("gz"), lax.axis_size("parts")
     patch_rows, patch_cols = n_rows // PATCH, n_cols // PATCH
     n_patches = patch_rows * patch_cols
     all_rows = n_rows * n_ty
@@ -393,25 +434,26 @@
     shape = jax.ShapeDtypeStruct
     to_next = [(i, (i + 1) % n_gz) for i in range(n_gz)]
 
-    swaps, tables = [], []
+    swaps, routes = [], []
     for d in range(-(-2 * SMOOTH_PASSES // patch_rows), 0, -1):
         for other in (False, True):
             if has_partners(n_ty, d, other):
                 swaps.append((d, other))
-                tables.append(swap_table(n_gz, n_ty, d, other))
-
-    held, send_first, mid_table, first_table, second_table, col_table = call(
+                routes.append(swap_table(n_gz, n_ty, d, other))
+
+    early = max(1, min(n_blocks - 1, int(n_blocks * EARLY_BLOCKS)))
+    window = BLOCK + 2 * LANES
+    send_first, held, row_pos, col_pos, tables = call(
         functools.partial(fetch_kernel, all_rows),
         (
+            shape((MARGIN, n_cols), bf16),
             shape((n_rows, n_cols), bf16),
-            shape((MARGIN, n_cols), bf16),
-            shape((n_mid, n_rows), bf16),
-            shape((MARGIN, MARGIN + half), bf16),
-            shape((MARGIN, MARGIN + half), bf16),
-            shape((n_blocks, BLOCK + 2 * LANES, BLOCK), bf16),
+            shape((1, n_rows), f32),
+            shape((1, n_cols), f32),
+            shape((early, window, BLOCK), bf16),
         ),
         [hbm] * 5,
-        [vmem] * 6,
+        [vmem] * 5,
         [
             pltpu.VMEM((1, n_rows), jnp.int32),
             pltpu.VMEM((1, n_rows), jnp.int32),
@@ -419,45 +461,42 @@
             pltpu.VMEM((1, n_cols), jnp.int32),
             pltpu.SemaphoreType.DMA((6,)),
         ],
-    )(*(pltpu.with_memory_space_constraint(x, pltpu.HBM) for x in (section, row_shift, row_frac, col_shift, col_frac)))
-    first = lax.ppermute(send_first, ("gz", "ty"), swap_table(n_gz, n_ty, 1, False))
-
-    mid, send_second = call(
+    )(*(in_hbm(x) for x in (section, row_shift, row_frac, col_shift, col_frac)))
+    first = lax.ppermute(send_first, ("parts", "gz", "ty"), halo_table(n_parts, n_gz, n_ty, False))
+
+    edge_shape = shape((MARGIN, MARGIN + half), bf16)
+    mid, more_tables, first_table, second_table = call(
         middle_kernel,
-        (shape((n_mid, n_cols), bf16), shape((MARGIN, n_cols), bf16)),
-        [vmem] * 3,
-        [vmem] * 2,
+        (shape((n_mid, n_cols), bf16), shape((n_blocks - early, window, BLOCK), bf16), edge_shape, edge_shape),
+        [vmem] * 4,
+        [vmem] * 4,
         [pltpu.VMEM((n_mid, n_cols + 2 * LANES), bf16)],
-    )(held, mid_table, col_table)
+    )(held, row_pos, col_pos, tables)
     old_mid = lax.ppermute(mid, "gz", to_next)
-    second = lax.ppermute(send_second, ("gz", "ty"), swap_table(n_gz, n_ty, 1, True))
-
-    terms = (len(swaps) + 1) * 2 * patch_rows
-    turned_mid, bands, peak, row_weights = call(
-        functools.partial(turn_middle_kernel, n_ty, tuple(swaps)),
-        (
-            shape((3 * n_patches, MARGIN, LANES), bf16),
-            shape((n_patches, PATCH // 8, LANES), f32),
-            shape((2, n_patches, LANES), f32),
-            shape((terms, 8, LANES), f32),
-        ),
+    turned_mid = call(
+        turn_middle_kernel,
+        shape((3 * n_patches, MARGIN, LANES), bf16),
         [smem, vmem],
-        [vmem] * 4,
+        vmem,
         flops=1_000_000_000,
         moved=3_000_000,
     )(peak_shift, mid)
 
+    send_second = call(send_kernel, shape((MARGIN, n_cols), bf16), [vmem, unread], vmem, flops=4_000_000_000)(
+        held, turned_mid
+    )
+    second = lax.ppermute(send_second, ("parts", "gz", "ty"), halo_table(n_parts, n_gz, n_ty, True))
     def render_edges(which, *args):
         return call(
             functools.partial(edges_kernel, which),
             shape((MARGIN, n_cols), bf16),
-            [vmem] * 4 + [unread] * (len(args) - 4),
+            [vmem] * 5 + [unread] * (len(args) - 5),
             vmem,
             [pltpu.VMEM((MARGIN, n_cols + 2 * LANES), bf16)],
         )(*args)
 
     turned_shape = shape((3 * patch_cols, MARGIN, LANES), bf16)
-    first_edge = render_edges(False, first, held, first_table, col_table)
+    first_edge = render_edges(False, first, held, first_table, tables, more_tables, send_second)
     old_first = lax.ppermute(first_edge, "gz", to_next)
     turned_first = call(
         functools.partial(turn_first_kernel, patch_rows),
@@ -467,34 +506,32 @@
         flops=500_000_000,
         moved=1_000_000,
     )(peak_shift, first_edge)
-    second_edge = render_edges(True, second, held, second_table, col_table, first_edge)
+    second_edge = render_edges(True, second, held, second_table, tables, more_tables, turned_first)
     old_second = lax.ppermute(second_edge, "gz", to_next)
-    rendered, turned_second = call(
-        functools.partial(turn_second_kernel, patch_rows),
-        (shape((n_rows, n_cols), bf16), turned_shape),
-        [smem] + [vmem] * 3,
-        [hbm, vmem],
-        [pltpu.SemaphoreType.DMA((3,))],
+    smooth = jnp.asarray(column_smoother(patch_cols))
+    acc = pltpu.VMEM((9 * patch_cols * 8, LANES), f32)
+    terms = (len(swaps) + 1) * 2 * patch_rows
+    rendered, turned_second, bands, peak, row_weights, payload = call(
+        functools.partial(waiting_kernel, n_ty, tuple(swaps)),
+        (
+            shape((n_rows, n_cols), bf16),
+            turned_shape,
+            shape((n_patches, PATCH // 8, LANES), f32),
+            shape((2, n_patches, LANES), f32),
+            shape((terms, 8, LANES), f32),
+            shape((8, LANES), f32),
+        ),
+        [smem] + [vmem] * 5 + [hbm, vmem, unread],
+        [hbm] + [vmem] * 5,
+        [acc, pltpu.VMEM((n_rows, n_cols), bf16), pltpu.SemaphoreType.DMA((4,))],
         flops=1_000_000_000,
         moved=3_000_000,
-    )(peak_shift, mid, first_edge, second_edge)
-
-    smooth = jnp.asarray(column_smoother(patch_cols))
-    acc = pltpu.VMEM((9 * patch_cols * 8, LANES), f32)
-    payload = call(
-        boundary_kernel,
-        shape((8, LANES), f32),
-        [vmem] * 5 + [hbm, vmem],
-        vmem,
-        [acc, pltpu.VMEM((n_rows, n_cols), bf16), pltpu.SemaphoreType.DMA],
-        flops=1_000_000_000,
-        moved=3_000_000,
-    )(turned_mid, turned_first, turned_second, bands, peak, boundary, smooth)
-    for which, turned, old in ((False, turned_first, old_first), (True, turned_second, old_second)):
+    )(peak_shift, mid, first_edge, second_edge, turned_mid, turned_first, in_hbm(boundary), smooth, old_mid)
+    for which, turned, old in ((True, turned_second, old_first), (False, turned_first, old_second)):
         payload = call(
             functools.partial(window_kernel, which), shape((8, LANES), f32), [vmem] * 8, vmem, [acc]
         )(turned_mid, turned, bands, peak, old_mid, old, smooth, payload)
-    blocks = [payload] + [lax.ppermute(payload, ("gz", "ty"), table) for table in tables]
+    blocks = [payload] + [lax.ppermute(payload, ("gz", "ty"), route) for route in routes]
     flow = call(
         rows_kernel, shape((2, 1, patch_rows, patch_cols), f32), [vmem] * (1 + len(blocks)), vmem
     )(row_weights, *blocks)

time: 28.3 us -> 27.4 us (0.968)
  starting transfers between devices: 9.75 us -> 9.08 us
    ppermute x1, waiting for transfers between devices: 0.01 us -> 1.27 us  [local(): old_second = lax.ppermute(second_edge, 'gz', to_next)]
    ppermute x5, waiting for transfers between devices: 7.16 us -> 5.95 us  [the longest x3 2.7 us: local(): lax.ppermute(payload, ('gz', 'ty'), route)]
    ppermute x1, starting transfers between devices: 1.8 us -> 0.78 us  [local(): old_second = lax.ppermute(second_edge, 'gz', to_next)]
    ppermute x5, starting transfers between devices: 7.4 us -> 8.18 us  [the longest x3 3.51 us: local(): lax.ppermute(payload, ('gz', 'ty'), route)]
    ppermute x1, starting transfers between devices: 0.5 us -> 0.06 us  [local(): old_mid = lax.ppermute(mid, 'gz', to_next)]
  transfers between devices with their start and end apart: 8 -> 8, of which waited for: 3 -> 5; matrix products, arithmetic and copies ran while one was open for 0% -> 0% of each run, Pallas kernels for 29% -> 30%
where the time goes in v5:
time: 27.4 us; the launch traced here: 27.2 us
  Pallas kernels  10.1 us (37%)
  starting transfers between devices  9.08 us (33%)
  waiting for transfers between devices  7.23 us (26%)
  between operations  0.75 us (3%)
    pallas_call x1, Pallas kernels, local(): call(functools.partial(waiting_kernel, n_ty, tuple(swaps)), (shape((n_row...  3.89 us
    ppermute x3, starting transfers between devices, local(): lax.ppermute(payload, ('gz', 'ty'), route)  3.51 us
    ppermute x1, starting transfers between devices, local(): lax.ppermute(send_first, ('parts', 'gz', 'ty'), halo_table(n_parts, n_gz,...  3.09 us
    ppermute x3, waiting for transfers between devices, local(): lax.ppermute(payload, ('gz', 'ty'), route)  2.7 us
    ppermute x1, waiting for transfers between devices, local(): lax.ppermute(send_second, ('parts', 'gz', 'ty'), halo_table(n_parts, n_gz...  2.62 us
    ppermute x1, starting transfers between devices, local(): lax.ppermute(send_second, ('parts', 'gz', 'ty'), halo_table(n_parts, n_gz...  1.59 us
    pallas_call x1, Pallas kernels, local(): call(functools.partial(fetch_kernel, all_rows), (shape((MARGIN, n_cols),...  1.43 us
    pallas_call x2, Pallas kernels, render_edges(): call(functools.partial(edges_kernel, which), shape((MARGIN, n_cols), bf16...  1.31 us
  transfers between devices with their start and end apart: 8, of which 5 were waited for; matrix products, arithmetic and copies ran while one was open for 0% of the time, Pallas kernels for 30%

profile of v5, /device:TPU:0, one launch (start us, length us, event | category | flops | bytes accessed | tf_op | source)
XLA Modules:
  0.0 27.2 jit_solution(7668932093598232721)
XLA Ops:
  0.6 0.0 copy-start.1
  0.6 1.4 %shard_map.95 = (bf16[64,2048]{1,0:T(8,128)(2,1)S(1)}, bf16[256,2048]{1,0:T(8,128)(2,1)S(1)}, f32[1,256]{1,0:T(1,128)S(1)}, f32[1,2048]{1,0:T(1,128)S(1)}, bf16[5,512,256]{2,1,0:T(8,128)(2,1)S(1)}) custom-call(bf16[256,2048]{1,0:T(8,128)(2,1)} %bitcast.2, s32[1,256]{1,0:T(1,128)} %row_shift.1, s32[1,256]{1,0:T(1,128)} %row_frac.1, s32[1,2048]{1,0:T(1,128)} %col_shift.1, ...), custom_call_target="tpu_custom_call" | custom-call | tf_op jit(solution)/shard_map/pallas_call | solution.py:446
  2.1 3.1 %collective-permute-start = (bf16[64,2048]{1,0:T(8,128)(2,1)S(1)}, bf16[64,2048]{1,0:T(8,128)(2,1)S(1)}, u32[]{:S(2)}, u32[]{:S(2)}) collective-permute-start(bf16[64,2048]{1,0:T(8,128)(2,1)S(1)} %get-tuple-element.22), channel_id=1, source_target_pairs={{0,1},{1,0},{2,3},{3,2},{4,20},{5,6},{6,5},{7,23},{8,9},{9,8},{10,... | collective-permute-start | bytes 786440 | tf_op jit(solution)/shard_map/ppermute | solution.py:465
  5.2 1.0 %shard_map.96 = (bf16[128,2048]{1,0:T(8,128)(2,1)S(1)}, bf16[3,512,256]{2,1,0:T(8,128)(2,1)S(1)}, bf16[64,192]{1,0:T(8,128)(2,1)S(1)}, bf16[64,192]{1,0:T(8,128)(2,1)S(1)}) custom-call(bf16[256,2048]{1,0:T(8,128)(2,1)S(1)} %get-tuple-element.17.held, f32[1,256]{1,0:T(1,128)S(1)} %get-tuple-element.18.row_pos, f32[1,2048]{1,0:T(1,128)S(1)} %get-tuple-element.19.col_pos, ...), custom_call_target="tpu_custom_call" | custom-call | tf_op jit(solution)/shard_map/pallas_call | solution.py:468
  6.1 0.1 collective-permute-start.2
  6.2 0.0 copy-done.1
  6.2 1.0 %shard_map.97._.turned_mid = bf16[96,64,128]{2,1,0:T(8,128)(2,1)S(1)} custom-call(s32[2,1,2,16]{3,2,1,0:T(2,128)S(1)} %copy-done.1, bf16[128,2048]{1,0:T(8,128)(2,1)S(1)} %get-tuple-element.21.mid), custom_call_target="tpu_custom_call" | custom-call | flops 1000000000 | bytes 3000000 | tf_op jit(solution)/shard_map/pallas_call | solution.py:476
  7.3 1.6 %collective-permute-start.1 = (bf16[64,2048]{1,0:T(8,128)(2,1)S(1)}, bf16[64,2048]{1,0:T(8,128)(2,1)S(1)}, u32[]{:S(2)}, u32[]{:S(2)}) collective-permute-start(bf16[64,2048]{1,0:T(8,128)(2,1)S(1)} %shard_map.98.rest_0_), channel_id=1, source_target_pairs={{0,16},{1,2},{2,1},{3,19},{4,5},{5,4},{6,7},{7,6},{8,24},{9,10},{1... | collective-permute-start | bytes 786440 | tf_op jit(solution)/shard_map/ppermute | solution.py:488
  8.9 0.6 %collective-permute-done.halo = bf16[64,2048]{1,0:T(8,128)(2,1)S(1)} collective-permute-done((bf16[64,2048]{1,0:T(8,128)(2,1)S(1)}, bf16[64,2048]{1,0:T(8,128)(2,1)S(1)}, u32[]{:S(2)}, u32[]{:S(2)}) %collective-permute-start) | collective-permute-done | bytes 262176 | tf_op jit(solution)/shard_map/ppermute | solution.py:465
  9.5 0.7 %shard_map.99.edge.first = bf16[64,2048]{1,0:T(8,128)(2,1)S(1)} custom-call(bf16[64,2048]{1,0:T(8,128)(2,1)S(1)} %collective-permute-done.halo, bf16[256,2048]{1,0:T(8,128)(2,1)S(1)} %get-tuple-element.17.held, bf16[64,192]{1,0:T(8,128)(2,1)S(1)} %get-tuple-element.23.table, bf16[5,512,256]{2,1,0:T(8,128)(2,1)S(1)} %get-tuple-element.20.tables, ...), custom_call_target="tpu_custom_call" | custom-call | tf_op jit(solution)/shard_map/pallas_call | solution.py:490
  10.2 0.1 collective-permute-start.4
  10.2 0.9 %shard_map.100.rest_0_.turned_first.turned_edge = bf16[48,64,128]{2,1,0:T(8,128)(2,1)S(1)} custom-call(s32[2,1,2,16]{3,2,1,0:T(2,128)S(1)} %copy-done.1, bf16[64,2048]{1,0:T(8,128)(2,1)S(1)} %shard_map.99.edge.first), custom_call_target="tpu_custom_call" | custom-call | flops 500000000 | bytes 1000000 | tf_op jit(solution)/shard_map/pallas_call | solution.py:501
  11.1 2.6 %collective-permute-done.1.halo = bf16[64,2048]{1,0:T(8,128)(2,1)S(1)} collective-permute-done((bf16[64,2048]{1,0:T(8,128)(2,1)S(1)}, bf16[64,2048]{1,0:T(8,128)(2,1)S(1)}, u32[]{:S(2)}, u32[]{:S(2)}) %collective-permute-start.1) | collective-permute-done | bytes 262176 | tf_op jit(solution)/shard_map/ppermute | solution.py:488
  13.7 0.0 copy-start
  13.7 0.7 %shard_map.101.second = bf16[64,2048]{1,0:T(8,128)(2,1)S(1)} custom-call(bf16[64,2048]{1,0:T(8,128)(2,1)S(1)} %collective-permute-done.1.halo, bf16[256,2048]{1,0:T(8,128)(2,1)S(1)} %get-tuple-element.17.held, bf16[64,192]{1,0:T(8,128)(2,1)S(1)} %get-tuple-element.25.table, bf16[5,512,256]{2,1,0:T(8,128)(2,1)S(1)} %get-tuple-element.20.tables, ...), custom_call_target="tpu_custom_call" | custom-call | tf_op jit(solution)/shard_map/pallas_call | solution.py:490
  14.4 0.8 %collective-permute-start.3 = (bf16[64,2048]{1,0:T(8,128)(2,1)S(1)}, bf16[64,2048]{1,0:T(8,128)(2,1)S(1)}, u32[]{:S(2)}, u32[]{:S(2)}) collective-permute-start(bf16[64,2048]{1,0:T(8,128)(2,1)S(1)} %shard_map.101.second), channel_id=1, source_target_pairs={{0,4},{4,8},{8,12},{12,0},{1,5},{5,9},{9,13},{13,1},{2,6},{6,10},{... | collective-permute-start | bytes 786440 | tf_op jit(solution)/shard_map/ppermute | solution.py:510
  15.2 0.0 collective-permute-done.2._.old_mid
  15.2 0.0 copy-done
  15.2 3.9 %shard_map.102 = (bf16[256,2048]{1,0:T(8,128)(2,1)}, bf16[48,64,128]{2,1,0:T(8,128)(2,1)S(1)}, f32[32,16,128]{2,1,0:T(8,128)S(1)}, f32[2,32,128]{2,1,0:T(8,128)S...) custom-call(s32[2,1,2,16]{3,2,1,0:T(2,128)S(1)} %copy-done.1, bf16[128,2048]{1,0:T(8,128)(2,1)S(1)} %get-tuple-element.21.mid, ...), custom_call_target="tpu_custom_call" | custom-call | flops 1000000000 | bytes 3000000 | tf_op jit(solution)/shard_map/pallas_call | solution.py:514
  19.1 0.0 collective-permute-done.4.old_edge
  19.1 1.3 %collective-permute-done.3.old_edge = bf16[64,2048]{1,0:T(8,128)(2,1)S(1)} collective-permute-done((bf16[64,2048]{1,0:T(8,128)(2,1)S(1)}, bf16[64,2048]{1,0:T(8,128)(2,1)S(1)}, u32[]{:S(2)}, u32[]{:S(2)}) %collective-permute-start.3) | collective-permute-done | bytes 262176 | tf_op jit(solution)/shard_map/ppermute | solution.py:510
  20.4 2.6 %collective-permute-start.5 = (f32[8,128]{1,0:T(8,128)S(1)}, f32[8,128]{1,0:T(8,128)S(1)}, u32[]{:S(2)}, u32[]{:S(2)}) collective-permute-start(f32[8,128]{1,0:T(8,128)S(1)} %shard_map.104.refs_0_), channel_id=1, source_target_pairs={{0,2},{1,3},{2,0},{3,1},{4,6},{5,7},{6,4},{7,5},{8,10},{9,11},{10,... | collective-permute-start | bytes 12296 | tf_op jit(solution)/shard_map/ppermute | solution.py:534
  23.0 0.9 %collective-permute-start.6 = (f32[8,128]{1,0:T(8,128)S(1)}, f32[8,128]{1,0:T(8,128)S(1)}, u32[]{:S(2)}, u32[]{:S(2)}) collective-permute-start(f32[8,128]{1,0:T(8,128)S(1)} %shard_map.104.refs_0_), channel_id=1, source_target_pairs={{0,1},{1,0},{2,3},{3,2},{4,5},{5,4},{6,7},{7,6},{8,9},{9,8},{10,11... | collective-permute-start | bytes 12296 | tf_op jit(solution)/shard_map/ppermute | solution.py:534
  23.9 0.0 collective-permute-start.7
  23.9 1.0 %collective-permute-done.5.refs_1_ = f32[8,128]{1,0:T(8,128)S(1)} collective-permute-done((f32[8,128]{1,0:T(8,128)S(1)}, f32[8,128]{1,0:T(8,128)S(1)}, u32[]{:S(2)}, u32[]{:S(2)}) %collective-permute-start.5) | collective-permute-done | bytes 4128 | tf_op jit(solution)/shard_map/ppermute | solution.py:534
  24.9 1.7 %collective-permute-done.6.refs_2_ = f32[8,128]{1,0:T(8,128)S(1)} collective-permute-done((f32[8,128]{1,0:T(8,128)S(1)}, f32[8,128]{1,0:T(8,128)S(1)}, u32[]{:S(2)}, u32[]{:S(2)}) %collective-permute-start.6) | collective-permute-done | bytes 4128 | tf_op jit(solution)/shard_map/ppermute | solution.py:534
  26.6 0.0 collective-permute-done.7.refs_3_
  26.6 0.6 %shard_map.105 = f32[2,1,2,16]{3,2,1,0:T(2,128)} custom-call(f32[16,8,128]{2,1,0:T(8,128)S(1)} %get-tuple-element.27.row_weights, f32[8,128]{1,0:T(8,128)S(1)} %shard_map.104.refs_0_, f32[8,128]{1,0:T(8,128)S(1)} %collective-permute-done.5.refs_1_, f32[8,128]{1,0:T(8,128)S(1)} %collective-permute-done.6.refs_2_, f32[8,128]{1,0:T(8,128)S(1)} %collective-permute-done.7.refs_3_), custom_call_target="tpu_custom_call" | custom-call | tf_op jit(solution)/shard_map/pallas_call | solution.py:535
  (3 shorter events, 0.1 us)
Async XLA Ops:
  0.6 5.6 %copy-start.1 = (s32[2,1,2,16]{3,2,1,0:T(2,128)S(1)}, s32[2,1,2,16]{3,2,1,0:T(2,128)}, u32[]{:S(2)}) copy-start(s32[2,1,2,16]{3,2,1,0:T(2,128)} %peaks.5) | copy-start | bytes 772
  2.1 7.4 %collective-permute-start = (bf16[64,2048]{1,0:T(8,128)(2,1)S(1)}, bf16[64,2048]{1,0:T(8,128)(2,1)S(1)}, u32[]{:S(2)}, u32[]{:S(2)}) collective-permute-start(bf16[64,2048]{1,0:T(8,128)(2,1)S(1)} %get-tuple-element.22), channel_id=1, source_target_pairs={{0,1},{1,0},{2,3},{3,2},{4,20},{5,6},{6,5},{7,23},{8,9},{9,8},{10,... | collective-permute-start | bytes 786440 | tf_op jit(solution)/shard_map/ppermute | solution.py:465
  6.1 9.1 %collective-permute-start.2 = (bf16[128,2048]{1,0:T(8,128)(2,1)S(1)}, bf16[128,2048]{1,0:T(8,128)(2,1)S(1)}, u32[]{:S(2)}, u32[]{:S(2)}) collective-permute-start(bf16[128,2048]{1,0:T(8,128)(2,1)S(1)} %get-tuple-element.21.mid), channel_id=1, source_target_pairs={{0,4},{4,8},{8,12},{12,0},{1,5},{5,9},{9,13},{13,1},{2,6},{6,10},{... | collective-permute-start | bytes 1572872 | tf_op jit(solution)/shard_map/ppermute | solution.py:475
  7.3 6.4 %collective-permute-start.1 = (bf16[64,2048]{1,0:T(8,128)(2,1)S(1)}, bf16[64,2048]{1,0:T(8,128)(2,1)S(1)}, u32[]{:S(2)}, u32[]{:S(2)}) collective-permute-start(bf16[64,2048]{1,0:T(8,128)(2,1)S(1)} %shard_map.98.rest_0_), channel_id=1, source_target_pairs={{0,16},{1,2},{2,1},{3,19},{4,5},{5,4},{6,7},{7,6},{8,24},{9,10},{1... | collective-permute-start | bytes 786440 | tf_op jit(solution)/shard_map/ppermute | solution.py:488
  10.2 8.9 %collective-permute-start.4 = (bf16[64,2048]{1,0:T(8,128)(2,1)S(1)}, bf16[64,2048]{1,0:T(8,128)(2,1)S(1)}, u32[]{:S(2)}, u32[]{:S(2)}) collective-permute-start(bf16[64,2048]{1,0:T(8,128)(2,1)S(1)} %shard_map.99.edge.first), channel_id=1, source_target_pairs={{0,4},{4,8},{8,12},{12,0},{1,5},{5,9},{9,13},{13,1},{2,6},{6,10},{... | collective-permute-start | bytes 786440 | tf_op jit(solution)/shard_map/ppermute | solution.py:500
  13.7 1.5 %copy-start = (f32[16,128]{1,0:T(8,128)S(1)}, f32[16,128]{1,0:T(8,128)}, u32[]{:S(2)}) copy-start(f32[16,128]{1,0:T(8,128)} %constant.2.clone.smooth) | copy-start | bytes 24580
  14.4 6.0 %collective-permute-start.3 = (bf16[64,2048]{1,0:T(8,128)(2,1)S(1)}, bf16[64,2048]{1,0:T(8,128)(2,1)S(1)}, u32[]{:S(2)}, u32[]{:S(2)}) collective-permute-start(bf16[64,2048]{1,0:T(8,128)(2,1)S(1)} %shard_map.101.second), channel_id=1, source_target_pairs={{0,4},{4,8},{8,12},{12,0},{1,5},{5,9},{9,13},{13,1},{2,6},{6,10},{... | collective-permute-start | bytes 786440 | tf_op jit(solution)/shard_map/ppermute | solution.py:510
  20.4 4.5 %collective-permute-start.5 = (f32[8,128]{1,0:T(8,128)S(1)}, f32[8,128]{1,0:T(8,128)S(1)}, u32[]{:S(2)}, u32[]{:S(2)}) collective-permute-start(f32[8,128]{1,0:T(8,128)S(1)} %shard_map.104.refs_0_), channel_id=1, source_target_pairs={{0,2},{1,3},{2,0},{3,1},{4,6},{5,7},{6,4},{7,5},{8,10},{9,11},{10,... | collective-permute-start | bytes 12296 | tf_op jit(solution)/shard_map/ppermute | solution.py:534
  23.0 3.6 %collective-permute-start.6 = (f32[8,128]{1,0:T(8,128)S(1)}, f32[8,128]{1,0:T(8,128)S(1)}, u32[]{:S(2)}, u32[]{:S(2)}) collective-permute-start(f32[8,128]{1,0:T(8,128)S(1)} %shard_map.104.refs_0_), channel_id=1, source_target_pairs={{0,1},{1,0},{2,3},{3,2},{4,5},{5,4},{6,7},{7,6},{8,9},{9,8},{10,11... | collective-permute-start | bytes 12296 | tf_op jit(solution)/shard_map/ppermute | solution.py:534
  23.9 2.7 %collective-permute-start.7 = (f32[8,128]{1,0:T(8,128)S(1)}, f32[8,128]{1,0:T(8,128)S(1)}, u32[]{:S(2)}, u32[]{:S(2)}) collective-permute-start(f32[8,128]{1,0:T(8,128)S(1)} %shard_map.104.refs_0_), channel_id=1, source_target_pairs={{0,4},{1,2},{2,1},{3,7},{4,0},{5,6},{6,5},{7,3},{8,12},{9,10},{10,... | collective-permute-start | bytes 12296 | tf_op jit(solution)/shard_map/ppermute | solution.py:534

commit v6 on v5

--- a/solution.py
+++ b/solution.py
@@ -18,7 +18,8 @@
 VMEM_LIMIT = 16 * 1024 * 1024
 TURN_UNROLL = 16
 PLAN_UNROLL = 8
-EARLY_BLOCKS = 5 / 8
+EARLY_BLOCKS = 7 / 8
+EDGE_PARTS = 2
 
 f32 = jnp.float32
 bf16 = jnp.bfloat16
@@ -124,11 +125,13 @@
         copy.wait()
 
 
-def columns_of(mix, tables, out_ref):
+def columns_of(mix, tables, *out_refs):
     j = 0
+    wide = out_refs[0].shape[1] // BLOCK
     for table in tables:
         for k in range(table.shape[0]):
-            out_ref[:, j * BLOCK : (j + 1) * BLOCK] = times(
+            at = j % wide
+            out_refs[j // wide][:, at * BLOCK : (at + 1) * BLOCK] = times(
                 mix[:, j * BLOCK : (j + 1) * BLOCK + 2 * LANES], table[k]
             )
             j += 1
@@ -173,8 +176,8 @@
     send_second[...] = held[pl.ds(at, MARGIN), :]
 
 
-def edges_kernel(second, halo, held, table, tables, more_tables, *rest):
-    edge_ref, mix = rest[-2:]
+def edges_kernel(second, parts, halo, held, table, tables, more_tables, *rest):
+    edge_refs, mix = rest[-1 - parts : -1], rest[-1]
     n_rows, n_cols = held.shape
     half = n_rows // 2
     own = pl.ds(pl.multiple_of(jnp.where(takes_bottom(second), half, 0), half), half)
@@ -183,18 +186,19 @@
         here = slice(j * BLOCK, (j + 1) * BLOCK)
         stack = jnp.concatenate([halo[:, here], held[own, here]], axis=0)
         mix[:, LANES + j * BLOCK : LANES + (j + 1) * BLOCK] = times(table[...], stack)
-    columns_of(mix, (tables, more_tables), edge_ref)
+    columns_of(mix, (tables, more_tables), *edge_refs)
 
 
 def turn_patches(peaks, i, rows, source, turned, first):
     patch_cols = source.shape[1] // PATCH
     n_turned = turned.shape[0] // 3
-
-    @pl.loop(0, patch_cols, unroll=TURN_UNROLL)
+    first_col = first % peaks.shape[3]
+
+    @pl.loop(0, patch_cols, unroll=min(TURN_UNROLL, patch_cols))
     def _(j):
         block = source[rows, pl.ds(pl.multiple_of(j * PATCH, PATCH), PATCH)]
         for dx in range(3):
-            turned[dx * n_turned + first + j] = pltpu.roll(block, (peaks[1, 0, i, j] + (dx - 1)) % PATCH, 1)
+            turned[dx * n_turned + first + j] = pltpu.roll(block, (peaks[1, 0, i, first_col + j] + (dx - 1)) % PATCH, 1)
 
 
 def plan_windows(peaks, bands, peak):
@@ -224,11 +228,12 @@
     turn_patches(peaks, edge_patch_row(False, patch_rows), slice(None), edge, turned, 0)
 
 
-def patch_row_flow(i, turned_edge, turned_mid, bands, peak, smooth, old_of, acc):
+def patch_row_flow(i, cols, turned_edge, turned_mid, bands, peak, smooth, old_of, acc):
     patch_cols = turned_edge.shape[0] // 3
     n_patches = bands.shape[0]
     lane = lax.broadcasted_iota(jnp.int32, (8, LANES), 1) - lax.broadcasted_iota(jnp.int32, (8, LANES), 0)
-    for j in range(patch_cols):
+    n_here = len(cols)
+    for at_j, j in enumerate(cols):
         p = i * patch_cols + j
         left = []
         for dx in range(3):
@@ -245,22 +250,23 @@
             ]
             even, odd = sum(lines[2::2], lines[0]), sum(lines[3::2], lines[1])
             for dy in range(3):
-                at = ((dy * 3 + dx) * patch_cols + j) * 8
+                at = ((dy * 3 + dx) * n_here + at_j) * 8
                 acc[at : at + 8, :] = jnp.where(place == (dy - 1) % 16, even, 0.0) + jnp.where(
                     place == (dy + 7) % 16, odd, 0.0
                 )
-    total = acc[pl.ds(0, 9 * patch_cols, stride=8), :]
+    total = acc[pl.ds(0, 9 * n_here, stride=8), :]
     for s in range(1, 8):
-        total = total + acc[pl.ds(s, 9 * patch_cols, stride=8), :]
+        total = total + acc[pl.ds(s, 9 * n_here, stride=8), :]
     weights = jnp.maximum(jnp.sum(total, axis=1, keepdims=True) * (1.0 / PATCH), 0.0)
-    w = [weights[k * patch_cols : (k + 1) * patch_cols] for k in range(9)]
+    w = [weights[k * n_here : (k + 1) * n_here] for k in range(9)]
     scale = 1.0 / jnp.maximum(sum(w), 1.0)
     moves = (
         (w[6] + w[7] + w[8] - w[0] - w[1] - w[2]) * scale,
         (w[2] + w[5] + w[8] - w[0] - w[3] - w[6]) * scale,
     )
-    here = pl.ds(pl.multiple_of(i * patch_cols, patch_cols), patch_cols)
-    return [jnp.sum((moves[c] + peak[c, here, :]) * smooth[...], axis=0, keepdims=True) for c in range(2)]
+    here = pl.ds(pl.multiple_of(i * patch_cols + cols[0], 8), n_here)
+    share = smooth[cols[0] : cols[0] + n_here, :]
+    return [jnp.sum((moves[c] + peak[c, here, :]) * share, axis=0, keepdims=True) for c in range(2)]
 
 
 def put_lines(lines, i, patch_rows):
@@ -268,15 +274,18 @@
     return sum(jnp.where(at == c * patch_rows + i, line, 0.0) for c, line in enumerate(lines))
 
 
-def waiting_kernel(n_ty, swaps, peaks, mid, first, second, turned_mid, turned_first, boundary, smooth, _, *rest):
-    rendered, turned_second, bands, peak, row_weights, flow, acc, whole, sems = rest
-    n_rows = boundary.shape[0]
+def waiting_kernel(n_ty, swaps, peaks, mid, first, *rest):
+    seconds, rest = rest[:EDGE_PARTS], rest[EDGE_PARTS:]
+    turned_mid, turned_first, boundary, smooth, _ = rest[:5]
+    rendered, turned_second, bands, peak, row_weights, flow, acc, whole, sems = rest[5:]
+    n_rows, n_cols = boundary.shape
     patch_rows = n_rows // PATCH
-    moves = [(mid, pl.ds(MARGIN, mid.shape[0]))]
-    for edge, which in ((first, False), (second, True)):
+    moves = [(mid, pl.ds(MARGIN, mid.shape[0]), pl.ds(0, n_cols))]
+    wide = n_cols // EDGE_PARTS
+    for edge, which, start in [(first, False, 0)] + [(e, True, k * wide) for k, e in enumerate(seconds)]:
         at = pl.multiple_of(jnp.where(takes_bottom(which), n_rows - MARGIN, 0), MARGIN)
-        moves.append((edge, pl.ds(at, MARGIN)))
-    copies = [pltpu.make_async_copy(a, rendered.at[b, :], sems.at[k]) for k, (a, b) in enumerate(moves)]
+        moves.append((edge, pl.ds(at, MARGIN), pl.ds(start, edge.shape[1])))
+    copies = [pltpu.make_async_copy(a, rendered.at[b, c], sems.at[k]) for k, (a, b, c) in enumerate(moves)]
     fetch = pltpu.make_async_copy(boundary, whole, sems.at[len(moves)])
     has_boundary = lax.axis_index("gz") == 0
 
@@ -287,7 +296,8 @@
     for copy in copies:
         copy.start()
     flow[...] = jnp.zeros_like(flow)
-    turn_patches(peaks, edge_patch_row(True, patch_rows), slice(None), second, turned_second, 0)
+    for k, edge in enumerate(seconds):
+        turn_patches(peaks, edge_patch_row(True, patch_rows), slice(None), edge, turned_second, k * (wide // PATCH))
     plan_windows(peaks, bands, peak)
     fill_row_weights(n_ty, swaps, patch_rows, row_weights)
 
@@ -307,7 +317,7 @@
 
             def flow_with(turned_edge):
                 flow[...] += put_lines(
-                    patch_row_flow(i, turned_edge, turned_mid, bands, peak, smooth, old_of, acc), i, patch_rows
+                    patch_row_flow(i, range(n_cols // PATCH), turned_edge, turned_mid, bands, peak, smooth, old_of, acc), i, patch_rows
                 )
 
             @pl.when(k == 0)
@@ -322,7 +332,7 @@
         copy.wait()
 
 
-def window_kernel(second, turned_mid, turned_edge, bands, peak, old_mid, old_edge, smooth, before, out_ref, acc):
+def window_kernel(second, cols, turned_mid, turned_edge, bands, peak, old_mid, old_edge, smooth, before, out_ref, acc):
     patch_rows = old_mid.shape[0] // MARGIN
     out_ref[...] = before[...]
 
@@ -332,10 +342,11 @@
         at_mid = pl.multiple_of(i * MARGIN, MARGIN)
 
         def old_of(j):
-            cols = slice(j * PATCH, (j + 1) * PATCH)
-            return jnp.concatenate([old_edge[:, cols], old_mid[pl.ds(at_mid, MARGIN), cols]], axis=0)
-
-        lines = patch_row_flow(i, turned_edge, turned_mid, bands, peak, smooth, old_of, acc)
+            here = slice((j - cols[0]) * PATCH, (j - cols[0] + 1) * PATCH)
+            there = slice(j * PATCH, (j + 1) * PATCH)
+            return jnp.concatenate([old_edge[:, here], old_mid[pl.ds(at_mid, MARGIN), there]], axis=0)
+
+        lines = patch_row_flow(i, cols, turned_edge, turned_mid, bands, peak, smooth, old_of, acc)
         out_ref[...] = before[...] + put_lines(lines, i, patch_rows)
 
 
@@ -434,12 +445,10 @@
     shape = jax.ShapeDtypeStruct
     to_next = [(i, (i + 1) % n_gz) for i in range(n_gz)]
 
-    swaps, routes = [], []
-    for d in range(-(-2 * SMOOTH_PASSES // patch_rows), 0, -1):
-        for other in (False, True):
-            if has_partners(n_ty, d, other):
-                swaps.append((d, other))
-                routes.append(swap_table(n_gz, n_ty, d, other))
+    reach = -(-2 * SMOOTH_PASSES // patch_rows)
+    steps = [(1, False)] + [(d, other) for d in range(reach, 1, -1) for other in (False, True)] + [(1, True)]
+    swaps = [step for step in steps if has_partners(n_ty, *step)]
+    routes = [swap_table(n_gz, n_ty, *step) for step in swaps]
 
     early = max(1, min(n_blocks - 1, int(n_blocks * EARLY_BLOCKS)))
     window = BLOCK + 2 * LANES
@@ -486,17 +495,17 @@
         held, turned_mid
     )
     second = lax.ppermute(send_second, ("parts", "gz", "ty"), halo_table(n_parts, n_gz, n_ty, True))
-    def render_edges(which, *args):
+    def render_edges(which, parts, *args):
         return call(
-            functools.partial(edges_kernel, which),
-            shape((MARGIN, n_cols), bf16),
+            functools.partial(edges_kernel, which, parts),
+            [shape((MARGIN, n_cols // parts), bf16)] * parts,
             [vmem] * 5 + [unread] * (len(args) - 5),
-            vmem,
+            [vmem] * parts,
             [pltpu.VMEM((MARGIN, n_cols + 2 * LANES), bf16)],
         )(*args)
 
     turned_shape = shape((3 * patch_cols, MARGIN, LANES), bf16)
-    first_edge = render_edges(False, first, held, first_table, tables, more_tables, send_second)
+    (first_edge,) = render_edges(False, 1, first, held, first_table, tables, more_tables, send_second)
     old_first = lax.ppermute(first_edge, "gz", to_next)
     turned_first = call(
         functools.partial(turn_first_kernel, patch_rows),
@@ -506,8 +515,9 @@
         flops=500_000_000,
         moved=1_000_000,
     )(peak_shift, first_edge)
-    second_edge = render_edges(True, second, held, second_table, tables, more_tables, turned_first)
-    old_second = lax.ppermute(second_edge, "gz", to_next)
+    second_edges = render_edges(True, EDGE_PARTS, second, held, second_table, tables, more_tables, turned_first)
+    part_cols = patch_cols // EDGE_PARTS
+    old_seconds = [lax.ppermute(e, "gz", to_next) for e in second_edges]
     smooth = jnp.asarray(column_smoother(patch_cols))
     acc = pltpu.VMEM((9 * patch_cols * 8, LANES), f32)
     terms = (len(swaps) + 1) * 2 * patch_rows
@@ -521,15 +531,18 @@
             shape((terms, 8, LANES), f32),
             shape((8, LANES), f32),
         ),
-        [smem] + [vmem] * 5 + [hbm, vmem, unread],
+        [smem] + [vmem] * (4 + EDGE_PARTS) + [hbm, vmem, unread],
         [hbm] + [vmem] * 5,
-        [acc, pltpu.VMEM((n_rows, n_cols), bf16), pltpu.SemaphoreType.DMA((4,))],
+        [acc, pltpu.VMEM((n_rows, n_cols), bf16), pltpu.SemaphoreType.DMA((3 + EDGE_PARTS,))],
         flops=1_000_000_000,
         moved=3_000_000,
-    )(peak_shift, mid, first_edge, second_edge, turned_mid, turned_first, in_hbm(boundary), smooth, old_mid)
-    for which, turned, old in ((True, turned_second, old_first), (False, turned_first, old_second)):
+    )(peak_shift, mid, first_edge, *second_edges, turned_mid, turned_first, in_hbm(boundary), smooth, old_mid)
+    windows = [(True, range(patch_cols), turned_second, old_first)]
+    for k, old in enumerate(old_seconds):
+        windows.append((False, range(k * part_cols, (k + 1) * part_cols), turned_first, old))
+    for which, cols, turned, old in windows:
         payload = call(
-            functools.partial(window_kernel, which), shape((8, LANES), f32), [vmem] * 8, vmem, [acc]
+            functools.partial(window_kernel, which, cols), shape((8, LANES), f32), [vmem] * 8, vmem, [acc]
         )(turned_mid, turned, bands, peak, old_mid, old, smooth, payload)
     blocks = [payload] + [lax.ppermute(payload, ("gz", "ty"), route) for route in routes]
     flow = call(

time: 27.4 us -> 26.8 us (0.978); the launches traced: 27.2 us -> 26.3 us
  waiting for transfers between devices: 7.23 us -> 5.63 us
  starting transfers between devices: 9.08 us -> 9.94 us
    ppermute x1 -> x2, waiting for transfers between devices: 1.27 us -> 0.38 us  [local(): old_seconds = [lax.ppermute(e, 'gz', to_next) for e in second_edges]]
    ppermute x1 -> x2, starting transfers between devices: 0.78 us -> 1.66 us  [local(): old_seconds = [lax.ppermute(e, 'gz', to_next) for e in second_edges]]
    ppermute x3, waiting for transfers between devices: 2.7 us -> 1.99 us  [local(): lax.ppermute(payload, ('gz', 'ty'), route)]
    pallas_call x4 -> x5, Pallas kernels: 1.33 us -> 1.34 us  [the longest x2 1.3 us: render_edges(): call(functools.partial(edges_kernel, which, parts), [shape((MARGIN, n_col...]
  transfers between devices with their start and end apart: 8 -> 9, of which waited for: 5 -> 5; matrix products, arithmetic and copies ran while one was open for 0% -> 0% of each run, Pallas kernels for 30% -> 30%
where the time goes in v6:
time: 26.8 us; the launch traced here: 26.3 us
  Pallas kernels  9.95 us (37%)
  starting transfers between devices  9.94 us (37%)
  waiting for transfers between devices  5.63 us (21%)
  between operations  0.76 us (3%)
    pallas_call x1, Pallas kernels, local(): call(functools.partial(waiting_kernel, n_ty, tuple(swaps)), (shape((n_row...  3.87 us
    ppermute x3, starting transfers between devices, local(): lax.ppermute(payload, ('gz', 'ty'), route)  3.49 us
    ppermute x1, starting transfers between devices, local(): lax.ppermute(send_first, ('parts', 'gz', 'ty'), halo_table(n_parts, n_gz,...  3.09 us
    ppermute x1, waiting for transfers between devices, local(): lax.ppermute(send_second, ('parts', 'gz', 'ty'), halo_table(n_parts, n_gz...  2.43 us
    ppermute x3, waiting for transfers between devices, local(): lax.ppermute(payload, ('gz', 'ty'), route)  1.99 us
    ppermute x2, starting transfers between devices, local(): old_seconds = [lax.ppermute(e, 'gz', to_next) for e in second_edges]  1.66 us
    ppermute x1, starting transfers between devices, local(): lax.ppermute(send_second, ('parts', 'gz', 'ty'), halo_table(n_parts, n_gz...  1.58 us
    pallas_call x1, Pallas kernels, local(): call(functools.partial(fetch_kernel, all_rows), (shape((MARGIN, n_cols),...  1.43 us
  transfers between devices with their start and end apart: 9, of which 5 were waited for; matrix products, arithmetic and copies ran while one was open for 0% of the time, Pallas kernels for 30%

profile of v6, /device:TPU:0, one launch (start us, length us, event | category | flops | bytes accessed | tf_op | source)
XLA Modules:
  0.0 26.3 jit_solution(1263526359761456494)
XLA Ops:
  0.6 0.0 copy-start.1
  0.6 1.4 %shard_map.95 = (bf16[64,2048]{1,0:T(8,128)(2,1)S(1)}, bf16[256,2048]{1,0:T(8,128)(2,1)S(1)}, f32[1,256]{1,0:T(1,128)S(1)}, f32[1,2048]{1,0:T(1,128)S(1)}, bf16[7,512,256]{2,1,0:T(8,128)(2,1)S(1)}) custom-call(bf16[256,2048]{1,0:T(8,128)(2,1)} %bitcast.2, s32[1,256]{1,0:T(1,128)} %row_shift.1, s32[1,256]{1,0:T(1,128)} %row_frac.1, s32[1,2048]{1,0:T(1,128)} %col_shift.1, ...), custom_call_target="tpu_custom_call" | custom-call | tf_op jit(solution)/shard_map/pallas_call | solution.py:455
  2.1 3.1 %collective-permute-start = (bf16[64,2048]{1,0:T(8,128)(2,1)S(1)}, bf16[64,2048]{1,0:T(8,128)(2,1)S(1)}, u32[]{:S(2)}, u32[]{:S(2)}) collective-permute-start(bf16[64,2048]{1,0:T(8,128)(2,1)S(1)} %get-tuple-element.24), channel_id=1, source_target_pairs={{0,1},{1,0},{2,3},{3,2},{4,20},{5,6},{6,5},{7,23},{8,9},{9,8},{10,... | collective-permute-start | bytes 786440 | tf_op jit(solution)/shard_map/ppermute | solution.py:474
  5.2 0.8 %shard_map.96 = (bf16[128,2048]{1,0:T(8,128)(2,1)S(1)}, bf16[1,512,256]{2,1,0:T(8,128)(2,1)S(1)}, bf16[64,192]{1,0:T(8,128)(2,1)S(1)}, bf16[64,192]{1,0:T(8,128)(2,1)S(1)}) custom-call(bf16[256,2048]{1,0:T(8,128)(2,1)S(1)} %get-tuple-element.19.held, f32[1,256]{1,0:T(1,128)S(1)} %get-tuple-element.20.row_pos, f32[1,2048]{1,0:T(1,128)S(1)} %get-tuple-element.21.col_pos, ...), custom_call_target="tpu_custom_call" | custom-call | tf_op jit(solution)/shard_map/pallas_call | solution.py:477
  5.9 0.1 collective-permute-start.2
  6.0 0.0 copy-done.1
  6.0 1.0 %shard_map.97._.rest_2_.turned_mid = bf16[96,64,128]{2,1,0:T(8,128)(2,1)S(1)} custom-call(s32[2,1,2,16]{3,2,1,0:T(2,128)S(1)} %copy-done.1, bf16[128,2048]{1,0:T(8,128)(2,1)S(1)} %get-tuple-element.23.mid), custom_call_target="tpu_custom_call" | custom-call | flops 1000000000 | bytes 3000000 | tf_op jit(solution)/shard_map/pallas_call | solution.py:485
  7.1 1.6 %collective-permute-start.1 = (bf16[64,2048]{1,0:T(8,128)(2,1)S(1)}, bf16[64,2048]{1,0:T(8,128)(2,1)S(1)}, u32[]{:S(2)}, u32[]{:S(2)}) collective-permute-start(bf16[64,2048]{1,0:T(8,128)(2,1)S(1)} %shard_map.98.rest_0_), channel_id=1, source_target_pairs={{0,16},{1,2},{2,1},{3,19},{4,5},{5,4},{6,7},{7,6},{8,24},{9,10},{1... | collective-permute-start | bytes 786440 | tf_op jit(solution)/shard_map/ppermute | solution.py:497
  8.7 0.8 %collective-permute-done.halo = bf16[64,2048]{1,0:T(8,128)(2,1)S(1)} collective-permute-done((bf16[64,2048]{1,0:T(8,128)(2,1)S(1)}, bf16[64,2048]{1,0:T(8,128)(2,1)S(1)}, u32[]{:S(2)}, u32[]{:S(2)}) %collective-permute-start) | collective-permute-done | bytes 262176 | tf_op jit(solution)/shard_map/ppermute | solution.py:474
  9.5 0.7 %shard_map.99.edge.first = bf16[64,2048]{1,0:T(8,128)(2,1)S(1)} custom-call(bf16[64,2048]{1,0:T(8,128)(2,1)S(1)} %collective-permute-done.halo, bf16[256,2048]{1,0:T(8,128)(2,1)S(1)} %get-tuple-element.19.held, bf16[64,192]{1,0:T(8,128)(2,1)S(1)} %get-tuple-element.25.table, bf16[7,512,256]{2,1,0:T(8,128)(2,1)S(1)} %get-tuple-element.22.tables, ...), custom_call_target="tpu_custom_call" | custom-call | tf_op jit(solution)/shard_map/pallas_call | solution.py:499
  10.2 0.1 collective-permute-start.5
  10.2 0.9 %shard_map.100.rest_0_.rest_3_.turned_edge = bf16[48,64,128]{2,1,0:T(8,128)(2,1)S(1)} custom-call(s32[2,1,2,16]{3,2,1,0:T(2,128)S(1)} %copy-done.1, bf16[64,2048]{1,0:T(8,128)(2,1)S(1)} %shard_map.99.edge.first), custom_call_target="tpu_custom_call" | custom-call | flops 500000000 | bytes 1000000 | tf_op jit(solution)/shard_map/pallas_call | solution.py:510
  11.1 2.4 %collective-permute-done.1.halo = bf16[64,2048]{1,0:T(8,128)(2,1)S(1)} collective-permute-done((bf16[64,2048]{1,0:T(8,128)(2,1)S(1)}, bf16[64,2048]{1,0:T(8,128)(2,1)S(1)}, u32[]{:S(2)}, u32[]{:S(2)}) %collective-permute-start.1) | collective-permute-done | bytes 262176 | tf_op jit(solution)/shard_map/ppermute | solution.py:497
  13.5 0.0 copy-start
  13.5 0.7 %shard_map.101 = (bf16[64,1024]{1,0:T(8,128)(2,1)S(1)}, bf16[64,1024]{1,0:T(8,128)(2,1)S(1)}) custom-call(bf16[64,2048]{1,0:T(8,128)(2,1)S(1)} %collective-permute-done.1.halo, bf16[256,2048]{1,0:T(8,128)(2,1)S(1)} %get-tuple-element.19.held, bf16[64,192]{1,0:T(8,128)(2,1)S(1)} %get-tuple-element.27.table, ...), custom_call_target="tpu_custom_call" | custom-call | tf_op jit(solution)/shard_map/pallas_call | solution.py:499
  14.2 0.8 %collective-permute-start.4 = (bf16[64,1024]{1,0:T(8,128)(2,1)S(1)}, bf16[64,1024]{1,0:T(8,128)(2,1)S(1)}, u32[]{:S(2)}, u32[]{:S(2)}) collective-permute-start(bf16[64,1024]{1,0:T(8,128)(2,1)S(1)} %get-tuple-element.28.rest_0_), channel_id=1, source_target_pairs={{0,4},{4,8},{8,12},{12,0},{1,5},{5,9},{9,13},{13,1},{2,6},{6,10},{... | collective-permute-start | bytes 393224 | tf_op jit(solution)/shard_map/ppermute | solution.py:520
  15.0 0.9 %collective-permute-start.3 = (bf16[64,1024]{1,0:T(8,128)(2,1)S(1)}, bf16[64,1024]{1,0:T(8,128)(2,1)S(1)}, u32[]{:S(2)}, u32[]{:S(2)}) collective-permute-start(bf16[64,1024]{1,0:T(8,128)(2,1)S(1)} %get-tuple-element.29.rest_1_), channel_id=1, source_target_pairs={{0,4},{4,8},{8,12},{12,0},{1,5},{5,9},{9,13},{13,1},{2,6},{6,10},{... | collective-permute-start | bytes 393224 | tf_op jit(solution)/shard_map/ppermute | solution.py:520
  15.9 0.0 collective-permute-done.2.rest_6_.old_mid
  15.9 0.0 copy-done
  15.9 3.9 %shard_map.102 = (bf16[256,2048]{1,0:T(8,128)(2,1)}, bf16[48,64,128]{2,1,0:T(8,128)(2,1)S(1)}, f32[32,16,128]{2,1,0:T(8,128)S(1)}, f32[2,32,128]{2,1,0:T(8,128)S...) custom-call(s32[2,1,2,16]{3,2,1,0:T(2,128)S(1)} %copy-done.1, bf16[128,2048]{1,0:T(8,128)(2,1)S(1)} %get-tuple-element.23.mid, ...), custom_call_target="tpu_custom_call" | custom-call | flops 1000000000 | bytes 3000000 | tf_op jit(solution)/shard_map/pallas_call | solution.py:524
  19.8 0.0 collective-permute-done.5.old_edge
  19.8 0.0 collective-permute-done.4.old_edge
  19.8 0.4 %collective-permute-done.3.old_edge = bf16[64,1024]{1,0:T(8,128)(2,1)S(1)} collective-permute-done((bf16[64,1024]{1,0:T(8,128)(2,1)S(1)}, bf16[64,1024]{1,0:T(8,128)(2,1)S(1)}, u32[]{:S(2)}, u32[]{:S(2)}) %collective-permute-start.3) | collective-permute-done | bytes 131104 | tf_op jit(solution)/shard_map/ppermute | solution.py:520
  20.2 1.0 %collective-permute-start.6 = (f32[8,128]{1,0:T(8,128)S(1)}, f32[8,128]{1,0:T(8,128)S(1)}, u32[]{:S(2)}, u32[]{:S(2)}) collective-permute-start(f32[8,128]{1,0:T(8,128)S(1)} %shard_map.105.refs_0_), channel_id=1, source_target_pairs={{0,1},{1,0},{2,3},{3,2},{4,5},{5,4},{6,7},{7,6},{8,9},{9,8},{10,11... | collective-permute-start | bytes 12296 | tf_op jit(solution)/shard_map/ppermute | solution.py:547
  21.2 2.5 %collective-permute-start.7 = (f32[8,128]{1,0:T(8,128)S(1)}, f32[8,128]{1,0:T(8,128)S(1)}, u32[]{:S(2)}, u32[]{:S(2)}) collective-permute-start(f32[8,128]{1,0:T(8,128)S(1)} %shard_map.105.refs_0_), channel_id=1, source_target_pairs={{0,2},{1,3},{2,0},{3,1},{4,6},{5,7},{6,4},{7,5},{8,10},{9,11},{10,... | collective-permute-start | bytes 12296 | tf_op jit(solution)/shard_map/ppermute | solution.py:547
  23.7 0.0 collective-permute-start.8
  23.7 0.1 collective-permute-done.6.refs_1_
  23.8 1.9 %collective-permute-done.7.refs_2_ = f32[8,128]{1,0:T(8,128)S(1)} collective-permute-done((f32[8,128]{1,0:T(8,128)S(1)}, f32[8,128]{1,0:T(8,128)S(1)}, u32[]{:S(2)}, u32[]{:S(2)}) %collective-permute-start.7) | collective-permute-done | bytes 4128 | tf_op jit(solution)/shard_map/ppermute | solution.py:547
  25.7 0.0 collective-permute-done.8.refs_3_
  25.7 0.6 %shard_map.106 = f32[2,1,2,16]{3,2,1,0:T(2,128)} custom-call(f32[16,8,128]{2,1,0:T(8,128)S(1)} %get-tuple-element.31.row_weights, f32[8,128]{1,0:T(8,128)S(1)} %shard_map.105.refs_0_, f32[8,128]{1,0:T(8,128)S(1)} %collective-permute-done.6.refs_1_, f32[8,128]{1,0:T(8,128)S(1)} %collective-permute-done.7.refs_2_, f32[8,128]{1,0:T(8,128)S(1)} %collective-permute-done.8.refs_3_), custom_call_target="tpu_custom_call" | custom-call | tf_op jit(solution)/shard_map/pallas_call | solution.py:548
  (4 shorter events, 0.1 us)
Async XLA Ops:
  0.6 5.4 %copy-start.1 = (s32[2,1,2,16]{3,2,1,0:T(2,128)S(1)}, s32[2,1,2,16]{3,2,1,0:T(2,128)}, u32[]{:S(2)}) copy-start(s32[2,1,2,16]{3,2,1,0:T(2,128)} %peaks.5) | copy-start | bytes 772
  2.1 7.4 %collective-permute-start = (bf16[64,2048]{1,0:T(8,128)(2,1)S(1)}, bf16[64,2048]{1,0:T(8,128)(2,1)S(1)}, u32[]{:S(2)}, u32[]{:S(2)}) collective-permute-start(bf16[64,2048]{1,0:T(8,128)(2,1)S(1)} %get-tuple-element.24), channel_id=1, source_target_pairs={{0,1},{1,0},{2,3},{3,2},{4,20},{5,6},{6,5},{7,23},{8,9},{9,8},{10,... | collective-permute-start | bytes 786440 | tf_op jit(solution)/shard_map/ppermute | solution.py:474
  5.9 9.9 %collective-permute-start.2 = (bf16[128,2048]{1,0:T(8,128)(2,1)S(1)}, bf16[128,2048]{1,0:T(8,128)(2,1)S(1)}, u32[]{:S(2)}, u32[]{:S(2)}) collective-permute-start(bf16[128,2048]{1,0:T(8,128)(2,1)S(1)} %get-tuple-element.23.mid), channel_id=1, source_target_pairs={{0,4},{4,8},{8,12},{12,0},{1,5},{5,9},{9,13},{13,1},{2,6},{6,10},{... | collective-permute-start | bytes 1572872 | tf_op jit(solution)/shard_map/ppermute | solution.py:484
  7.1 6.4 %collective-permute-start.1 = (bf16[64,2048]{1,0:T(8,128)(2,1)S(1)}, bf16[64,2048]{1,0:T(8,128)(2,1)S(1)}, u32[]{:S(2)}, u32[]{:S(2)}) collective-permute-start(bf16[64,2048]{1,0:T(8,128)(2,1)S(1)} %shard_map.98.rest_0_), channel_id=1, source_target_pairs={{0,16},{1,2},{2,1},{3,19},{4,5},{5,4},{6,7},{7,6},{8,24},{9,10},{1... | collective-permute-start | bytes 786440 | tf_op jit(solution)/shard_map/ppermute | solution.py:497
  10.2 9.6 %collective-permute-start.5 = (bf16[64,2048]{1,0:T(8,128)(2,1)S(1)}, bf16[64,2048]{1,0:T(8,128)(2,1)S(1)}, u32[]{:S(2)}, u32[]{:S(2)}) collective-permute-start(bf16[64,2048]{1,0:T(8,128)(2,1)S(1)} %shard_map.99.edge.first), channel_id=1, source_target_pairs={{0,4},{4,8},{8,12},{12,0},{1,5},{5,9},{9,13},{13,1},{2,6},{6,10},{... | collective-permute-start | bytes 786440 | tf_op jit(solution)/shard_map/ppermute | solution.py:509
  13.5 2.3 %copy-start = (f32[16,128]{1,0:T(8,128)S(1)}, f32[16,128]{1,0:T(8,128)}, u32[]{:S(2)}) copy-start(f32[16,128]{1,0:T(8,128)} %constant.2.clone.rest_5_.smooth) | copy-start | bytes 24580
  14.2 5.6 %collective-permute-start.4 = (bf16[64,1024]{1,0:T(8,128)(2,1)S(1)}, bf16[64,1024]{1,0:T(8,128)(2,1)S(1)}, u32[]{:S(2)}, u32[]{:S(2)}) collective-permute-start(bf16[64,1024]{1,0:T(8,128)(2,1)S(1)} %get-tuple-element.28.rest_0_), channel_id=1, source_target_pairs={{0,4},{4,8},{8,12},{12,0},{1,5},{5,9},{9,13},{13,1},{2,6},{6,10},{... | collective-permute-start | bytes 393224 | tf_op jit(solution)/shard_map/ppermute | solution.py:520
  15.0 5.2 %collective-permute-start.3 = (bf16[64,1024]{1,0:T(8,128)(2,1)S(1)}, bf16[64,1024]{1,0:T(8,128)(2,1)S(1)}, u32[]{:S(2)}, u32[]{:S(2)}) collective-permute-start(bf16[64,1024]{1,0:T(8,128)(2,1)S(1)} %get-tuple-element.29.rest_1_), channel_id=1, source_target_pairs={{0,4},{4,8},{8,12},{12,0},{1,5},{5,9},{9,13},{13,1},{2,6},{6,10},{... | collective-permute-start | bytes 393224 | tf_op jit(solution)/shard_map/ppermute | solution.py:520
  20.2 3.6 %collective-permute-start.6 = (f32[8,128]{1,0:T(8,128)S(1)}, f32[8,128]{1,0:T(8,128)S(1)}, u32[]{:S(2)}, u32[]{:S(2)}) collective-permute-start(f32[8,128]{1,0:T(8,128)S(1)} %shard_map.105.refs_0_), channel_id=1, source_target_pairs={{0,1},{1,0},{2,3},{3,2},{4,5},{5,4},{6,7},{7,6},{8,9},{9,8},{10,11... | collective-permute-start | bytes 12296 | tf_op jit(solution)/shard_map/ppermute | solution.py:547
  21.2 4.5 %collective-permute-start.7 = (f32[8,128]{1,0:T(8,128)S(1)}, f32[8,128]{1,0:T(8,128)S(1)}, u32[]{:S(2)}, u32[]{:S(2)}) collective-permute-start(f32[8,128]{1,0:T(8,128)S(1)} %shard_map.105.refs_0_), channel_id=1, source_target_pairs={{0,2},{1,3},{2,0},{3,1},{4,6},{5,7},{6,4},{7,5},{8,10},{9,11},{10,... | collective-permute-start | bytes 12296 | tf_op jit(solution)/shard_map/ppermute | solution.py:547
  23.7 2.0 %collective-permute-start.8 = (f32[8,128]{1,0:T(8,128)S(1)}, f32[8,128]{1,0:T(8,128)S(1)}, u32[]{:S(2)}, u32[]{:S(2)}) collective-permute-start(f32[8,128]{1,0:T(8,128)S(1)} %shard_map.105.refs_0_), channel_id=1, source_target_pairs={{0,4},{1,2},{2,1},{3,7},{4,0},{5,6},{6,5},{7,3},{8,12},{9,10},{10,... | collective-permute-start | bytes 12296 | tf_op jit(solution)/shard_map/ppermute | solution.py:547

commit v7 on v6

--- a/solution.py
+++ b/solution.py
@@ -18,16 +18,17 @@
 VMEM_LIMIT = 16 * 1024 * 1024
 TURN_UNROLL = 16
 PLAN_UNROLL = 8
-EARLY_BLOCKS = 7 / 8
+EARLY_BLOCKS = 3 / 8
 EDGE_PARTS = 2
 
 f32 = jnp.float32
 bf16 = jnp.bfloat16
 
 
-def swap_table(n_gz, n_ty, d, second):
+def swap_table(n_gz, n_ty, steps):
     table = []
     for z in range(n_gz):
+        d, second = steps[z // 2 % 2]
         for t in range(n_ty):
             partner = t + d if ((t // d) % 2 == 0) != second else t - d
             if 0 <= partner < n_ty:
@@ -94,8 +95,8 @@
 
 
 def fetch_kernel(all_rows, section, row_shift, row_frac, col_shift, col_frac, *rest):
-    send_first, held, row_pos, col_pos, tables = rest[:5]
-    row_shift_v, row_frac_v, col_shift_v, col_frac_v, sems = rest[5:]
+    send_first, row_pos, col_pos, tables = rest[:4]
+    row_shift_v, row_frac_v, col_shift_v, col_frac_v, sems = rest[4:]
     n_rows, n_cols = section.shape
     base = lax.axis_index("ty") * n_rows
     at = pl.multiple_of(jnp.where(takes_bottom(False), n_rows - MARGIN, 0), MARGIN)
@@ -108,7 +109,6 @@
                 (row_shift, row_shift_v),
                 (row_frac, row_frac_v),
                 (section.at[pl.ds(at, MARGIN), :], send_first),
-                (section, held),
             )
         )
     ]
@@ -358,8 +358,10 @@
     at = lax.broadcasted_iota(jnp.int32, (8, depth), 0)
     slot = lax.broadcasted_iota(jnp.int32, (8, depth), 1)
     holder = jnp.full((8, depth), tile, jnp.int32)
-    for k, (d, second) in enumerate(swaps):
-        holder = jnp.where((slot >> 3) == k + 1, partner_of(tile, d, second), holder)
+    even_chip = (lax.axis_index("gz") // 2) % 2 == 0
+    for k, (step, other) in enumerate(swaps):
+        partner = jnp.where(even_chip, partner_of(tile, *step), partner_of(tile, *other))
+        holder = jnp.where((slot >> 3) == k + 1, partner, holder)
     inner = slot & 7
     c_out = (at >= patch_rows).astype(jnp.int32)
     c_in = (inner >= patch_rows).astype(jnp.int32)
@@ -446,30 +448,33 @@
     to_next = [(i, (i + 1) % n_gz) for i in range(n_gz)]
 
     reach = -(-2 * SMOOTH_PASSES // patch_rows)
-    steps = [(1, False)] + [(d, other) for d in range(reach, 1, -1) for other in (False, True)] + [(1, True)]
-    swaps = [step for step in steps if has_partners(n_ty, *step)]
-    routes = [swap_table(n_gz, n_ty, *step) for step in swaps]
+    far = [(d, other) for d in range(reach, 1, -1) for other in (False, True)]
+    swaps = list(zip([(1, False), *far, (1, True)], [(1, True), *far, (1, False)]))
+    swaps = [steps for steps in swaps if any(has_partners(n_ty, *step) for step in steps)]
+    routes = [swap_table(n_gz, n_ty, steps) for steps in swaps]
 
     early = max(1, min(n_blocks - 1, int(n_blocks * EARLY_BLOCKS)))
     window = BLOCK + 2 * LANES
-    send_first, held, row_pos, col_pos, tables = call(
+    held = section
+    send_first, row_pos, col_pos, tables = call(
         functools.partial(fetch_kernel, all_rows),
         (
             shape((MARGIN, n_cols), bf16),
-            shape((n_rows, n_cols), bf16),
             shape((1, n_rows), f32),
             shape((1, n_cols), f32),
             shape((early, window, BLOCK), bf16),
         ),
         [hbm] * 5,
-        [vmem] * 5,
+        [vmem] * 4,
         [
             pltpu.VMEM((1, n_rows), jnp.int32),
             pltpu.VMEM((1, n_rows), jnp.int32),
             pltpu.VMEM((1, n_cols), jnp.int32),
             pltpu.VMEM((1, n_cols), jnp.int32),
-            pltpu.SemaphoreType.DMA((6,)),
+            pltpu.SemaphoreType.DMA((5,)),
         ],
+        flops=0,
+        moved=0,
     )(*(in_hbm(x) for x in (section, row_shift, row_frac, col_shift, col_frac)))
     first = lax.ppermute(send_first, ("parts", "gz", "ty"), halo_table(n_parts, n_gz, n_ty, False))
 

time: 26.8 us -> 26.6 us (level); the launches traced: 26.3 us -> 26.4 us
    ppermute x1, waiting for transfers between devices: 2.43 us -> 2.79 us  [local(): lax.ppermute(send_second, ('parts', 'gz', 'ty'), halo_table(n_parts, n_gz...]
    ppermute x1, waiting for transfers between devices: 0.83 us -> 0.48 us  [local(): lax.ppermute(send_first, ('parts', 'gz', 'ty'), halo_table(n_parts, n_gz,...]
    pallas_call x1, Pallas kernels: 0.76 us -> 1.11 us  [local(): call(middle_kernel, (shape((n_mid, n_cols), bf16), shape((n_blocks - earl...]
    pallas_call x1, Pallas kernels: 1.43 us -> 1.15 us  [local(): call(functools.partial(fetch_kernel, all_rows), (shape((MARGIN, n_cols),...]
  transfers between devices with their start and end apart: 9 -> 9, of which waited for: 5 -> 5; matrix products, arithmetic and copies ran while one was open for 0% -> 0% of each run, Pallas kernels for 30% -> 31%
where the time goes in v7:
time: 26.6 us; the launch traced here: 26.4 us
  Pallas kernels  10 us (38%)
  starting transfers between devices  9.92 us (37%)
  waiting for transfers between devices  5.64 us (21%)
  between operations  0.77 us (3%)
    pallas_call x1, Pallas kernels, local(): call(functools.partial(waiting_kernel, n_ty, tuple(swaps)), (shape((n_row...  3.9 us
    ppermute x3, starting transfers between devices, local(): lax.ppermute(payload, ('gz', 'ty'), route)  3.48 us
    ppermute x1, starting transfers between devices, local(): lax.ppermute(send_first, ('parts', 'gz', 'ty'), halo_table(n_parts, n_gz,...  3.09 us
    ppermute x1, waiting for transfers between devices, local(): lax.ppermute(send_second, ('parts', 'gz', 'ty'), halo_table(n_parts, n_gz...  2.79 us
    ppermute x3, waiting for transfers between devices, local(): lax.ppermute(payload, ('gz', 'ty'), route)  2 us
    ppermute x2, starting transfers between devices, local(): old_seconds = [lax.ppermute(e, 'gz', to_next) for e in second_edges]  1.65 us
    ppermute x1, starting transfers between devices, local(): lax.ppermute(send_second, ('parts', 'gz', 'ty'), halo_table(n_parts, n_gz...  1.58 us
    pallas_call x2, Pallas kernels, render_edges(): call(functools.partial(edges_kernel, which, parts), [shape((MARGIN, n_col...  1.29 us
  transfers between devices with their start and end apart: 9, of which 5 were waited for; matrix products, arithmetic and copies ran while one was open for 0% of the time, Pallas kernels for 31%

profile of v7, /device:TPU:0, one launch (start us, length us, event | category | flops | bytes accessed | tf_op | source)
XLA Modules:
  0.0 26.4 jit_solution(16655697329589213192)
XLA Ops:
  0.6 0.0 copy-start
  0.6 0.0 copy-start.2
  0.7 1.1 %shard_map.95 = (bf16[64,2048]{1,0:T(8,128)(2,1)S(1)}, f32[1,256]{1,0:T(1,128)S(1)}, f32[1,2048]{1,0:T(1,128)S(1)}, bf16[3,512,256]{2,1,0:T(8,128)(2,1)S(1)}) custom-call(bf16[256,2048]{1,0:T(8,128)(2,1)} %bitcast.2, s32[1,256]{1,0:T(1,128)} %row_shift.1, s32[1,256]{1,0:T(1,128)} %row_frac.1, s32[1,2048]{1,0:T(1,128)} %col_shift.1, s32[1,2048]{1,0:T(1,128)} %col_frac.1), custom_call_target="tpu_custom_call" | custom-call | tf_op jit(solution)/shard_map/pallas_call | solution.py:459
  1.8 3.1 %collective-permute-start = (bf16[64,2048]{1,0:T(8,128)(2,1)S(1)}, bf16[64,2048]{1,0:T(8,128)(2,1)S(1)}, u32[]{:S(2)}, u32[]{:S(2)}) collective-permute-start(bf16[64,2048]{1,0:T(8,128)(2,1)S(1)} %get-tuple-element.22), channel_id=1, source_target_pairs={{0,1},{1,0},{2,3},{3,2},{4,20},{5,6},{6,5},{7,23},{8,9},{9,8},{10,... | collective-permute-start | bytes 786440 | tf_op jit(solution)/shard_map/ppermute | solution.py:479
  4.9 0.0 copy-done
  4.9 1.1 %shard_map.96 = (bf16[128,2048]{1,0:T(8,128)(2,1)S(1)}, bf16[5,512,256]{2,1,0:T(8,128)(2,1)S(1)}, bf16[64,192]{1,0:T(8,128)(2,1)S(1)}, bf16[64,192]{1,0:T(8,128)(2,1)S(1)}) custom-call(bf16[256,2048]{1,0:T(8,128)(2,1)S(1)} %bitcast.3, f32[1,256]{1,0:T(1,128)S(1)} %get-tuple-element.18.row_pos, f32[1,2048]{1,0:T(1,128)S(1)} %get-tuple-element.19.col_pos, ...), custom_call_target="tpu_custom_call" | custom-call | tf_op jit(solution)/shard_map/pallas_call | solution.py:482
  6.0 0.1 collective-permute-start.2
  6.1 0.0 copy-done.2
  6.1 1.0 %shard_map.97._.rest_2_.turned_mid = bf16[96,64,128]{2,1,0:T(8,128)(2,1)S(1)} custom-call(s32[2,1,2,16]{3,2,1,0:T(2,128)S(1)} %copy-done.2, bf16[128,2048]{1,0:T(8,128)(2,1)S(1)} %get-tuple-element.21.mid), custom_call_target="tpu_custom_call" | custom-call | flops 1000000000 | bytes 3000000 | tf_op jit(solution)/shard_map/pallas_call | solution.py:490
  7.2 1.6 %collective-permute-start.1 = (bf16[64,2048]{1,0:T(8,128)(2,1)S(1)}, bf16[64,2048]{1,0:T(8,128)(2,1)S(1)}, u32[]{:S(2)}, u32[]{:S(2)}) collective-permute-start(bf16[64,2048]{1,0:T(8,128)(2,1)S(1)} %shard_map.98.rest_0_), channel_id=1, source_target_pairs={{0,16},{1,2},{2,1},{3,19},{4,5},{5,4},{6,7},{7,6},{8,24},{9,10},{1... | collective-permute-start | bytes 786440 | tf_op jit(solution)/shard_map/ppermute | solution.py:502
  8.8 0.5 %collective-permute-done.halo = bf16[64,2048]{1,0:T(8,128)(2,1)S(1)} collective-permute-done((bf16[64,2048]{1,0:T(8,128)(2,1)S(1)}, bf16[64,2048]{1,0:T(8,128)(2,1)S(1)}, u32[]{:S(2)}, u32[]{:S(2)}) %collective-permute-start) | collective-permute-done | bytes 262176 | tf_op jit(solution)/shard_map/ppermute | solution.py:479
  9.2 0.6 %shard_map.99.edge.first = bf16[64,2048]{1,0:T(8,128)(2,1)S(1)} custom-call(bf16[64,2048]{1,0:T(8,128)(2,1)S(1)} %collective-permute-done.halo, bf16[256,2048]{1,0:T(8,128)(2,1)S(1)} %bitcast.5, bf16[64,192]{1,0:T(8,128)(2,1)S(1)} %get-tuple-element.23.table, bf16[3,512,256]{2,1,0:T(8,128)(2,1)S(1)} %get-tuple-element.20.tables, ...), custom_call_target="tpu_custom_call" | custom-call | tf_op jit(solution)/shard_map/pallas_call | solution.py:504
  9.9 0.1 collective-permute-start.5
  10.0 0.9 %shard_map.100.rest_0_.rest_3_.turned_edge = bf16[48,64,128]{2,1,0:T(8,128)(2,1)S(1)} custom-call(s32[2,1,2,16]{3,2,1,0:T(2,128)S(1)} %copy-done.2, bf16[64,2048]{1,0:T(8,128)(2,1)S(1)} %shard_map.99.edge.first), custom_call_target="tpu_custom_call" | custom-call | flops 500000000 | bytes 1000000 | tf_op jit(solution)/shard_map/pallas_call | solution.py:515
  10.8 2.8 %collective-permute-done.1.halo = bf16[64,2048]{1,0:T(8,128)(2,1)S(1)} collective-permute-done((bf16[64,2048]{1,0:T(8,128)(2,1)S(1)}, bf16[64,2048]{1,0:T(8,128)(2,1)S(1)}, u32[]{:S(2)}, u32[]{:S(2)}) %collective-permute-start.1) | collective-permute-done | bytes 262176 | tf_op jit(solution)/shard_map/ppermute | solution.py:502
  13.6 0.0 copy-start.1
  13.6 0.6 %shard_map.101 = (bf16[64,1024]{1,0:T(8,128)(2,1)S(1)}, bf16[64,1024]{1,0:T(8,128)(2,1)S(1)}) custom-call(bf16[64,2048]{1,0:T(8,128)(2,1)S(1)} %collective-permute-done.1.halo, bf16[256,2048]{1,0:T(8,128)(2,1)S(1)} %bitcast.6, bf16[64,192]{1,0:T(8,128)(2,1)S(1)} %get-tuple-element.25.table, bf16[3,512,256]{2,1,0:T(8,128)(2,1)S(1)} %get-tuple-element.20.tables, ...), custom_call_target="tpu_custom_call" | custom-call | tf_op jit(solution)/shard_map/pallas_call | solution.py:504
  14.3 0.8 %collective-permute-start.4 = (bf16[64,1024]{1,0:T(8,128)(2,1)S(1)}, bf16[64,1024]{1,0:T(8,128)(2,1)S(1)}, u32[]{:S(2)}, u32[]{:S(2)}) collective-permute-start(bf16[64,1024]{1,0:T(8,128)(2,1)S(1)} %get-tuple-element.26.rest_0_), channel_id=1, source_target_pairs={{0,4},{4,8},{8,12},{12,0},{1,5},{5,9},{9,13},{13,1},{2,6},{6,10},{... | collective-permute-start | bytes 393224 | tf_op jit(solution)/shard_map/ppermute | solution.py:525
  15.1 0.9 %collective-permute-start.3 = (bf16[64,1024]{1,0:T(8,128)(2,1)S(1)}, bf16[64,1024]{1,0:T(8,128)(2,1)S(1)}, u32[]{:S(2)}, u32[]{:S(2)}) collective-permute-start(bf16[64,1024]{1,0:T(8,128)(2,1)S(1)} %get-tuple-element.27.rest_1_), channel_id=1, source_target_pairs={{0,4},{4,8},{8,12},{12,0},{1,5},{5,9},{9,13},{13,1},{2,6},{6,10},{... | collective-permute-start | bytes 393224 | tf_op jit(solution)/shard_map/ppermute | solution.py:525
  15.9 0.0 collective-permute-done.2.rest_6_.old_mid
  15.9 0.0 copy-done.1
  15.9 3.9 %shard_map.102 = (bf16[256,2048]{1,0:T(8,128)(2,1)}, bf16[48,64,128]{2,1,0:T(8,128)(2,1)S(1)}, f32[32,16,128]{2,1,0:T(8,128)S(1)}, f32[2,32,128]{2,1,0:T(8,128)S...) custom-call(s32[2,1,2,16]{3,2,1,0:T(2,128)S(1)} %copy-done.2, bf16[128,2048]{1,0:T(8,128)(2,1)S(1)} %get-tuple-element.21.mid, ...), custom_call_target="tpu_custom_call" | custom-call | flops 1000000000 | bytes 3000000 | tf_op jit(solution)/shard_map/pallas_call | solution.py:529
  19.8 0.0 collective-permute-done.5.old_edge
  19.9 0.0 collective-permute-done.4.old_edge
  19.9 0.4 %collective-permute-done.3.old_edge = bf16[64,1024]{1,0:T(8,128)(2,1)S(1)} collective-permute-done((bf16[64,1024]{1,0:T(8,128)(2,1)S(1)}, bf16[64,1024]{1,0:T(8,128)(2,1)S(1)}, u32[]{:S(2)}, u32[]{:S(2)}) %collective-permute-start.3) | collective-permute-done | bytes 131104 | tf_op jit(solution)/shard_map/ppermute | solution.py:525
  20.3 1.0 %collective-permute-start.6 = (f32[8,128]{1,0:T(8,128)S(1)}, f32[8,128]{1,0:T(8,128)S(1)}, u32[]{:S(2)}, u32[]{:S(2)}) collective-permute-start(f32[8,128]{1,0:T(8,128)S(1)} %shard_map.105.refs_0_), channel_id=1, source_target_pairs={{0,1},{1,0},{2,3},{3,2},{4,5},{5,4},{6,7},{7,6},{8,12},{9,10},{10,... | collective-permute-start | bytes 12296 | tf_op jit(solution)/shard_map/ppermute | solution.py:552
  21.3 2.5 %collective-permute-start.7 = (f32[8,128]{1,0:T(8,128)S(1)}, f32[8,128]{1,0:T(8,128)S(1)}, u32[]{:S(2)}, u32[]{:S(2)}) collective-permute-start(f32[8,128]{1,0:T(8,128)S(1)} %shard_map.105.refs_0_), channel_id=1, source_target_pairs={{0,2},{1,3},{2,0},{3,1},{4,6},{5,7},{6,4},{7,5},{8,10},{9,11},{10,... | collective-permute-start | bytes 12296 | tf_op jit(solution)/shard_map/ppermute | solution.py:552
  23.8 0.0 collective-permute-start.8
  23.8 0.1 collective-permute-done.6.refs_1_
  23.9 1.9 %collective-permute-done.7.refs_2_ = f32[8,128]{1,0:T(8,128)S(1)} collective-permute-done((f32[8,128]{1,0:T(8,128)S(1)}, f32[8,128]{1,0:T(8,128)S(1)}, u32[]{:S(2)}, u32[]{:S(2)}) %collective-permute-start.7) | collective-permute-done | bytes 4128 | tf_op jit(solution)/shard_map/ppermute | solution.py:552
  25.8 0.0 collective-permute-done.8.refs_3_
  25.8 0.6 %shard_map.106 = f32[2,1,2,16]{3,2,1,0:T(2,128)} custom-call(f32[16,8,128]{2,1,0:T(8,128)S(1)} %get-tuple-element.29.row_weights, f32[8,128]{1,0:T(8,128)S(1)} %shard_map.105.refs_0_, f32[8,128]{1,0:T(8,128)S(1)} %collective-permute-done.6.refs_1_, f32[8,128]{1,0:T(8,128)S(1)} %collective-permute-done.7.refs_2_, f32[8,128]{1,0:T(8,128)S(1)} %collective-permute-done.8.refs_3_), custom_call_target="tpu_custom_call" | custom-call | tf_op jit(solution)/shard_map/pallas_call | solution.py:553
  (4 shorter events, 0.1 us)
Async XLA Ops:
  0.6 4.3 %copy-start = (bf16[1,256,2048]{2,1,0:T(8,128)(2,1)S(1)}, bf16[1,256,2048]{2,1,0:T(8,128)(2,1)}, u32[]{:S(2)}) copy-start(bf16[1,256,2048]{2,1,0:T(8,128)(2,1)} %param.8) | copy-start | bytes 3145732
  0.6 5.4 %copy-start.2 = (s32[2,1,2,16]{3,2,1,0:T(2,128)S(1)}, s32[2,1,2,16]{3,2,1,0:T(2,128)}, u32[]{:S(2)}) copy-start(s32[2,1,2,16]{3,2,1,0:T(2,128)} %peaks.5) | copy-start | bytes 772
  1.8 7.4 %collective-permute-start = (bf16[64,2048]{1,0:T(8,128)(2,1)S(1)}, bf16[64,2048]{1,0:T(8,128)(2,1)S(1)}, u32[]{:S(2)}, u32[]{:S(2)}) collective-permute-start(bf16[64,2048]{1,0:T(8,128)(2,1)S(1)} %get-tuple-element.22), channel_id=1, source_target_pairs={{0,1},{1,0},{2,3},{3,2},{4,20},{5,6},{6,5},{7,23},{8,9},{9,8},{10,... | collective-permute-start | bytes 786440 | tf_op jit(solution)/shard_map/ppermute | solution.py:479
  6.0 9.9 %collective-permute-start.2 = (bf16[128,2048]{1,0:T(8,128)(2,1)S(1)}, bf16[128,2048]{1,0:T(8,128)(2,1)S(1)}, u32[]{:S(2)}, u32[]{:S(2)}) collective-permute-start(bf16[128,2048]{1,0:T(8,128)(2,1)S(1)} %get-tuple-element.21.mid), channel_id=1, source_target_pairs={{0,4},{4,8},{8,12},{12,0},{1,5},{5,9},{9,13},{13,1},{2,6},{6,10},{... | collective-permute-start | bytes 1572872 | tf_op jit(solution)/shard_map/ppermute | solution.py:489
  7.2 6.4 %collective-permute-start.1 = (bf16[64,2048]{1,0:T(8,128)(2,1)S(1)}, bf16[64,2048]{1,0:T(8,128)(2,1)S(1)}, u32[]{:S(2)}, u32[]{:S(2)}) collective-permute-start(bf16[64,2048]{1,0:T(8,128)(2,1)S(1)} %shard_map.98.rest_0_), channel_id=1, source_target_pairs={{0,16},{1,2},{2,1},{3,19},{4,5},{5,4},{6,7},{7,6},{8,24},{9,10},{1... | collective-permute-start | bytes 786440 | tf_op jit(solution)/shard_map/ppermute | solution.py:502
  9.9 9.9 %collective-permute-start.5 = (bf16[64,2048]{1,0:T(8,128)(2,1)S(1)}, bf16[64,2048]{1,0:T(8,128)(2,1)S(1)}, u32[]{:S(2)}, u32[]{:S(2)}) collective-permute-start(bf16[64,2048]{1,0:T(8,128)(2,1)S(1)} %shard_map.99.edge.first), channel_id=1, source_target_pairs={{0,4},{4,8},{8,12},{12,0},{1,5},{5,9},{9,13},{13,1},{2,6},{6,10},{... | collective-permute-start | bytes 786440 | tf_op jit(solution)/shard_map/ppermute | solution.py:514
  13.6 2.3 %copy-start.1 = (f32[16,128]{1,0:T(8,128)S(1)}, f32[16,128]{1,0:T(8,128)}, u32[]{:S(2)}) copy-start(f32[16,128]{1,0:T(8,128)} %constant.2.clone.rest_5_.smooth) | copy-start | bytes 24580
  14.3 5.6 %collective-permute-start.4 = (bf16[64,1024]{1,0:T(8,128)(2,1)S(1)}, bf16[64,1024]{1,0:T(8,128)(2,1)S(1)}, u32[]{:S(2)}, u32[]{:S(2)}) collective-permute-start(bf16[64,1024]{1,0:T(8,128)(2,1)S(1)} %get-tuple-element.26.rest_0_), channel_id=1, source_target_pairs={{0,4},{4,8},{8,12},{12,0},{1,5},{5,9},{9,13},{13,1},{2,6},{6,10},{... | collective-permute-start | bytes 393224 | tf_op jit(solution)/shard_map/ppermute | solution.py:525
  15.1 5.2 %collective-permute-start.3 = (bf16[64,1024]{1,0:T(8,128)(2,1)S(1)}, bf16[64,1024]{1,0:T(8,128)(2,1)S(1)}, u32[]{:S(2)}, u32[]{:S(2)}) collective-permute-start(bf16[64,1024]{1,0:T(8,128)(2,1)S(1)} %get-tuple-element.27.rest_1_), channel_id=1, source_target_pairs={{0,4},{4,8},{8,12},{12,0},{1,5},{5,9},{9,13},{13,1},{2,6},{6,10},{... | collective-permute-start | bytes 393224 | tf_op jit(solution)/shard_map/ppermute | solution.py:525
  20.3 3.6 %collective-permute-start.6 = (f32[8,128]{1,0:T(8,128)S(1)}, f32[8,128]{1,0:T(8,128)S(1)}, u32[]{:S(2)}, u32[]{:S(2)}) collective-permute-start(f32[8,128]{1,0:T(8,128)S(1)} %shard_map.105.refs_0_), channel_id=1, source_target_pairs={{0,1},{1,0},{2,3},{3,2},{4,5},{5,4},{6,7},{7,6},{8,12},{9,10},{10,... | collective-permute-start | bytes 12296 | tf_op jit(solution)/shard_map/ppermute | solution.py:552
  21.3 4.5 %collective-permute-start.7 = (f32[8,128]{1,0:T(8,128)S(1)}, f32[8,128]{1,0:T(8,128)S(1)}, u32[]{:S(2)}, u32[]{:S(2)}) collective-permute-start(f32[8,128]{1,0:T(8,128)S(1)} %shard_map.105.refs_0_), channel_id=1, source_target_pairs={{0,2},{1,3},{2,0},{3,1},{4,6},{5,7},{6,4},{7,5},{8,10},{9,11},{10,... | collective-permute-start | bytes 12296 | tf_op jit(solution)/shard_map/ppermute | solution.py:552
  23.8 2.0 %collective-permute-start.8 = (f32[8,128]{1,0:T(8,128)S(1)}, f32[8,128]{1,0:T(8,128)S(1)}, u32[]{:S(2)}, u32[]{:S(2)}) collective-permute-start(f32[8,128]{1,0:T(8,128)S(1)} %shard_map.105.refs_0_), channel_id=1, source_target_pairs={{0,4},{1,2},{2,1},{3,7},{4,0},{5,6},{6,5},{7,3},{8,9},{9,8},{10,11... | collective-permute-start | bytes 12296 | tf_op jit(solution)/shard_map/ppermute | solution.py:552

commit v8 on v7

--- a/solution.py
+++ b/solution.py
@@ -18,7 +18,7 @@
 VMEM_LIMIT = 16 * 1024 * 1024
 TURN_UNROLL = 16
 PLAN_UNROLL = 8
-EARLY_BLOCKS = 3 / 8
+EARLY_BLOCKS = 6 / 8
 EDGE_PARTS = 2
 
 f32 = jnp.float32
@@ -82,15 +82,22 @@
 
 def build_tables(col_pos, first, tables):
     reach = BLOCK + LANES
-    coord = lax.broadcasted_iota(jnp.int32, (reach, BLOCK), 0).astype(f32) - float(LANES // 2)
+    whole = (reach, BLOCK)
+    slot = lax.broadcasted_iota(jnp.int16, whole, 0)
     edge = jnp.zeros((LANES // 2, BLOCK), bf16)
 
     @pl.loop(0, tables.shape[0])
     def _(k):
         at = pl.multiple_of((first + k) * BLOCK, BLOCK)
-        pos = col_pos[:, pl.ds(at, BLOCK)] - at.astype(f32)
+        pos = col_pos[:, pl.ds(at, BLOCK)] - at.astype(f32) + float(LANES // 2)
+        low = pos.astype(jnp.int32)
+        part = pos - low.astype(f32)
+        near = jnp.broadcast_to(low, whole).astype(jnp.int16)
+        left = jnp.broadcast_to(1.0 - part, whole).astype(bf16)
+        right = jnp.broadcast_to(part, whole).astype(bf16)
+        weight = jnp.where(slot == near, left, jnp.where(slot == near + 1, right, jnp.zeros((), bf16)))
         tables[k, 0 : LANES // 2, :] = edge
-        tables[k, LANES // 2 : LANES // 2 + reach, :] = hat(coord, pos).astype(bf16)
+        tables[k, LANES // 2 : LANES // 2 + reach, :] = weight
         tables[k, LANES // 2 + reach :, :] = edge
 
 

time: 26.6 us -> 26.3 us (0.989)
  Pallas kernels: 10 us -> 9.73 us
    pallas_call x1, Pallas kernels: 1.11 us -> 0.81 us  [local(): call(middle_kernel, (shape((n_mid, n_cols), bf16), shape((n_blocks - earl...]
    ppermute x1, waiting for transfers between devices: 2.79 us -> 2.49 us  [local(): lax.ppermute(send_second, ('parts', 'gz', 'ty'), halo_table(n_parts, n_gz...]
    ppermute x1, waiting for transfers between devices: 0.48 us -> 0.78 us  [local(): lax.ppermute(send_first, ('parts', 'gz', 'ty'), halo_table(n_parts, n_gz,...]
where the time goes in v8:
time: 26.3 us; the launch traced here: 26.1 us
  starting transfers between devices  9.93 us (38%)
  Pallas kernels  9.73 us (37%)
  waiting for transfers between devices  5.63 us (21%)
  between operations  0.77 us (3%)
    pallas_call x1, Pallas kernels, local(): call(functools.partial(waiting_kernel, n_ty, tuple(swaps)), (shape((n_row...  3.9 us
    ppermute x3, starting transfers between devices, local(): lax.ppermute(payload, ('gz', 'ty'), route)  3.49 us
    ppermute x1, starting transfers between devices, local(): lax.ppermute(send_first, ('parts', 'gz', 'ty'), halo_table(n_parts, n_gz,...  3.09 us
    ppermute x1, waiting for transfers between devices, local(): lax.ppermute(send_second, ('parts', 'gz', 'ty'), halo_table(n_parts, n_gz...  2.49 us
    ppermute x3, waiting for transfers between devices, local(): lax.ppermute(payload, ('gz', 'ty'), route)  1.99 us
    ppermute x2, starting transfers between devices, local(): old_seconds = [lax.ppermute(e, 'gz', to_next) for e in second_edges]  1.66 us
    ppermute x1, starting transfers between devices, local(): lax.ppermute(send_second, ('parts', 'gz', 'ty'), halo_table(n_parts, n_gz...  1.58 us
    pallas_call x2, Pallas kernels, render_edges(): call(functools.partial(edges_kernel, which, parts), [shape((MARGIN, n_col...  1.3 us
  transfers between devices with their start and end apart: 9, of which 5 were waited for; matrix products, arithmetic and copies ran while one was open for 0% of the time, Pallas kernels for 31%

profile of v8, /device:TPU:0, one launch (start us, length us, event | category | flops | bytes accessed | tf_op | source)
XLA Modules:
  0.0 26.1 jit_solution(9861668346886041703)
XLA Ops:
  0.6 0.0 copy-start
  0.6 1.2 %shard_map.95 = (bf16[64,2048]{1,0:T(8,128)(2,1)S(1)}, f32[1,256]{1,0:T(1,128)S(1)}, f32[1,2048]{1,0:T(1,128)S(1)}, bf16[6,512,256]{2,1,0:T(8,128)(2,1)S(1)}) custom-call(bf16[256,2048]{1,0:T(8,128)(2,1)} %bitcast.2, s32[1,256]{1,0:T(1,128)} %row_shift.1, s32[1,256]{1,0:T(1,128)} %row_frac.1, s32[1,2048]{1,0:T(1,128)} %col_shift.1, s32[1,2048]{1,0:T(1,128)} %col_frac.1), custom_call_target="tpu_custom_call" | custom-call | tf_op jit(solution)/shard_map/pallas_call | solution.py:466
  1.8 0.0 copy-start.2
  1.8 3.1 %collective-permute-start = (bf16[64,2048]{1,0:T(8,128)(2,1)S(1)}, bf16[64,2048]{1,0:T(8,128)(2,1)S(1)}, u32[]{:S(2)}, u32[]{:S(2)}) collective-permute-start(bf16[64,2048]{1,0:T(8,128)(2,1)S(1)} %get-tuple-element.22), channel_id=1, source_target_pairs={{0,1},{1,0},{2,3},{3,2},{4,20},{5,6},{6,5},{7,23},{8,9},{9,8},{10,... | collective-permute-start | bytes 786440 | tf_op jit(solution)/shard_map/ppermute | solution.py:486
  4.9 0.0 copy-done
  4.9 0.8 %shard_map.96 = (bf16[128,2048]{1,0:T(8,128)(2,1)S(1)}, bf16[2,512,256]{2,1,0:T(8,128)(2,1)S(1)}, bf16[64,192]{1,0:T(8,128)(2,1)S(1)}, bf16[64,192]{1,0:T(8,128)(2,1)S(1)}) custom-call(bf16[256,2048]{1,0:T(8,128)(2,1)S(1)} %bitcast.3, f32[1,256]{1,0:T(1,128)S(1)} %get-tuple-element.18.row_pos, f32[1,2048]{1,0:T(1,128)S(1)} %get-tuple-element.19.col_pos, ...), custom_call_target="tpu_custom_call" | custom-call | tf_op jit(solution)/shard_map/pallas_call | solution.py:489
  5.7 0.1 collective-permute-start.2
  5.8 0.0 copy-done.2
  5.8 1.0 %shard_map.97._.rest_2_.turned_mid = bf16[96,64,128]{2,1,0:T(8,128)(2,1)S(1)} custom-call(s32[2,1,2,16]{3,2,1,0:T(2,128)S(1)} %copy-done.2, bf16[128,2048]{1,0:T(8,128)(2,1)S(1)} %get-tuple-element.21.mid), custom_call_target="tpu_custom_call" | custom-call | flops 1000000000 | bytes 3000000 | tf_op jit(solution)/shard_map/pallas_call | solution.py:497
  6.9 1.6 %collective-permute-start.1 = (bf16[64,2048]{1,0:T(8,128)(2,1)S(1)}, bf16[64,2048]{1,0:T(8,128)(2,1)S(1)}, u32[]{:S(2)}, u32[]{:S(2)}) collective-permute-start(bf16[64,2048]{1,0:T(8,128)(2,1)S(1)} %shard_map.98.rest_0_), channel_id=1, source_target_pairs={{0,16},{1,2},{2,1},{3,19},{4,5},{5,4},{6,7},{7,6},{8,24},{9,10},{1... | collective-permute-start | bytes 786440 | tf_op jit(solution)/shard_map/ppermute | solution.py:509
  8.5 0.8 %collective-permute-done.halo = bf16[64,2048]{1,0:T(8,128)(2,1)S(1)} collective-permute-done((bf16[64,2048]{1,0:T(8,128)(2,1)S(1)}, bf16[64,2048]{1,0:T(8,128)(2,1)S(1)}, u32[]{:S(2)}, u32[]{:S(2)}) %collective-permute-start) | collective-permute-done | bytes 262176 | tf_op jit(solution)/shard_map/ppermute | solution.py:486
  9.3 0.6 %shard_map.99.edge.first = bf16[64,2048]{1,0:T(8,128)(2,1)S(1)} custom-call(bf16[64,2048]{1,0:T(8,128)(2,1)S(1)} %collective-permute-done.halo, bf16[256,2048]{1,0:T(8,128)(2,1)S(1)} %bitcast.5, bf16[64,192]{1,0:T(8,128)(2,1)S(1)} %get-tuple-element.23.table, bf16[6,512,256]{2,1,0:T(8,128)(2,1)S(1)} %get-tuple-element.20.tables, ...), custom_call_target="tpu_custom_call" | custom-call | tf_op jit(solution)/shard_map/pallas_call | solution.py:511
  9.9 0.1 collective-permute-start.5
  10.0 0.9 %shard_map.100.rest_0_.rest_3_.turned_edge = bf16[48,64,128]{2,1,0:T(8,128)(2,1)S(1)} custom-call(s32[2,1,2,16]{3,2,1,0:T(2,128)S(1)} %copy-done.2, bf16[64,2048]{1,0:T(8,128)(2,1)S(1)} %shard_map.99.edge.first), custom_call_target="tpu_custom_call" | custom-call | flops 500000000 | bytes 1000000 | tf_op jit(solution)/shard_map/pallas_call | solution.py:522
  10.8 2.5 %collective-permute-done.1.halo = bf16[64,2048]{1,0:T(8,128)(2,1)S(1)} collective-permute-done((bf16[64,2048]{1,0:T(8,128)(2,1)S(1)}, bf16[64,2048]{1,0:T(8,128)(2,1)S(1)}, u32[]{:S(2)}, u32[]{:S(2)}) %collective-permute-start.1) | collective-permute-done | bytes 262176 | tf_op jit(solution)/shard_map/ppermute | solution.py:509
  13.3 0.0 copy-start.1
  13.3 0.6 %shard_map.101 = (bf16[64,1024]{1,0:T(8,128)(2,1)S(1)}, bf16[64,1024]{1,0:T(8,128)(2,1)S(1)}) custom-call(bf16[64,2048]{1,0:T(8,128)(2,1)S(1)} %collective-permute-done.1.halo, bf16[256,2048]{1,0:T(8,128)(2,1)S(1)} %bitcast.6, bf16[64,192]{1,0:T(8,128)(2,1)S(1)} %get-tuple-element.25.table, bf16[6,512,256]{2,1,0:T(8,128)(2,1)S(1)} %get-tuple-element.20.tables, ...), custom_call_target="tpu_custom_call" | custom-call | tf_op jit(solution)/shard_map/pallas_call | solution.py:511
  14.0 0.8 %collective-permute-start.4 = (bf16[64,1024]{1,0:T(8,128)(2,1)S(1)}, bf16[64,1024]{1,0:T(8,128)(2,1)S(1)}, u32[]{:S(2)}, u32[]{:S(2)}) collective-permute-start(bf16[64,1024]{1,0:T(8,128)(2,1)S(1)} %get-tuple-element.26.rest_0_), channel_id=1, source_target_pairs={{0,4},{4,8},{8,12},{12,0},{1,5},{5,9},{9,13},{13,1},{2,6},{6,10},{... | collective-permute-start | bytes 393224 | tf_op jit(solution)/shard_map/ppermute | solution.py:532
  14.8 0.9 %collective-permute-start.3 = (bf16[64,1024]{1,0:T(8,128)(2,1)S(1)}, bf16[64,1024]{1,0:T(8,128)(2,1)S(1)}, u32[]{:S(2)}, u32[]{:S(2)}) collective-permute-start(bf16[64,1024]{1,0:T(8,128)(2,1)S(1)} %get-tuple-element.27.rest_1_), channel_id=1, source_target_pairs={{0,4},{4,8},{8,12},{12,0},{1,5},{5,9},{9,13},{13,1},{2,6},{6,10},{... | collective-permute-start | bytes 393224 | tf_op jit(solution)/shard_map/ppermute | solution.py:532
  15.6 0.0 collective-permute-done.2.rest_6_.old_mid
  15.7 0.0 copy-done.1
  15.7 3.9 %shard_map.102 = (bf16[256,2048]{1,0:T(8,128)(2,1)}, bf16[48,64,128]{2,1,0:T(8,128)(2,1)S(1)}, f32[32,16,128]{2,1,0:T(8,128)S(1)}, f32[2,32,128]{2,1,0:T(8,128)S...) custom-call(s32[2,1,2,16]{3,2,1,0:T(2,128)S(1)} %copy-done.2, bf16[128,2048]{1,0:T(8,128)(2,1)S(1)} %get-tuple-element.21.mid, ...), custom_call_target="tpu_custom_call" | custom-call | flops 1000000000 | bytes 3000000 | tf_op jit(solution)/shard_map/pallas_call | solution.py:536
  19.6 0.0 collective-permute-done.5.old_edge
  19.6 0.0 collective-permute-done.4.old_edge
  19.6 0.4 %collective-permute-done.3.old_edge = bf16[64,1024]{1,0:T(8,128)(2,1)S(1)} collective-permute-done((bf16[64,1024]{1,0:T(8,128)(2,1)S(1)}, bf16[64,1024]{1,0:T(8,128)(2,1)S(1)}, u32[]{:S(2)}, u32[]{:S(2)}) %collective-permute-start.3) | collective-permute-done | bytes 131104 | tf_op jit(solution)/shard_map/ppermute | solution.py:532
  20.0 1.0 %collective-permute-start.6 = (f32[8,128]{1,0:T(8,128)S(1)}, f32[8,128]{1,0:T(8,128)S(1)}, u32[]{:S(2)}, u32[]{:S(2)}) collective-permute-start(f32[8,128]{1,0:T(8,128)S(1)} %shard_map.105.refs_0_), channel_id=1, source_target_pairs={{0,1},{1,0},{2,3},{3,2},{4,5},{5,4},{6,7},{7,6},{8,12},{9,10},{10,... | collective-permute-start | bytes 12296 | tf_op jit(solution)/shard_map/ppermute | solution.py:559
  21.0 2.5 %collective-permute-start.7 = (f32[8,128]{1,0:T(8,128)S(1)}, f32[8,128]{1,0:T(8,128)S(1)}, u32[]{:S(2)}, u32[]{:S(2)}) collective-permute-start(f32[8,128]{1,0:T(8,128)S(1)} %shard_map.105.refs_0_), channel_id=1, source_target_pairs={{0,2},{1,3},{2,0},{3,1},{4,6},{5,7},{6,4},{7,5},{8,10},{9,11},{10,... | collective-permute-start | bytes 12296 | tf_op jit(solution)/shard_map/ppermute | solution.py:559
  23.5 0.0 collective-permute-start.8
  23.5 0.1 collective-permute-done.6.refs_1_
  23.6 1.9 %collective-permute-done.7.refs_2_ = f32[8,128]{1,0:T(8,128)S(1)} collective-permute-done((f32[8,128]{1,0:T(8,128)S(1)}, f32[8,128]{1,0:T(8,128)S(1)}, u32[]{:S(2)}, u32[]{:S(2)}) %collective-permute-start.7) | collective-permute-done | bytes 4128 | tf_op jit(solution)/shard_map/ppermute | solution.py:559
  25.5 0.0 collective-permute-done.8.refs_3_
  25.5 0.6 %shard_map.106 = f32[2,1,2,16]{3,2,1,0:T(2,128)} custom-call(f32[16,8,128]{2,1,0:T(8,128)S(1)} %get-tuple-element.29.row_weights, f32[8,128]{1,0:T(8,128)S(1)} %shard_map.105.refs_0_, f32[8,128]{1,0:T(8,128)S(1)} %collective-permute-done.6.refs_1_, f32[8,128]{1,0:T(8,128)S(1)} %collective-permute-done.7.refs_2_, f32[8,128]{1,0:T(8,128)S(1)} %collective-permute-done.8.refs_3_), custom_call_target="tpu_custom_call" | custom-call | tf_op jit(solution)/shard_map/pallas_call | solution.py:560
  (4 shorter events, 0.1 us)
Async XLA Ops:
  0.6 4.3 %copy-start = (bf16[1,256,2048]{2,1,0:T(8,128)(2,1)S(1)}, bf16[1,256,2048]{2,1,0:T(8,128)(2,1)}, u32[]{:S(2)}) copy-start(bf16[1,256,2048]{2,1,0:T(8,128)(2,1)} %param.8) | copy-start | bytes 3145732
  1.8 4.0 %copy-start.2 = (s32[2,1,2,16]{3,2,1,0:T(2,128)S(1)}, s32[2,1,2,16]{3,2,1,0:T(2,128)}, u32[]{:S(2)}) copy-start(s32[2,1,2,16]{3,2,1,0:T(2,128)} %peaks.5) | copy-start | bytes 772
  1.8 7.4 %collective-permute-start = (bf16[64,2048]{1,0:T(8,128)(2,1)S(1)}, bf16[64,2048]{1,0:T(8,128)(2,1)S(1)}, u32[]{:S(2)}, u32[]{:S(2)}) collective-permute-start(bf16[64,2048]{1,0:T(8,128)(2,1)S(1)} %get-tuple-element.22), channel_id=1, source_target_pairs={{0,1},{1,0},{2,3},{3,2},{4,20},{5,6},{6,5},{7,23},{8,9},{9,8},{10,... | collective-permute-start | bytes 786440 | tf_op jit(solution)/shard_map/ppermute | solution.py:486
  5.7 9.9 %collective-permute-start.2 = (bf16[128,2048]{1,0:T(8,128)(2,1)S(1)}, bf16[128,2048]{1,0:T(8,128)(2,1)S(1)}, u32[]{:S(2)}, u32[]{:S(2)}) collective-permute-start(bf16[128,2048]{1,0:T(8,128)(2,1)S(1)} %get-tuple-element.21.mid), channel_id=1, source_target_pairs={{0,4},{4,8},{8,12},{12,0},{1,5},{5,9},{9,13},{13,1},{2,6},{6,10},{... | collective-permute-start | bytes 1572872 | tf_op jit(solution)/shard_map/ppermute | solution.py:496
  6.9 6.4 %collective-permute-start.1 = (bf16[64,2048]{1,0:T(8,128)(2,1)S(1)}, bf16[64,2048]{1,0:T(8,128)(2,1)S(1)}, u32[]{:S(2)}, u32[]{:S(2)}) collective-permute-start(bf16[64,2048]{1,0:T(8,128)(2,1)S(1)} %shard_map.98.rest_0_), channel_id=1, source_target_pairs={{0,16},{1,2},{2,1},{3,19},{4,5},{5,4},{6,7},{7,6},{8,24},{9,10},{1... | collective-permute-start | bytes 786440 | tf_op jit(solution)/shard_map/ppermute | solution.py:509
  9.9 9.7 %collective-permute-start.5 = (bf16[64,2048]{1,0:T(8,128)(2,1)S(1)}, bf16[64,2048]{1,0:T(8,128)(2,1)S(1)}, u32[]{:S(2)}, u32[]{:S(2)}) collective-permute-start(bf16[64,2048]{1,0:T(8,128)(2,1)S(1)} %shard_map.99.edge.first), channel_id=1, source_target_pairs={{0,4},{4,8},{8,12},{12,0},{1,5},{5,9},{9,13},{13,1},{2,6},{6,10},{... | collective-permute-start | bytes 786440 | tf_op jit(solution)/shard_map/ppermute | solution.py:521
  13.3 2.3 %copy-start.1 = (f32[16,128]{1,0:T(8,128)S(1)}, f32[16,128]{1,0:T(8,128)}, u32[]{:S(2)}) copy-start(f32[16,128]{1,0:T(8,128)} %constant.2.clone.rest_5_.smooth) | copy-start | bytes 24580
  14.0 5.6 %collective-permute-start.4 = (bf16[64,1024]{1,0:T(8,128)(2,1)S(1)}, bf16[64,1024]{1,0:T(8,128)(2,1)S(1)}, u32[]{:S(2)}, u32[]{:S(2)}) collective-permute-start(bf16[64,1024]{1,0:T(8,128)(2,1)S(1)} %get-tuple-element.26.rest_0_), channel_id=1, source_target_pairs={{0,4},{4,8},{8,12},{12,0},{1,5},{5,9},{9,13},{13,1},{2,6},{6,10},{... | collective-permute-start | bytes 393224 | tf_op jit(solution)/shard_map/ppermute | solution.py:532
  14.8 5.2 %collective-permute-start.3 = (bf16[64,1024]{1,0:T(8,128)(2,1)S(1)}, bf16[64,1024]{1,0:T(8,128)(2,1)S(1)}, u32[]{:S(2)}, u32[]{:S(2)}) collective-permute-start(bf16[64,1024]{1,0:T(8,128)(2,1)S(1)} %get-tuple-element.27.rest_1_), channel_id=1, source_target_pairs={{0,4},{4,8},{8,12},{12,0},{1,5},{5,9},{9,13},{13,1},{2,6},{6,10},{... | collective-permute-start | bytes 393224 | tf_op jit(solution)/shard_map/ppermute | solution.py:532
  20.0 3.6 %collective-permute-start.6 = (f32[8,128]{1,0:T(8,128)S(1)}, f32[8,128]{1,0:T(8,128)S(1)}, u32[]{:S(2)}, u32[]{:S(2)}) collective-permute-start(f32[8,128]{1,0:T(8,128)S(1)} %shard_map.105.refs_0_), channel_id=1, source_target_pairs={{0,1},{1,0},{2,3},{3,2},{4,5},{5,4},{6,7},{7,6},{8,12},{9,10},{10,... | collective-permute-start | bytes 12296 | tf_op jit(solution)/shard_map/ppermute | solution.py:559
  21.0 4.5 %collective-permute-start.7 = (f32[8,128]{1,0:T(8,128)S(1)}, f32[8,128]{1,0:T(8,128)S(1)}, u32[]{:S(2)}, u32[]{:S(2)}) collective-permute-start(f32[8,128]{1,0:T(8,128)S(1)} %shard_map.105.refs_0_), channel_id=1, source_target_pairs={{0,2},{1,3},{2,0},{3,1},{4,6},{5,7},{6,4},{7,5},{8,10},{9,11},{10,... | collective-permute-start | bytes 12296 | tf_op jit(solution)/shard_map/ppermute | solution.py:559
  23.5 2.0 %collective-permute-start.8 = (f32[8,128]{1,0:T(8,128)S(1)}, f32[8,128]{1,0:T(8,128)S(1)}, u32[]{:S(2)}, u32[]{:S(2)}) collective-permute-start(f32[8,128]{1,0:T(8,128)S(1)} %shard_map.105.refs_0_), channel_id=1, source_target_pairs={{0,4},{1,2},{2,1},{3,7},{4,0},{5,6},{6,5},{7,3},{8,9},{9,8},{10,11... | collective-permute-start | bytes 12296 | tf_op jit(solution)/shard_map/ppermute | solution.py:559

commit v9 on v8

--- a/solution.py
+++ b/solution.py
@@ -51,6 +51,21 @@
                 else:
                     continue
                 table.append(tuple((a * n_gz + b) * n_ty + c for a, b, c in ((p, z, t), there)))
+    return tuple(table)
+
+
+def next_chip_table(n_parts, n_gz):
+    table = []
+    for p in range(n_parts):
+        for z in range(n_gz):
+            partner = z + 1 if z % 2 else z - 1
+            if 0 <= partner < n_gz:
+                there = (p, partner)
+            elif (p ^ 1) < n_parts:
+                there = (p ^ 1, z)
+            else:
+                continue
+            table.append((p * n_gz + z, there[0] * n_gz + there[1]))
     return tuple(table)
 
 
@@ -229,10 +244,6 @@
 
 def edge_patch_row(second, patch_rows):
     return jnp.where(takes_bottom(second), patch_rows - 1, 0)
-
-
-def turn_first_kernel(patch_rows, peaks, edge, turned):
-    turn_patches(peaks, edge_patch_row(False, patch_rows), slice(None), edge, turned, 0)
 
 
 def patch_row_flow(i, cols, turned_edge, turned_mid, bands, peak, smooth, old_of, acc):
@@ -281,11 +292,47 @@
     return sum(jnp.where(at == c * patch_rows + i, line, 0.0) for c, line in enumerate(lines))
 
 
-def waiting_kernel(n_ty, swaps, peaks, mid, first, *rest):
+def boundary_flow(i, patch_rows, turned_edge, turned_mid, bands, peak, whole, smooth, acc):
+    at_edge = pl.multiple_of(i * PATCH + jnp.where(i == 0, 0, PATCH - MARGIN), MARGIN)
+    at_mid = pl.multiple_of(i * PATCH + jnp.where(i == 0, MARGIN, 0), MARGIN)
+
+    def old_of(j):
+        here = slice(j * PATCH, (j + 1) * PATCH)
+        return jnp.concatenate([whole[pl.ds(at_edge, MARGIN), here], whole[pl.ds(at_mid, MARGIN), here]], axis=0)
+
+    cols = range(whole.shape[1] // PATCH)
+    return put_lines(
+        patch_row_flow(i, cols, turned_edge, turned_mid, bands, peak, smooth, old_of, acc), i, patch_rows
+    )
+
+
+def first_waiting_kernel(n_ty, swaps, peaks, edge, turned_mid, boundary, smooth, *rest):
+    turned, bands, peak, row_weights, flow, whole, acc, sem = rest
+    patch_rows = boundary.shape[0] // PATCH
+    i = edge_patch_row(False, patch_rows)
+    fetch = pltpu.make_async_copy(boundary, whole, sem)
+    has_boundary = lax.axis_index("gz") == 0
+
+    @pl.when(has_boundary)
+    def _():
+        fetch.start()
+
+    flow[...] = jnp.zeros_like(flow)
+    turn_patches(peaks, i, slice(None), edge, turned, 0)
+    plan_windows(peaks, bands, peak)
+    fill_row_weights(n_ty, swaps, patch_rows, row_weights)
+
+    @pl.when(has_boundary)
+    def _():
+        fetch.wait()
+        flow[...] = boundary_flow(i, patch_rows, turned, turned_mid, bands, peak, whole, smooth, acc)
+
+
+def waiting_kernel(peaks, mid, first, *rest):
     seconds, rest = rest[:EDGE_PARTS], rest[EDGE_PARTS:]
-    turned_mid, turned_first, boundary, smooth, _ = rest[:5]
-    rendered, turned_second, bands, peak, row_weights, flow, acc, whole, sems = rest[5:]
-    n_rows, n_cols = boundary.shape
+    turned_mid, bands, peak, whole, smooth, before, _ = rest[:7]
+    rendered, turned, flow, acc, sems = rest[7:]
+    n_rows, n_cols = whole.shape
     patch_rows = n_rows // PATCH
     moves = [(mid, pl.ds(MARGIN, mid.shape[0]), pl.ds(0, n_cols))]
     wide = n_cols // EDGE_PARTS
@@ -293,55 +340,29 @@
         at = pl.multiple_of(jnp.where(takes_bottom(which), n_rows - MARGIN, 0), MARGIN)
         moves.append((edge, pl.ds(at, MARGIN), pl.ds(start, edge.shape[1])))
     copies = [pltpu.make_async_copy(a, rendered.at[b, c], sems.at[k]) for k, (a, b, c) in enumerate(moves)]
-    fetch = pltpu.make_async_copy(boundary, whole, sems.at[len(moves)])
+    i = edge_patch_row(True, patch_rows)
     has_boundary = lax.axis_index("gz") == 0
+    for copy in copies:
+        copy.start()
+    flow[...] = before[...]
+    for k, edge in enumerate(seconds):
+        turn_patches(peaks, i, slice(None), edge, turned, k * (wide // PATCH))
 
     @pl.when(has_boundary)
     def _():
-        fetch.start()
-
-    for copy in copies:
-        copy.start()
-    flow[...] = jnp.zeros_like(flow)
-    for k, edge in enumerate(seconds):
-        turn_patches(peaks, edge_patch_row(True, patch_rows), slice(None), edge, turned_second, k * (wide // PATCH))
-    plan_windows(peaks, bands, peak)
-    fill_row_weights(n_ty, swaps, patch_rows, row_weights)
-
-    @pl.when(has_boundary)
-    def _():
-        fetch.wait()
-
-        @pl.loop(0, patch_rows)
-        def _(k):
-            i = jnp.where(k == 0, edge_patch_row(False, patch_rows), edge_patch_row(True, patch_rows))
-            at_edge = pl.multiple_of(i * (n_rows - MARGIN), MARGIN)
-            at_mid = pl.multiple_of(MARGIN + i * MARGIN, MARGIN)
-
-            def old_of(j):
-                cols = slice(j * PATCH, (j + 1) * PATCH)
-                return jnp.concatenate([whole[pl.ds(at_edge, MARGIN), cols], whole[pl.ds(at_mid, MARGIN), cols]], axis=0)
-
-            def flow_with(turned_edge):
-                flow[...] += put_lines(
-                    patch_row_flow(i, range(n_cols // PATCH), turned_edge, turned_mid, bands, peak, smooth, old_of, acc), i, patch_rows
-                )
-
-            @pl.when(k == 0)
-            def _():
-                flow_with(turned_first)
-
-            @pl.when(k != 0)
-            def _():
-                flow_with(turned_second)
+        flow[...] = before[...] + boundary_flow(
+            i, patch_rows, turned, turned_mid, bands, peak, whole, smooth, acc
+        )
 
     for copy in copies:
         copy.wait()
 
 
-def window_kernel(second, cols, turned_mid, turned_edge, bands, peak, old_mid, old_edge, smooth, before, out_ref, acc):
+def window_kernel(second, cols, turned_mid, turned_edge, bands, peak, old_mid, smooth, before, *rest):
+    old_edges, (out_ref, acc) = rest[:-2], rest[-2:]
     patch_rows = old_mid.shape[0] // MARGIN
     out_ref[...] = before[...]
+    odd = lax.axis_index("gz") % 2 == 1
 
     @pl.when(lax.axis_index("gz") != 0)
     def _():
@@ -351,7 +372,10 @@
         def old_of(j):
             here = slice((j - cols[0]) * PATCH, (j - cols[0] + 1) * PATCH)
             there = slice(j * PATCH, (j + 1) * PATCH)
-            return jnp.concatenate([old_edge[:, here], old_mid[pl.ds(at_mid, MARGIN), there]], axis=0)
+            old_edge = old_edges[0][:, here]
+            for other in old_edges[1:]:
+                old_edge = jnp.where(odd, other[:, here], old_edge)
+            return jnp.concatenate([old_edge, old_mid[pl.ds(at_mid, MARGIN), there]], axis=0)
 
         lines = patch_row_flow(i, cols, turned_edge, turned_mid, bands, peak, smooth, old_of, acc)
         out_ref[...] = before[...] + put_lines(lines, i, patch_rows)
@@ -519,43 +543,63 @@
     turned_shape = shape((3 * patch_cols, MARGIN, LANES), bf16)
     (first_edge,) = render_edges(False, 1, first, held, first_table, tables, more_tables, send_second)
     old_first = lax.ppermute(first_edge, "gz", to_next)
-    turned_first = call(
-        functools.partial(turn_first_kernel, patch_rows),
-        turned_shape,
-        [smem, vmem],
-        vmem,
-        flops=500_000_000,
-        moved=1_000_000,
-    )(peak_shift, first_edge)
-    second_edges = render_edges(True, EDGE_PARTS, second, held, second_table, tables, more_tables, turned_first)
-    part_cols = patch_cols // EDGE_PARTS
-    old_seconds = [lax.ppermute(e, "gz", to_next) for e in second_edges]
     smooth = jnp.asarray(column_smoother(patch_cols))
     acc = pltpu.VMEM((9 * patch_cols * 8, LANES), f32)
-    terms = (len(swaps) + 1) * 2 * patch_rows
-    rendered, turned_second, bands, peak, row_weights, payload = call(
-        functools.partial(waiting_kernel, n_ty, tuple(swaps)),
+    line_shape = shape((8, LANES), f32)
+    turned_first, bands, peak, row_weights, payload, old_boundary = call(
+        functools.partial(first_waiting_kernel, n_ty, tuple(swaps)),
         (
-            shape((n_rows, n_cols), bf16),
             turned_shape,
             shape((n_patches, PATCH // 8, LANES), f32),
             shape((2, n_patches, LANES), f32),
-            shape((terms, 8, LANES), f32),
-            shape((8, LANES), f32),
+            shape(((len(swaps) + 1) * 2 * patch_rows, 8, LANES), f32),
+            line_shape,
+            shape((n_rows, n_cols), bf16),
         ),
-        [smem] + [vmem] * (4 + EDGE_PARTS) + [hbm, vmem, unread],
-        [hbm] + [vmem] * 5,
-        [acc, pltpu.VMEM((n_rows, n_cols), bf16), pltpu.SemaphoreType.DMA((3 + EDGE_PARTS,))],
+        [smem, vmem, vmem, hbm, vmem],
+        [vmem] * 6,
+        [acc, pltpu.SemaphoreType.DMA],
+        flops=500_000_000,
+        moved=1_000_000,
+    )(peak_shift, first_edge, turned_mid, in_hbm(boundary), smooth)
+    second_edges = render_edges(True, EDGE_PARTS, second, held, second_table, tables, more_tables, turned_first)
+    part_cols = patch_cols // EDGE_PARTS
+    old_seconds = [[lax.ppermute(e, "gz", to_next)] for e in second_edges[:-1]]
+    in_chip = [(z, z ^ 1) for z in range(n_gz) if (z ^ 1) < n_gz]
+    old_seconds.append(
+        [
+            lax.ppermute(second_edges[-1], ("parts", "gz"), next_chip_table(n_parts, n_gz)),
+            lax.ppermute(second_edges[-1], "gz", in_chip),
+        ]
+    )
+    rendered, turned_second, payload = call(
+        waiting_kernel,
+        (shape((n_rows, n_cols), bf16), turned_shape, line_shape),
+        [smem] + [vmem] * (8 + EDGE_PARTS) + [unread],
+        [hbm] + [vmem] * 2,
+        [acc, pltpu.SemaphoreType.DMA((2 + EDGE_PARTS,))],
         flops=1_000_000_000,
         moved=3_000_000,
-    )(peak_shift, mid, first_edge, *second_edges, turned_mid, turned_first, in_hbm(boundary), smooth, old_mid)
-    windows = [(True, range(patch_cols), turned_second, old_first)]
+    )(
+        peak_shift,
+        mid,
+        first_edge,
+        *second_edges,
+        turned_mid,
+        bands,
+        peak,
+        old_boundary,
+        smooth,
+        payload,
+        old_mid,
+    )
+    windows = [(True, range(patch_cols), turned_second, [old_first])]
     for k, old in enumerate(old_seconds):
         windows.append((False, range(k * part_cols, (k + 1) * part_cols), turned_first, old))
     for which, cols, turned, old in windows:
         payload = call(
-            functools.partial(window_kernel, which, cols), shape((8, LANES), f32), [vmem] * 8, vmem, [acc]
-        )(turned_mid, turned, bands, peak, old_mid, old, smooth, payload)
+            functools.partial(window_kernel, which, cols), line_shape, [vmem] * (7 + len(old)), vmem, [acc]
+        )(turned_mid, turned, bands, peak, old_mid, smooth, payload, *old)
     blocks = [payload] + [lax.ppermute(payload, ("gz", "ty"), route) for route in routes]
     flow = call(
         rows_kernel, shape((2, 1, patch_rows, patch_cols), f32), [vmem] * (1 + len(blocks)), vmem

time: 26.3 us -> 26.3 us (level)
  starting transfers between devices: 9.93 us -> 11.1 us
  waiting for transfers between devices: 5.63 us -> 4.71 us
    ppermute x1, waiting for transfers between devices: 2.49 us -> 0.6 us  [local(): lax.ppermute(send_second, ('parts', 'gz', 'ty'), halo_table(n_parts, n_gz...]
    ppermute x2 -> x3, waiting for transfers between devices: 0.37 us -> 1.64 us  [the longest x1 1.15 us: local(): lax.ppermute(second_edges[-1], ('parts', 'gz'), next_chip_table(n_parts,...]
    ppermute x2 -> x3, starting transfers between devices: 1.66 us -> 2.3 us  [the longest x1 1.52 us: local(): lax.ppermute(second_edges[-1], ('parts', 'gz'), next_chip_table(n_parts,...]
    ppermute x3, starting transfers between devices: 3.49 us -> 4 us  [local(): lax.ppermute(payload, ('gz', 'ty'), route)]
    ppermute x3, waiting for transfers between devices: 1.99 us -> 1.71 us  [local(): lax.ppermute(payload, ('gz', 'ty'), route)]
    pallas_call x5, Pallas kernels: 4.8 us -> 4.51 us  [the longest x1 2.73 us: local(): call(functools.partial(first_waiting_kernel, n_ty, tuple(swaps)), (turned...]
  transfers between devices with their start and end apart: 9 -> 10, of which waited for: 5 -> 5; matrix products, arithmetic and copies ran while one was open for 0% -> 0% of each run, Pallas kernels for 31% -> 30%
where the time goes in v9:
time: 26.3 us; the launch traced here: 26.1 us
  starting transfers between devices  11.1 us (42%)
  Pallas kernels  9.49 us (36%)
  waiting for transfers between devices  4.71 us (18%)
  between operations  0.77 us (3%)
    ppermute x3, starting transfers between devices, local(): lax.ppermute(payload, ('gz', 'ty'), route)  4 us
    ppermute x1, starting transfers between devices, local(): lax.ppermute(send_first, ('parts', 'gz', 'ty'), halo_table(n_parts, n_gz,...  3.09 us
    pallas_call x1, Pallas kernels, local(): call(functools.partial(first_waiting_kernel, n_ty, tuple(swaps)), (turned...  2.73 us
    pallas_call x1, Pallas kernels, local(): call(waiting_kernel, (shape((n_rows, n_cols), bf16), turned_shape, line_s...  1.76 us
    ppermute x3, waiting for transfers between devices, local(): lax.ppermute(payload, ('gz', 'ty'), route)  1.71 us
    ppermute x1, starting transfers between devices, local(): lax.ppermute(send_second, ('parts', 'gz', 'ty'), halo_table(n_parts, n_gz...  1.58 us
    ppermute x1, starting transfers between devices, local(): lax.ppermute(second_edges[-1], ('parts', 'gz'), next_chip_table(n_parts,...  1.52 us
    pallas_call x2, Pallas kernels, render_edges(): call(functools.partial(edges_kernel, which, parts), [shape((MARGIN, n_col...  1.32 us
  transfers between devices with their start and end apart: 10, of which 5 were waited for; matrix products, arithmetic and copies ran while one was open for 0% of the time, Pallas kernels for 30%

profile of v9, /device:TPU:0, one launch (start us, length us, event | category | flops | bytes accessed | tf_op | source)
XLA Modules:
  0.0 26.1 jit_solution(8974275277376408681)
XLA Ops:
  0.6 0.0 copy-start
  0.6 1.2 %shard_map.95 = (bf16[64,2048]{1,0:T(8,128)(2,1)S(1)}, f32[1,256]{1,0:T(1,128)S(1)}, f32[1,2048]{1,0:T(1,128)S(1)}, bf16[6,512,256]{2,1,0:T(8,128)(2,1)S(1)}) custom-call(bf16[256,2048]{1,0:T(8,128)(2,1)} %bitcast.2, s32[1,256]{1,0:T(1,128)} %row_shift.1, s32[1,256]{1,0:T(1,128)} %row_frac.1, s32[1,2048]{1,0:T(1,128)} %col_shift.1, s32[1,2048]{1,0:T(1,128)} %col_frac.1), custom_call_target="tpu_custom_call" | custom-call | tf_op jit(solution)/shard_map/pallas_call | solution.py:490
  1.8 0.0 copy-start.2
  1.8 3.1 %collective-permute-start = (bf16[64,2048]{1,0:T(8,128)(2,1)S(1)}, bf16[64,2048]{1,0:T(8,128)(2,1)S(1)}, u32[]{:S(2)}, u32[]{:S(2)}) collective-permute-start(bf16[64,2048]{1,0:T(8,128)(2,1)S(1)} %get-tuple-element.25), channel_id=1, source_target_pairs={{0,1},{1,0},{2,3},{3,2},{4,20},{5,6},{6,5},{7,23},{8,9},{9,8},{10,... | collective-permute-start | bytes 786440 | tf_op jit(solution)/shard_map/ppermute | solution.py:510
  4.9 0.0 copy-done
  4.9 0.8 %shard_map.96 = (bf16[128,2048]{1,0:T(8,128)(2,1)S(1)}, bf16[2,512,256]{2,1,0:T(8,128)(2,1)S(1)}, bf16[64,192]{1,0:T(8,128)(2,1)S(1)}, bf16[64,192]{1,0:T(8,128)(2,1)S(1)}) custom-call(bf16[256,2048]{1,0:T(8,128)(2,1)S(1)} %bitcast.3, f32[1,256]{1,0:T(1,128)S(1)} %get-tuple-element.21.row_pos, f32[1,2048]{1,0:T(1,128)S(1)} %get-tuple-element.22.col_pos, ...), custom_call_target="tpu_custom_call" | custom-call | tf_op jit(solution)/shard_map/pallas_call | solution.py:513
  5.7 0.1 collective-permute-start.2
  5.8 0.0 copy-done.2
  5.8 1.0 %shard_map.97._.turned_mid.rest_2_ = bf16[96,64,128]{2,1,0:T(8,128)(2,1)S(1)} custom-call(s32[2,1,2,16]{3,2,1,0:T(2,128)S(1)} %copy-done.2, bf16[128,2048]{1,0:T(8,128)(2,1)S(1)} %get-tuple-element.24.mid), custom_call_target="tpu_custom_call" | custom-call | flops 1000000000 | bytes 3000000 | tf_op jit(solution)/shard_map/pallas_call | solution.py:521
  6.9 1.6 %collective-permute-start.1 = (bf16[64,2048]{1,0:T(8,128)(2,1)S(1)}, bf16[64,2048]{1,0:T(8,128)(2,1)S(1)}, u32[]{:S(2)}, u32[]{:S(2)}) collective-permute-start(bf16[64,2048]{1,0:T(8,128)(2,1)S(1)} %shard_map.98.rest_0_), channel_id=1, source_target_pairs={{0,16},{1,2},{2,1},{3,19},{4,5},{5,4},{6,7},{7,6},{8,24},{9,10},{1... | collective-permute-start | bytes 786440 | tf_op jit(solution)/shard_map/ppermute | solution.py:533
  8.5 0.8 %collective-permute-done.halo = bf16[64,2048]{1,0:T(8,128)(2,1)S(1)} collective-permute-done((bf16[64,2048]{1,0:T(8,128)(2,1)S(1)}, bf16[64,2048]{1,0:T(8,128)(2,1)S(1)}, u32[]{:S(2)}, u32[]{:S(2)}) %collective-permute-start) | collective-permute-done | bytes 262176 | tf_op jit(solution)/shard_map/ppermute | solution.py:510
  9.3 0.0 copy-start.1
  9.3 0.7 %shard_map.99.edge.first = bf16[64,2048]{1,0:T(8,128)(2,1)S(1)} custom-call(bf16[64,2048]{1,0:T(8,128)(2,1)S(1)} %collective-permute-done.halo, bf16[256,2048]{1,0:T(8,128)(2,1)S(1)} %bitcast.5, bf16[64,192]{1,0:T(8,128)(2,1)S(1)} %get-tuple-element.26.table, bf16[6,512,256]{2,1,0:T(8,128)(2,1)S(1)} %get-tuple-element.23.tables, ...), custom_call_target="tpu_custom_call" | custom-call | tf_op jit(solution)/shard_map/pallas_call | solution.py:535
  9.9 0.1 collective-permute-start.3
  10.0 0.0 copy-done.1
  10.0 2.7 %shard_map.100 = (bf16[48,64,128]{2,1,0:T(8,128)(2,1)S(1)}, f32[32,16,128]{2,1,0:T(8,128)S(1)}, f32[2,32,128]{2,1,0:T(8,128)S(1)}, f32[16,8,128]{2,1,0:T(8,128)S...) custom-call(s32[2,1,2,16]{3,2,1,0:T(2,128)S(1)} %copy-done.2, bf16[64,2048]{1,0:T(8,128)(2,1)S(1)} %shard_map.99.edge.first, ...), custom_call_target="tpu_custom_call" | custom-call | flops 500000000 | bytes 1000000 | tf_op jit(solution)/shard_map/pallas_call | solution.py:549
  12.7 0.6 %collective-permute-done.1.halo = bf16[64,2048]{1,0:T(8,128)(2,1)S(1)} collective-permute-done((bf16[64,2048]{1,0:T(8,128)(2,1)S(1)}, bf16[64,2048]{1,0:T(8,128)(2,1)S(1)}, u32[]{:S(2)}, u32[]{:S(2)}) %collective-permute-start.1) | collective-permute-done | bytes 262176 | tf_op jit(solution)/shard_map/ppermute | solution.py:533
  13.3 0.7 %shard_map.101 = (bf16[64,1024]{1,0:T(8,128)(2,1)S(1)}, bf16[64,1024]{1,0:T(8,128)(2,1)S(1)}) custom-call(bf16[64,2048]{1,0:T(8,128)(2,1)S(1)} %collective-permute-done.1.halo, bf16[256,2048]{1,0:T(8,128)(2,1)S(1)} %bitcast.6, bf16[64,192]{1,0:T(8,128)(2,1)S(1)} %get-tuple-element.28.table, bf16[6,512,256]{2,1,0:T(8,128)(2,1)S(1)} %get-tuple-element.23.tables, ...), custom_call_target="tpu_custom_call" | custom-call | tf_op jit(solution)/shard_map/pallas_call | solution.py:535
  14.0 0.8 %collective-permute-start.4 = (bf16[64,1024]{1,0:T(8,128)(2,1)S(1)}, bf16[64,1024]{1,0:T(8,128)(2,1)S(1)}, u32[]{:S(2)}, u32[]{:S(2)}) collective-permute-start(bf16[64,1024]{1,0:T(8,128)(2,1)S(1)} %get-tuple-element.30.rest_0_), channel_id=1, source_target_pairs={{0,4},{4,8},{8,12},{12,0},{1,5},{5,9},{9,13},{13,1},{2,6},{6,10},{... | collective-permute-start | bytes 393224 | tf_op jit(solution)/shard_map/ppermute | solution.py:567
  14.8 1.5 %collective-permute-start.5 = (bf16[64,1024]{1,0:T(8,128)(2,1)S(1)}, bf16[64,1024]{1,0:T(8,128)(2,1)S(1)}, u32[]{:S(2)}, u32[]{:S(2)}) collective-permute-start(bf16[64,1024]{1,0:T(8,128)(2,1)S(1)} %get-tuple-element.31.rest_1_), channel_id=1, source_target_pairs={{0,16},{4,8},{8,4},{12,28},{16,0},{20,24},{24,20},{28,12},{1,17},{... | collective-permute-start | bytes 393224 | tf_op jit(solution)/shard_map/ppermute | solution.py:571
  16.3 0.0 collective-permute-start.6
  16.3 0.0 collective-permute-done.2.rest_8_.old_mid
  16.3 1.8 %shard_map.102 = (bf16[256,2048]{1,0:T(8,128)(2,1)}, bf16[48,64,128]{2,1,0:T(8,128)(2,1)S(1)}, f32[8,128]{1,0:T(8,128)S(1)}) custom-call(s32[2,1,2,16]{3,2,1,0:T(2,128)S(1)} %copy-done.2, bf16[128,2048]{1,0:T(8,128)(2,1)S(1)} %get-tuple-element.24.mid, bf16[64,2048]{1,0:T(8,128)(2,1)S(1)} %shard_map.99.edge.first, ...), custom_call_target="tpu_custom_call" | custom-call | flops 1000000000 | bytes 3000000 | tf_op jit(solution)/shard_map/pallas_call | solution.py:575
  18.1 0.0 collective-permute-done.3.rest_0_
  18.1 0.5 %collective-permute-done.4.rest_0_ = bf16[64,1024]{1,0:T(8,128)(2,1)S(1)} collective-permute-done((bf16[64,1024]{1,0:T(8,128)(2,1)S(1)}, bf16[64,1024]{1,0:T(8,128)(2,1)S(1)}, u32[]{:S(2)}, u32[]{:S(2)}) %collective-permute-start.4) | collective-permute-done | bytes 131104 | tf_op jit(solution)/shard_map/ppermute | solution.py:567
  18.6 1.2 %collective-permute-done.5.rest_0_ = bf16[64,1024]{1,0:T(8,128)(2,1)S(1)} collective-permute-done((bf16[64,1024]{1,0:T(8,128)(2,1)S(1)}, bf16[64,1024]{1,0:T(8,128)(2,1)S(1)}, u32[]{:S(2)}, u32[]{:S(2)}) %collective-permute-start.5) | collective-permute-done | bytes 131104 | tf_op jit(solution)/shard_map/ppermute | solution.py:571
  19.8 0.0 collective-permute-done.6.rest_1_
  19.8 1.2 %collective-permute-start.7 = (f32[8,128]{1,0:T(8,128)S(1)}, f32[8,128]{1,0:T(8,128)S(1)}, u32[]{:S(2)}, u32[]{:S(2)}) collective-permute-start(f32[8,128]{1,0:T(8,128)S(1)} %shard_map.105.refs_0_), channel_id=1, source_target_pairs={{0,1},{1,0},{2,3},{3,2},{4,5},{5,4},{6,7},{7,6},{8,12},{9,10},{10,... | collective-permute-start | bytes 12296 | tf_op jit(solution)/shard_map/ppermute | solution.py:603
  21.0 2.6 %collective-permute-start.8 = (f32[8,128]{1,0:T(8,128)S(1)}, f32[8,128]{1,0:T(8,128)S(1)}, u32[]{:S(2)}, u32[]{:S(2)}) collective-permute-start(f32[8,128]{1,0:T(8,128)S(1)} %shard_map.105.refs_0_), channel_id=1, source_target_pairs={{0,2},{1,3},{2,0},{3,1},{4,6},{5,7},{6,4},{7,5},{8,10},{9,11},{10,... | collective-permute-start | bytes 12296 | tf_op jit(solution)/shard_map/ppermute | solution.py:603
  23.6 0.2 collective-permute-start.9
  23.8 0.0 collective-permute-done.7.refs_1_
  23.8 1.7 %collective-permute-done.8.refs_2_ = f32[8,128]{1,0:T(8,128)S(1)} collective-permute-done((f32[8,128]{1,0:T(8,128)S(1)}, f32[8,128]{1,0:T(8,128)S(1)}, u32[]{:S(2)}, u32[]{:S(2)}) %collective-permute-start.8) | collective-permute-done | bytes 4128 | tf_op jit(solution)/shard_map/ppermute | solution.py:603
  25.5 0.0 collective-permute-done.9.refs_3_
  25.5 0.6 %shard_map.106 = f32[2,1,2,16]{3,2,1,0:T(2,128)} custom-call(f32[16,8,128]{2,1,0:T(8,128)S(1)} %get-tuple-element.37.row_weights, f32[8,128]{1,0:T(8,128)S(1)} %shard_map.105.refs_0_, f32[8,128]{1,0:T(8,128)S(1)} %collective-permute-done.7.refs_1_, f32[8,128]{1,0:T(8,128)S(1)} %collective-permute-done.8.refs_2_, f32[8,128]{1,0:T(8,128)S(1)} %collective-permute-done.9.refs_3_), custom_call_target="tpu_custom_call" | custom-call | tf_op jit(solution)/shard_map/pallas_call | solution.py:604
  (4 shorter events, 0.1 us)
Async XLA Ops:
  0.6 4.3 %copy-start = (bf16[1,256,2048]{2,1,0:T(8,128)(2,1)S(1)}, bf16[1,256,2048]{2,1,0:T(8,128)(2,1)}, u32[]{:S(2)}) copy-start(bf16[1,256,2048]{2,1,0:T(8,128)(2,1)} %param.8) | copy-start | bytes 3145732
  1.8 4.0 %copy-start.2 = (s32[2,1,2,16]{3,2,1,0:T(2,128)S(1)}, s32[2,1,2,16]{3,2,1,0:T(2,128)}, u32[]{:S(2)}) copy-start(s32[2,1,2,16]{3,2,1,0:T(2,128)} %peaks.5) | copy-start | bytes 772
  1.8 7.4 %collective-permute-start = (bf16[64,2048]{1,0:T(8,128)(2,1)S(1)}, bf16[64,2048]{1,0:T(8,128)(2,1)S(1)}, u32[]{:S(2)}, u32[]{:S(2)}) collective-permute-start(bf16[64,2048]{1,0:T(8,128)(2,1)S(1)} %get-tuple-element.25), channel_id=1, source_target_pairs={{0,1},{1,0},{2,3},{3,2},{4,20},{5,6},{6,5},{7,23},{8,9},{9,8},{10,... | collective-permute-start | bytes 786440 | tf_op jit(solution)/shard_map/ppermute | solution.py:510
  5.7 10.6 %collective-permute-start.2 = (bf16[128,2048]{1,0:T(8,128)(2,1)S(1)}, bf16[128,2048]{1,0:T(8,128)(2,1)S(1)}, u32[]{:S(2)}, u32[]{:S(2)}) collective-permute-start(bf16[128,2048]{1,0:T(8,128)(2,1)S(1)} %get-tuple-element.24.mid), channel_id=1, source_target_pairs={{0,4},{4,8},{8,12},{12,0},{1,5},{5,9},{9,13},{13,1},{2,6},{6,10},{... | collective-permute-start | bytes 1572872 | tf_op jit(solution)/shard_map/ppermute | solution.py:520
  6.9 6.4 %collective-permute-start.1 = (bf16[64,2048]{1,0:T(8,128)(2,1)S(1)}, bf16[64,2048]{1,0:T(8,128)(2,1)S(1)}, u32[]{:S(2)}, u32[]{:S(2)}) collective-permute-start(bf16[64,2048]{1,0:T(8,128)(2,1)S(1)} %shard_map.98.rest_0_), channel_id=1, source_target_pairs={{0,16},{1,2},{2,1},{3,19},{4,5},{5,4},{6,7},{7,6},{8,24},{9,10},{1... | collective-permute-start | bytes 786440 | tf_op jit(solution)/shard_map/ppermute | solution.py:533
  9.3 0.7 %copy-start.1 = (f32[16,128]{1,0:T(8,128)S(1)}, f32[16,128]{1,0:T(8,128)}, u32[]{:S(2)}) copy-start(f32[16,128]{1,0:T(8,128)} %constant.2.clone.smooth.rest_6_) | copy-start | bytes 24580
  9.9 8.2 %collective-permute-start.3 = (bf16[64,2048]{1,0:T(8,128)(2,1)S(1)}, bf16[64,2048]{1,0:T(8,128)(2,1)S(1)}, u32[]{:S(2)}, u32[]{:S(2)}) collective-permute-start(bf16[64,2048]{1,0:T(8,128)(2,1)S(1)} %shard_map.99.edge.first), channel_id=1, source_target_pairs={{0,4},{4,8},{8,12},{12,0},{1,5},{5,9},{9,13},{13,1},{2,6},{6,10},{... | collective-permute-start | bytes 786440 | tf_op jit(solution)/shard_map/ppermute | solution.py:545
  14.0 4.6 %collective-permute-start.4 = (bf16[64,1024]{1,0:T(8,128)(2,1)S(1)}, bf16[64,1024]{1,0:T(8,128)(2,1)S(1)}, u32[]{:S(2)}, u32[]{:S(2)}) collective-permute-start(bf16[64,1024]{1,0:T(8,128)(2,1)S(1)} %get-tuple-element.30.rest_0_), channel_id=1, source_target_pairs={{0,4},{4,8},{8,12},{12,0},{1,5},{5,9},{9,13},{13,1},{2,6},{6,10},{... | collective-permute-start | bytes 393224 | tf_op jit(solution)/shard_map/ppermute | solution.py:567
  14.8 5.0 %collective-permute-start.5 = (bf16[64,1024]{1,0:T(8,128)(2,1)S(1)}, bf16[64,1024]{1,0:T(8,128)(2,1)S(1)}, u32[]{:S(2)}, u32[]{:S(2)}) collective-permute-start(bf16[64,1024]{1,0:T(8,128)(2,1)S(1)} %get-tuple-element.31.rest_1_), channel_id=1, source_target_pairs={{0,16},{4,8},{8,4},{12,28},{16,0},{20,24},{24,20},{28,12},{1,17},{... | collective-permute-start | bytes 393224 | tf_op jit(solution)/shard_map/ppermute | solution.py:571
  16.3 3.5 %collective-permute-start.6 = (bf16[64,1024]{1,0:T(8,128)(2,1)S(1)}, bf16[64,1024]{1,0:T(8,128)(2,1)S(1)}, u32[]{:S(2)}, u32[]{:S(2)}) collective-permute-start(bf16[64,1024]{1,0:T(8,128)(2,1)S(1)} %get-tuple-element.31.rest_1_), channel_id=1, source_target_pairs={{0,4},{4,0},{8,12},{12,8},{1,5},{5,1},{9,13},{13,9},{2,6},{6,2},{1... | collective-permute-start | bytes 393224 | tf_op jit(solution)/shard_map/ppermute | solution.py:572
  19.8 4.0 %collective-permute-start.7 = (f32[8,128]{1,0:T(8,128)S(1)}, f32[8,128]{1,0:T(8,128)S(1)}, u32[]{:S(2)}, u32[]{:S(2)}) collective-permute-start(f32[8,128]{1,0:T(8,128)S(1)} %shard_map.105.refs_0_), channel_id=1, source_target_pairs={{0,1},{1,0},{2,3},{3,2},{4,5},{5,4},{6,7},{7,6},{8,12},{9,10},{10,... | collective-permute-start | bytes 12296 | tf_op jit(solution)/shard_map/ppermute | solution.py:603
  21.0 4.5 %collective-permute-start.8 = (f32[8,128]{1,0:T(8,128)S(1)}, f32[8,128]{1,0:T(8,128)S(1)}, u32[]{:S(2)}, u32[]{:S(2)}) collective-permute-start(f32[8,128]{1,0:T(8,128)S(1)} %shard_map.105.refs_0_), channel_id=1, source_target_pairs={{0,2},{1,3},{2,0},{3,1},{4,6},{5,7},{6,4},{7,5},{8,10},{9,11},{10,... | collective-permute-start | bytes 12296 | tf_op jit(solution)/shard_map/ppermute | solution.py:603
  23.6 1.9 %collective-permute-start.9 = (f32[8,128]{1,0:T(8,128)S(1)}, f32[8,128]{1,0:T(8,128)S(1)}, u32[]{:S(2)}, u32[]{:S(2)}) collective-permute-start(f32[8,128]{1,0:T(8,128)S(1)} %shard_map.105.refs_0_), channel_id=1, source_target_pairs={{0,4},{1,2},{2,1},{3,7},{4,0},{5,6},{6,5},{7,3},{8,9},{9,8},{10,11... | collective-permute-start | bytes 12296 | tf_op jit(solution)/shard_map/ppermute | solution.py:603

commit v10 on v9

--- a/solution.py
+++ b/solution.py
@@ -16,7 +16,7 @@
 TAPS = (0.0625, 0.25, 0.375, 0.25, 0.0625)
 FAR = 1 << 20
 VMEM_LIMIT = 16 * 1024 * 1024
-TURN_UNROLL = 16
+TURN_UNROLL = 8
 PLAN_UNROLL = 8
 EARLY_BLOCKS = 6 / 8
 EDGE_PARTS = 2

time: 26.3 us -> 26.3 us (level)
    ppermute x1, waiting for transfers between devices: 0.6 us -> 1.02 us  [local(): lax.ppermute(send_second, ('parts', 'gz', 'ty'), halo_table(n_parts, n_gz...]
    ppermute x3, waiting for transfers between devices: 1.71 us -> 1.37 us  [local(): lax.ppermute(payload, ('gz', 'ty'), route)]
where the time goes in v10:
time: 26.3 us; the launch traced here: 25.9 us
  starting transfers between devices  11 us (42%)
  Pallas kernels  9.52 us (36%)
  waiting for transfers between devices  4.57 us (17%)
  between operations  0.76 us (3%)
    ppermute x3, starting transfers between devices, local(): lax.ppermute(payload, ('gz', 'ty'), route)  3.95 us
    ppermute x1, starting transfers between devices, local(): lax.ppermute(send_first, ('parts', 'gz', 'ty'), halo_table(n_parts, n_gz,...  3.09 us
    pallas_call x1, Pallas kernels, local(): call(functools.partial(first_waiting_kernel, n_ty, tuple(swaps)), (turned...  2.54 us
    pallas_call x1, Pallas kernels, local(): call(waiting_kernel, (shape((n_rows, n_cols), bf16), turned_shape, line_s...  1.76 us
    ppermute x1, starting transfers between devices, local(): lax.ppermute(send_second, ('parts', 'gz', 'ty'), halo_table(n_parts, n_gz...  1.58 us
    ppermute x1, starting transfers between devices, local(): lax.ppermute(second_edges[-1], ('parts', 'gz'), next_chip_table(n_parts,...  1.52 us
    ppermute x3, waiting for transfers between devices, local(): lax.ppermute(payload, ('gz', 'ty'), route)  1.37 us
    pallas_call x2, Pallas kernels, render_edges(): call(functools.partial(edges_kernel, which, parts), [shape((MARGIN, n_col...  1.32 us
  transfers between devices with their start and end apart: 10, of which 5 were waited for; matrix products, arithmetic and copies ran while one was open for 0% of the time, Pallas kernels for 30%

profile of v10, /device:TPU:0, one launch (start us, length us, event | category | flops | bytes accessed | tf_op | source)
XLA Modules:
  0.0 25.9 jit_solution(12508864945082554205)
XLA Ops:
  0.6 0.0 copy-start
  0.6 1.2 %shard_map.95 = (bf16[64,2048]{1,0:T(8,128)(2,1)S(1)}, f32[1,256]{1,0:T(1,128)S(1)}, f32[1,2048]{1,0:T(1,128)S(1)}, bf16[6,512,256]{2,1,0:T(8,128)(2,1)S(1)}) custom-call(bf16[256,2048]{1,0:T(8,128)(2,1)} %bitcast.2, s32[1,256]{1,0:T(1,128)} %row_shift.1, s32[1,256]{1,0:T(1,128)} %row_frac.1, s32[1,2048]{1,0:T(1,128)} %col_shift.1, s32[1,2048]{1,0:T(1,128)} %col_frac.1), custom_call_target="tpu_custom_call" | custom-call | tf_op jit(solution)/shard_map/pallas_call | solution.py:490
  1.8 0.0 copy-start.2
  1.8 3.1 %collective-permute-start = (bf16[64,2048]{1,0:T(8,128)(2,1)S(1)}, bf16[64,2048]{1,0:T(8,128)(2,1)S(1)}, u32[]{:S(2)}, u32[]{:S(2)}) collective-permute-start(bf16[64,2048]{1,0:T(8,128)(2,1)S(1)} %get-tuple-element.25), channel_id=1, source_target_pairs={{0,1},{1,0},{2,3},{3,2},{4,20},{5,6},{6,5},{7,23},{8,9},{9,8},{10,... | collective-permute-start | bytes 786440 | tf_op jit(solution)/shard_map/ppermute | solution.py:510
  4.9 0.0 copy-done
  4.9 0.8 %shard_map.96 = (bf16[128,2048]{1,0:T(8,128)(2,1)S(1)}, bf16[2,512,256]{2,1,0:T(8,128)(2,1)S(1)}, bf16[64,192]{1,0:T(8,128)(2,1)S(1)}, bf16[64,192]{1,0:T(8,128)(2,1)S(1)}) custom-call(bf16[256,2048]{1,0:T(8,128)(2,1)S(1)} %bitcast.3, f32[1,256]{1,0:T(1,128)S(1)} %get-tuple-element.21.row_pos, f32[1,2048]{1,0:T(1,128)S(1)} %get-tuple-element.22.col_pos, ...), custom_call_target="tpu_custom_call" | custom-call | tf_op jit(solution)/shard_map/pallas_call | solution.py:513
  5.7 0.1 collective-permute-start.2
  5.8 0.0 copy-done.2
  5.8 1.3 %shard_map.97._.turned_mid.rest_2_ = bf16[96,64,128]{2,1,0:T(8,128)(2,1)S(1)} custom-call(s32[2,1,2,16]{3,2,1,0:T(2,128)S(1)} %copy-done.2, bf16[128,2048]{1,0:T(8,128)(2,1)S(1)} %get-tuple-element.24.mid), custom_call_target="tpu_custom_call" | custom-call | flops 1000000000 | bytes 3000000 | tf_op jit(solution)/shard_map/pallas_call | solution.py:521
  7.1 1.6 %collective-permute-start.1 = (bf16[64,2048]{1,0:T(8,128)(2,1)S(1)}, bf16[64,2048]{1,0:T(8,128)(2,1)S(1)}, u32[]{:S(2)}, u32[]{:S(2)}) collective-permute-start(bf16[64,2048]{1,0:T(8,128)(2,1)S(1)} %shard_map.98.rest_0_), channel_id=1, source_target_pairs={{0,16},{1,2},{2,1},{3,19},{4,5},{5,4},{6,7},{7,6},{8,24},{9,10},{1... | collective-permute-start | bytes 786440 | tf_op jit(solution)/shard_map/ppermute | solution.py:533
  8.7 0.5 %collective-permute-done.halo = bf16[64,2048]{1,0:T(8,128)(2,1)S(1)} collective-permute-done((bf16[64,2048]{1,0:T(8,128)(2,1)S(1)}, bf16[64,2048]{1,0:T(8,128)(2,1)S(1)}, u32[]{:S(2)}, u32[]{:S(2)}) %collective-permute-start) | collective-permute-done | bytes 262176 | tf_op jit(solution)/shard_map/ppermute | solution.py:510
  9.3 0.0 copy-start.1
  9.3 0.7 %shard_map.99.edge.first = bf16[64,2048]{1,0:T(8,128)(2,1)S(1)} custom-call(bf16[64,2048]{1,0:T(8,128)(2,1)S(1)} %collective-permute-done.halo, bf16[256,2048]{1,0:T(8,128)(2,1)S(1)} %bitcast.5, bf16[64,192]{1,0:T(8,128)(2,1)S(1)} %get-tuple-element.26.table, bf16[6,512,256]{2,1,0:T(8,128)(2,1)S(1)} %get-tuple-element.23.tables, ...), custom_call_target="tpu_custom_call" | custom-call | tf_op jit(solution)/shard_map/pallas_call | solution.py:535
  9.9 0.1 collective-permute-start.3
  10.0 0.0 copy-done.1
  10.0 2.5 %shard_map.100 = (bf16[48,64,128]{2,1,0:T(8,128)(2,1)S(1)}, f32[32,16,128]{2,1,0:T(8,128)S(1)}, f32[2,32,128]{2,1,0:T(8,128)S(1)}, f32[16,8,128]{2,1,0:T(8,128)S...) custom-call(s32[2,1,2,16]{3,2,1,0:T(2,128)S(1)} %copy-done.2, bf16[64,2048]{1,0:T(8,128)(2,1)S(1)} %shard_map.99.edge.first, ...), custom_call_target="tpu_custom_call" | custom-call | flops 500000000 | bytes 1000000 | tf_op jit(solution)/shard_map/pallas_call | solution.py:549
  12.5 1.0 %collective-permute-done.1.halo = bf16[64,2048]{1,0:T(8,128)(2,1)S(1)} collective-permute-done((bf16[64,2048]{1,0:T(8,128)(2,1)S(1)}, bf16[64,2048]{1,0:T(8,128)(2,1)S(1)}, u32[]{:S(2)}, u32[]{:S(2)}) %collective-permute-start.1) | collective-permute-done | bytes 262176 | tf_op jit(solution)/shard_map/ppermute | solution.py:533
  13.6 0.7 %shard_map.101 = (bf16[64,1024]{1,0:T(8,128)(2,1)S(1)}, bf16[64,1024]{1,0:T(8,128)(2,1)S(1)}) custom-call(bf16[64,2048]{1,0:T(8,128)(2,1)S(1)} %collective-permute-done.1.halo, bf16[256,2048]{1,0:T(8,128)(2,1)S(1)} %bitcast.6, bf16[64,192]{1,0:T(8,128)(2,1)S(1)} %get-tuple-element.28.table, bf16[6,512,256]{2,1,0:T(8,128)(2,1)S(1)} %get-tuple-element.23.tables, ...), custom_call_target="tpu_custom_call" | custom-call | tf_op jit(solution)/shard_map/pallas_call | solution.py:535
  14.2 0.8 %collective-permute-start.4 = (bf16[64,1024]{1,0:T(8,128)(2,1)S(1)}, bf16[64,1024]{1,0:T(8,128)(2,1)S(1)}, u32[]{:S(2)}, u32[]{:S(2)}) collective-permute-start(bf16[64,1024]{1,0:T(8,128)(2,1)S(1)} %get-tuple-element.30.rest_0_), channel_id=1, source_target_pairs={{0,4},{4,8},{8,12},{12,0},{1,5},{5,9},{9,13},{13,1},{2,6},{6,10},{... | collective-permute-start | bytes 393224 | tf_op jit(solution)/shard_map/ppermute | solution.py:567
  15.0 1.5 %collective-permute-start.5 = (bf16[64,1024]{1,0:T(8,128)(2,1)S(1)}, bf16[64,1024]{1,0:T(8,128)(2,1)S(1)}, u32[]{:S(2)}, u32[]{:S(2)}) collective-permute-start(bf16[64,1024]{1,0:T(8,128)(2,1)S(1)} %get-tuple-element.31.rest_1_), channel_id=1, source_target_pairs={{0,16},{4,8},{8,4},{12,28},{16,0},{20,24},{24,20},{28,12},{1,17},{... | collective-permute-start | bytes 393224 | tf_op jit(solution)/shard_map/ppermute | solution.py:571
  16.5 0.0 collective-permute-start.6
  16.5 0.0 collective-permute-done.2.rest_8_.old_mid
  16.5 1.8 %shard_map.102 = (bf16[256,2048]{1,0:T(8,128)(2,1)}, bf16[48,64,128]{2,1,0:T(8,128)(2,1)S(1)}, f32[8,128]{1,0:T(8,128)S(1)}) custom-call(s32[2,1,2,16]{3,2,1,0:T(2,128)S(1)} %copy-done.2, bf16[128,2048]{1,0:T(8,128)(2,1)S(1)} %get-tuple-element.24.mid, bf16[64,2048]{1,0:T(8,128)(2,1)S(1)} %shard_map.99.edge.first, ...), custom_call_target="tpu_custom_call" | custom-call | flops 1000000000 | bytes 3000000 | tf_op jit(solution)/shard_map/pallas_call | solution.py:575
  18.3 0.0 collective-permute-done.3.rest_0_
  18.4 0.3 %collective-permute-done.4.rest_0_ = bf16[64,1024]{1,0:T(8,128)(2,1)S(1)} collective-permute-done((bf16[64,1024]{1,0:T(8,128)(2,1)S(1)}, bf16[64,1024]{1,0:T(8,128)(2,1)S(1)}, u32[]{:S(2)}, u32[]{:S(2)}) %collective-permute-start.4) | collective-permute-done | bytes 131104 | tf_op jit(solution)/shard_map/ppermute | solution.py:567
  18.7 1.3 %collective-permute-done.5.rest_0_ = bf16[64,1024]{1,0:T(8,128)(2,1)S(1)} collective-permute-done((bf16[64,1024]{1,0:T(8,128)(2,1)S(1)}, bf16[64,1024]{1,0:T(8,128)(2,1)S(1)}, u32[]{:S(2)}, u32[]{:S(2)}) %collective-permute-start.5) | collective-permute-done | bytes 131104 | tf_op jit(solution)/shard_map/ppermute | solution.py:571
  20.0 0.0 collective-permute-done.6.rest_1_
  20.0 0.8 %collective-permute-start.7 = (f32[8,128]{1,0:T(8,128)S(1)}, f32[8,128]{1,0:T(8,128)S(1)}, u32[]{:S(2)}, u32[]{:S(2)}) collective-permute-start(f32[8,128]{1,0:T(8,128)S(1)} %shard_map.105.refs_0_), channel_id=1, source_target_pairs={{0,1},{1,0},{2,3},{3,2},{4,5},{5,4},{6,7},{7,6},{8,12},{9,10},{10,... | collective-permute-start | bytes 12296 | tf_op jit(solution)/shard_map/ppermute | solution.py:603
  20.8 2.6 %collective-permute-start.8 = (f32[8,128]{1,0:T(8,128)S(1)}, f32[8,128]{1,0:T(8,128)S(1)}, u32[]{:S(2)}, u32[]{:S(2)}) collective-permute-start(f32[8,128]{1,0:T(8,128)S(1)} %shard_map.105.refs_0_), channel_id=1, source_target_pairs={{0,2},{1,3},{2,0},{3,1},{4,6},{5,7},{6,4},{7,5},{8,10},{9,11},{10,... | collective-permute-start | bytes 12296 | tf_op jit(solution)/shard_map/ppermute | solution.py:603
  23.5 0.5 %collective-permute-start.9 = (f32[8,128]{1,0:T(8,128)S(1)}, f32[8,128]{1,0:T(8,128)S(1)}, u32[]{:S(2)}, u32[]{:S(2)}) collective-permute-start(f32[8,128]{1,0:T(8,128)S(1)} %shard_map.105.refs_0_), channel_id=1, source_target_pairs={{0,4},{1,2},{2,1},{3,7},{4,0},{5,6},{6,5},{7,3},{8,9},{9,8},{10,11... | collective-permute-start | bytes 12296 | tf_op jit(solution)/shard_map/ppermute | solution.py:603
  23.9 0.0 collective-permute-done.7.refs_1_
  24.0 1.4 %collective-permute-done.8.refs_2_ = f32[8,128]{1,0:T(8,128)S(1)} collective-permute-done((f32[8,128]{1,0:T(8,128)S(1)}, f32[8,128]{1,0:T(8,128)S(1)}, u32[]{:S(2)}, u32[]{:S(2)}) %collective-permute-start.8) | collective-permute-done | bytes 4128 | tf_op jit(solution)/shard_map/ppermute | solution.py:603
  25.3 0.0 collective-permute-done.9.refs_3_
  25.3 0.6 %shard_map.106 = f32[2,1,2,16]{3,2,1,0:T(2,128)} custom-call(f32[16,8,128]{2,1,0:T(8,128)S(1)} %get-tuple-element.37.row_weights, f32[8,128]{1,0:T(8,128)S(1)} %shard_map.105.refs_0_, f32[8,128]{1,0:T(8,128)S(1)} %collective-permute-done.7.refs_1_, f32[8,128]{1,0:T(8,128)S(1)} %collective-permute-done.8.refs_2_, f32[8,128]{1,0:T(8,128)S(1)} %collective-permute-done.9.refs_3_), custom_call_target="tpu_custom_call" | custom-call | tf_op jit(solution)/shard_map/pallas_call | solution.py:604
  (4 shorter events, 0.1 us)
Async XLA Ops:
  0.6 4.3 %copy-start = (bf16[1,256,2048]{2,1,0:T(8,128)(2,1)S(1)}, bf16[1,256,2048]{2,1,0:T(8,128)(2,1)}, u32[]{:S(2)}) copy-start(bf16[1,256,2048]{2,1,0:T(8,128)(2,1)} %param.8) | copy-start | bytes 3145732
  1.8 4.0 %copy-start.2 = (s32[2,1,2,16]{3,2,1,0:T(2,128)S(1)}, s32[2,1,2,16]{3,2,1,0:T(2,128)}, u32[]{:S(2)}) copy-start(s32[2,1,2,16]{3,2,1,0:T(2,128)} %peaks.5) | copy-start | bytes 772
  1.8 7.4 %collective-permute-start = (bf16[64,2048]{1,0:T(8,128)(2,1)S(1)}, bf16[64,2048]{1,0:T(8,128)(2,1)S(1)}, u32[]{:S(2)}, u32[]{:S(2)}) collective-permute-start(bf16[64,2048]{1,0:T(8,128)(2,1)S(1)} %get-tuple-element.25), channel_id=1, source_target_pairs={{0,1},{1,0},{2,3},{3,2},{4,20},{5,6},{6,5},{7,23},{8,9},{9,8},{10,... | collective-permute-start | bytes 786440 | tf_op jit(solution)/shard_map/ppermute | solution.py:510
  5.7 10.8 %collective-permute-start.2 = (bf16[128,2048]{1,0:T(8,128)(2,1)S(1)}, bf16[128,2048]{1,0:T(8,128)(2,1)S(1)}, u32[]{:S(2)}, u32[]{:S(2)}) collective-permute-start(bf16[128,2048]{1,0:T(8,128)(2,1)S(1)} %get-tuple-element.24.mid), channel_id=1, source_target_pairs={{0,4},{4,8},{8,12},{12,0},{1,5},{5,9},{9,13},{13,1},{2,6},{6,10},{... | collective-permute-start | bytes 1572872 | tf_op jit(solution)/shard_map/ppermute | solution.py:520
  7.1 6.4 %collective-permute-start.1 = (bf16[64,2048]{1,0:T(8,128)(2,1)S(1)}, bf16[64,2048]{1,0:T(8,128)(2,1)S(1)}, u32[]{:S(2)}, u32[]{:S(2)}) collective-permute-start(bf16[64,2048]{1,0:T(8,128)(2,1)S(1)} %shard_map.98.rest_0_), channel_id=1, source_target_pairs={{0,16},{1,2},{2,1},{3,19},{4,5},{5,4},{6,7},{7,6},{8,24},{9,10},{1... | collective-permute-start | bytes 786440 | tf_op jit(solution)/shard_map/ppermute | solution.py:533
  9.3 0.7 %copy-start.1 = (f32[16,128]{1,0:T(8,128)S(1)}, f32[16,128]{1,0:T(8,128)}, u32[]{:S(2)}) copy-start(f32[16,128]{1,0:T(8,128)} %constant.2.clone.smooth.rest_6_) | copy-start | bytes 24580
  9.9 8.4 %collective-permute-start.3 = (bf16[64,2048]{1,0:T(8,128)(2,1)S(1)}, bf16[64,2048]{1,0:T(8,128)(2,1)S(1)}, u32[]{:S(2)}, u32[]{:S(2)}) collective-permute-start(bf16[64,2048]{1,0:T(8,128)(2,1)S(1)} %shard_map.99.edge.first), channel_id=1, source_target_pairs={{0,4},{4,8},{8,12},{12,0},{1,5},{5,9},{9,13},{13,1},{2,6},{6,10},{... | collective-permute-start | bytes 786440 | tf_op jit(solution)/shard_map/ppermute | solution.py:545
  14.2 4.4 %collective-permute-start.4 = (bf16[64,1024]{1,0:T(8,128)(2,1)S(1)}, bf16[64,1024]{1,0:T(8,128)(2,1)S(1)}, u32[]{:S(2)}, u32[]{:S(2)}) collective-permute-start(bf16[64,1024]{1,0:T(8,128)(2,1)S(1)} %get-tuple-element.30.rest_0_), channel_id=1, source_target_pairs={{0,4},{4,8},{8,12},{12,0},{1,5},{5,9},{9,13},{13,1},{2,6},{6,10},{... | collective-permute-start | bytes 393224 | tf_op jit(solution)/shard_map/ppermute | solution.py:567
  15.0 5.0 %collective-permute-start.5 = (bf16[64,1024]{1,0:T(8,128)(2,1)S(1)}, bf16[64,1024]{1,0:T(8,128)(2,1)S(1)}, u32[]{:S(2)}, u32[]{:S(2)}) collective-permute-start(bf16[64,1024]{1,0:T(8,128)(2,1)S(1)} %get-tuple-element.31.rest_1_), channel_id=1, source_target_pairs={{0,16},{4,8},{8,4},{12,28},{16,0},{20,24},{24,20},{28,12},{1,17},{... | collective-permute-start | bytes 393224 | tf_op jit(solution)/shard_map/ppermute | solution.py:571
  16.5 3.5 %collective-permute-start.6 = (bf16[64,1024]{1,0:T(8,128)(2,1)S(1)}, bf16[64,1024]{1,0:T(8,128)(2,1)S(1)}, u32[]{:S(2)}, u32[]{:S(2)}) collective-permute-start(bf16[64,1024]{1,0:T(8,128)(2,1)S(1)} %get-tuple-element.31.rest_1_), channel_id=1, source_target_pairs={{0,4},{4,0},{8,12},{12,8},{1,5},{5,1},{9,13},{13,9},{2,6},{6,2},{1... | collective-permute-start | bytes 393224 | tf_op jit(solution)/shard_map/ppermute | solution.py:572
  20.0 4.0 %collective-permute-start.7 = (f32[8,128]{1,0:T(8,128)S(1)}, f32[8,128]{1,0:T(8,128)S(1)}, u32[]{:S(2)}, u32[]{:S(2)}) collective-permute-start(f32[8,128]{1,0:T(8,128)S(1)} %shard_map.105.refs_0_), channel_id=1, source_target_pairs={{0,1},{1,0},{2,3},{3,2},{4,5},{5,4},{6,7},{7,6},{8,12},{9,10},{10,... | collective-permute-start | bytes 12296 | tf_op jit(solution)/shard_map/ppermute | solution.py:603
  20.8 4.5 %collective-permute-start.8 = (f32[8,128]{1,0:T(8,128)S(1)}, f32[8,128]{1,0:T(8,128)S(1)}, u32[]{:S(2)}, u32[]{:S(2)}) collective-permute-start(f32[8,128]{1,0:T(8,128)S(1)} %shard_map.105.refs_0_), channel_id=1, source_target_pairs={{0,2},{1,3},{2,0},{3,1},{4,6},{5,7},{6,4},{7,5},{8,10},{9,11},{10,... | collective-permute-start | bytes 12296 | tf_op jit(solution)/shard_map/ppermute | solution.py:603
  23.5 1.9 %collective-permute-start.9 = (f32[8,128]{1,0:T(8,128)S(1)}, f32[8,128]{1,0:T(8,128)S(1)}, u32[]{:S(2)}, u32[]{:S(2)}) collective-permute-start(f32[8,128]{1,0:T(8,128)S(1)} %shard_map.105.refs_0_), channel_id=1, source_target_pairs={{0,4},{1,2},{2,1},{3,7},{4,0},{5,6},{6,5},{7,3},{8,9},{9,8},{10,11... | collective-permute-start | bytes 12296 | tf_op jit(solution)/shard_map/ppermute | solution.py:603
